TPU v7x, 32 devices: a whole 2x2x4 slice. The times are simulated.
32 devices in a mesh: groups: 2 (over y), expert: 4 (over z), tensor: 2 (over x), seq: 2 (over core).
Axes of the slice: x: 2, y: 2, z: 4, core: 2. Of those that a mesh axis runs over, the one named last changes fastest.
Arguments:
- tokens: bfloat16 [2048, 4096], P(('groups', 'expert'), 'seq'), parts along dimension 0, may hold values from -6 to 6
- gate_weight: bfloat16 [4, 4096, 768], P('expert', 'seq', 'tensor'), may hold values from -0.09375 to 0.09375
- up_weight: bfloat16 [4, 4096, 768], P('expert', 'seq', 'tensor'), may hold values from -0.09375 to 0.09375
- down_weight: bfloat16 [4, 768, 4096], P('expert', None, ('tensor', 'seq')), may hold values from -0.15625 to 0.15625
- expert_ids: int32 [2048, 1], P(('groups', 'expert')), parts along dimension 0, may hold values from 0 to 1; in each aligned block of 256 rows (0 to 255, 256 to 511, ...) at most 256 rows name the same one
- codes: int32 [2048, 1], P(('groups', 'expert')), parts along dimension 0, may hold values from 64 to 1024
- expert_home: int32 [2], replicated, may hold values from 0 to 1, each once
Outputs:
- mixed: bfloat16 [2048, 4096], P(('groups', 'expert'), ('tensor', 'seq')), parts along dimension 0
There are 2 independent parts, one for each index of `groups`. A program takes and returns all parts, laid end to end along the dimension named above; an argument that names none is the same for every part. Nothing has to cross between parts.
Inputs may be any that keep to these rules, and one draw needn't show every extreme that they name: `expert_ids`: in each aligned block of 256 rows no expert is named by more than 256 rows, and in some block an expert is named by exactly 256 rows. `expert_home`: every slot is the home of exactly one expert.
All inputs are finite; a program needn't handle non-finite values.
Results may differ from a plain program's by a relative error of at most 0.0057.
Values may be sent and summed in bfloat16 or wider, within the bound.
No kernel may reach another device: no remote copies, remote signals or barrier semaphores. Data moves between devices by JAX's collectives and lax.ppermute only.
A program may use at most 64 MiB of HBM per device.

v0:
```python
import jax
import jax.numpy as jnp
from jax import lax
from jax.sharding import PartitionSpec as P


def swapped(x, axis, distance):
    return lax.ppermute(x, axis, [(i, i ^ 1 << distance) for i in range(lax.axis_size(axis))])


def local(tokens, gate_weight, up_weight, down_weight, expert_ids, codes, expert_home):
    tok_rows, columns_dev = tokens.shape
    experts = expert_home.shape[0]
    capacity = min(tok_rows, 2 * tok_rows // experts)
    owners = 2 * experts
    numbers = jnp.arange(experts, dtype=jnp.int32)
    chosen = (expert_ids == numbers[None, :]).astype(jnp.int32)
    home_slot = jnp.sum(chosen * expert_home[None, :], axis=1)
    onehot = (home_slot[:, None] == numbers[None, :]).astype(jnp.int32)
    before = jnp.cumsum(onehot, axis=0) - onehot
    position = jnp.sum(before * onehot, axis=1)
    target = home_slot * capacity + position
    select = (jnp.arange(experts * capacity, dtype=jnp.int32)[:, None] == target[None, :]).astype(
        jnp.bfloat16
    )
    packed = jnp.dot(select, tokens, preferred_element_type=jnp.float32).astype(jnp.bfloat16)
    packed = packed.reshape(experts, capacity, columns_dev)
    member = lax.axis_index("expert") % 2
    doubled = jnp.broadcast_to(packed[:, None], (experts, 2, capacity, columns_dev))
    doubled = doubled.reshape(owners, capacity, columns_dev)
    arrived = lax.all_to_all(doubled, "expert", split_axis=0, concat_axis=0, tiled=True)
    slot_count = owners * capacity
    received = arrived.reshape(slot_count, columns_dev)
    gate_part = jnp.dot(received, gate_weight[0], preferred_element_type=jnp.float32)
    up_part = jnp.dot(received, up_weight[0], preferred_element_type=jnp.float32)
    gate_act, up_act = lax.psum((gate_part, up_part), "seq")
    activated = (jax.nn.silu(gate_act) * up_act).astype(jnp.bfloat16)
    down_block = down_weight[0]
    out_columns = down_block.shape[1]
    partial_value = jnp.dot(
        lax.all_gather(activated, "tensor", axis=1, tiled=True),
        down_block,
        preferred_element_type=jnp.float32,
    )
    partial_value = partial_value.reshape(owners, capacity, out_columns)
    kept_rows = capacity // 2
    own_part = lax.dynamic_slice_in_dim(partial_value, member * kept_rows, kept_rows, 1)
    handed = lax.dynamic_slice_in_dim(partial_value, (1 - member) * kept_rows, kept_rows, 1)
    summed = own_part + swapped(handed, "expert", 0)
    returned = lax.all_to_all(
        summed.astype(jnp.bfloat16), "expert", split_axis=0, concat_axis=0, tiled=True
    )
    returned = returned.reshape(experts * capacity, out_columns)
    gathered = jnp.einsum("pt,pd->td", select, returned, preferred_element_type=jnp.float32)
    weights = codes[:, 0].astype(jnp.float32) / 1024.0
    return (weights[:, None] * gathered).astype(jnp.bfloat16)


def solution(mesh):
    in_specs = (
        P(("groups", "expert"), "seq"),
        P("expert", "seq", "tensor"),
        P("expert", "seq", "tensor"),
        P("expert", None, ("tensor", "seq")),
        P(("groups", "expert"), None),
        P(("groups", "expert"), None),
        P(),
    )
    out_specs = P(("groups", "expert"), ("tensor", "seq"))
    return jax.shard_map(local, mesh=mesh, in_specs=in_specs, out_specs=out_specs, check_vma=False)
```

profile of v0, /device:TPU:0, one launch (start us, length us, event | category | flops | bytes accessed | tf_op | source)
XLA Modules:
  0.0 266.7 jit_solution(3935224250710227818)
XLA Ops:
  6.5 0.0 copy-start
  6.5 0.0 all-reduce.3.cloned.1.call-start
  6.5 0.9 fusion.9
  7.4 0.6 reduce-window.6
  8.1 0.2 slice_reduce_fusion
  8.3 0.2 reduce-window.9
  8.5 0.1 add_bitcast_fusion
  8.6 1.9 convolution_convert_fusion
  10.5 0.5 broadcast_in_dim.5
  11.1 0.0 copy-start.3
  11.1 99.4 %all_to_all.10 = bf16[4,256,2048]{2,1,0:T(8,128)(2,1)S(1)} all-to-all(bf16[4,256,2048]{2,1,0:T(8,128)(2,1)S(1)} %bitcast.42), channel_id=1, replica_groups=mesh['groups'=2,'expert'=4,'tensor'=2,'seq'=2] {'expert'}, dimensions={0} | all-to-all | bytes 8388608 | tf_op jit(solution)/shard_map/all_to_all | solution.py:31
  110.5 0.0 copy-done.3
  110.5 0.0 copy-start.4
  110.5 3.5 %fusion.2 = f32[1024,384]{1,0:T(8,128)} fusion(bf16[1024,2048]{1,0:T(8,128)(2,1)S(1)} %bitcast.44, bf16[1,2048,384]{2,1,0:T(8,128)(2,1)S(1)} %copy-done.3), kind=kOutput, calls=%fused_computation.4 | convolution fusion | flops 1610612736 | bytes 7340032 | tf_op jit(solution)/shard_map/dot_general | solution.py:35
  113.9 0.0 copy-done.4
  113.9 3.5 %fusion.4 = f32[1024,384]{1,0:T(8,128)} fusion(bf16[1024,2048]{1,0:T(8,128)(2,1)S(1)} %bitcast.45, bf16[1,2048,384]{2,1,0:T(8,128)(2,1)S(1)} %copy-done.4), kind=kOutput, calls=%fused_computation.6 | convolution fusion | flops 1610612736 | bytes 7340032 | tf_op jit(solution)/shard_map/dot_general | solution.py:34
  117.4 0.0 all-reduce.3.cloned.1.call-update
  117.5 0.0 all-gather.2.cloned.1.call-start
  117.5 22.7 %all-reduce.3.cloned.1.call-done = (f32[1024,384]{1,0:T(8,128)}, f32[1024,384]{1,0:T(8,128)}) async-done(((f32[1024,384]{1,0:T(8,128)}, f32[1024,384]{1,0:T(8,128)}), (f32[1024,384]{1,0:T(8,128)}, f32[1024,384]{1,0:T(8,128)})) %all-reduce.3.cloned.1.call-update) | async-done | bytes 3145744 | tf_op jit(solution)/shard_map/psum | solution.py:36
  140.3 3.2 %multiply_convert_fusion = bf16[1024,384]{1,0:T(8,128)(2,1)} fusion(f32[1024,384]{1,0:T(8,128)} %get-tuple-element.5, f32[1024,384]{1,0:T(8,128)} %get-tuple-element.6), kind=kLoop, calls=%fused_computation.8 | loop fusion | flops 2359296 | bytes 3932160 | tf_op jit(solution)/shard_map/convert_element_type | solution.py:37
  143.4 0.0 all-gather.2.cloned.1.call-update
  143.5 28.5 %all-gather.2.cloned.1.call-done = bf16[1024,768]{1,0:T(8,128)(2,1)} async-done(((bf16[1024,384]{1,0:T(8,128)(2,1)}), bf16[1024,768]{1,0:T(8,128)(2,1)}) %all-gather.2.cloned.1.call-update) | async-done | bytes 1572880 | tf_op jit(solution)/shard_map/all_gather | solution.py:41
  172.0 0.0 copy-done
  172.0 3.2 %fusion = f32[4,256,1024]{2,1,0:T(8,128)S(1)} fusion(bf16[4,256,768]{2,1,0:T(8,128)(2,1)} %bitcast.51, bf16[1,768,1024]{2,1,0:T(8,128)(2,1)S(1)} %copy-done), kind=kOutput, calls=%fused_computation.2 | convolution fusion | flops 1610612736 | bytes 7340032 | tf_op jit(solution)/shard_map/dot_general | solution.py:40
  175.2 0.0 copy-start.1
  175.2 1.6 constant_dynamic-slice_fusion
  176.8 1.0 copy-done.1
  177.8 1.5 collective-permute-start
  179.2 46.2 %collective-permute-done = f32[4,128,1024]{2,1,0:T(8,128)} collective-permute-done((f32[4,128,1024]{2,1,0:T(8,128)}, f32[4,128,1024]{2,1,0:T(8,128)}, u32[]{:S(2)}, u32[]{:S(2)}) %collective-permute-start) | collective-permute-done | bytes 2097184 | tf_op jit(solution)/shard_map/ppermute | solution.py:8
  225.4 3.5 %add_convert_fusion = bf16[4,128,1024]{2,1,0:T(8,128)(2,1)} fusion(f32[4,128,1024]{2,1,0:T(8,128)} %collective-permute-done, f32[4,256,1024]{2,1,0:T(8,128)} %copy-done.1, s32[]{:T(128)S(6)} %select_n.14), kind=kLoop, calls=%fused_computation.1 | loop fusion | flops 1048576 | bytes 5242884 | tf_op jit(solution)/shard_map/convert_element_type | solution.py:51
  229.0 0.0 copy-start.2
  229.0 4.7 %all-to-all-start.1 = ((bf16[4,128,1024]{2,1,0:T(8,128)(2,1)}), bf16[4,128,1024]{2,1,0:T(8,128)(2,1)S(1)}, u32[]{:S(2)}, u32[]{:S(2)}) async-start(bf16[4,128,1024]{2,1,0:T(8,128)(2,1)} %add_convert_fusion), calls=%async_computation.1 | async-start | bytes 2097152 | tf_op jit(solution)/shard_map/all_to_all | solution.py:50
  233.7 0.0 copy-done.2
  233.7 24.8 %all-to-all-done.1 = bf16[4,128,1024]{2,1,0:T(8,128)(2,1)S(1)} async-done(((bf16[4,128,1024]{2,1,0:T(8,128)(2,1)}), bf16[4,128,1024]{2,1,0:T(8,128)(2,1)S(1)}, u32[]{:S(2)}, u32[]{:S(2)}) %all-to-all-start.1) | async-done | bytes 1048608 | tf_op jit(solution)/shard_map/all_to_all | solution.py:50
  258.6 1.3 fusion.6
  (4 shorter events, 0.0 us)
Async XLA Ops:
  6.5 165.5 %copy-start = (bf16[1,768,1024]{2,1,0:T(8,128)(2,1)S(1)}, bf16[1,768,1024]{2,1,0:T(8,128)(2,1)}, u32[]{:S(2)}) copy-start(bf16[1,768,1024]{2,1,0:T(8,128)(2,1)} %param.10) | copy-start | bytes 4718596
  6.5 133.7 %all-reduce.3.cloned.1.call-start = ((), (), s32[]{:S(2)}) async-start(), calls=%async_computation.3 | async-start | bytes 6291456 | tf_op jit(solution)/shard_map/psum | solution.py:36
  11.1 99.4 %copy-start.3 = (bf16[1,2048,384]{2,1,0:T(8,128)(2,1)S(1)}, bf16[1,2048,384]{2,1,0:T(8,128)(2,1)}, u32[]{:S(2)}) copy-start(bf16[1,2048,384]{2,1,0:T(8,128)(2,1)} %param.9) | copy-start | bytes 4718596
  110.5 3.5 %copy-start.4 = (bf16[1,2048,384]{2,1,0:T(8,128)(2,1)S(1)}, bf16[1,2048,384]{2,1,0:T(8,128)(2,1)}, u32[]{:S(2)}) copy-start(bf16[1,2048,384]{2,1,0:T(8,128)(2,1)} %param.8) | copy-start | bytes 4718596
  117.5 54.5 %all-gather.2.cloned.1.call-start = ((), (), s32[]{:S(2)}) async-start(), calls=%async_computation.2 | async-start | bytes 2359296 | tf_op jit(solution)/shard_map/all_gather | solution.py:41
  175.2 2.6 copy-start.1
  177.8 47.7 %collective-permute-start = (f32[4,128,1024]{2,1,0:T(8,128)}, f32[4,128,1024]{2,1,0:T(8,128)}, u32[]{:S(2)}, u32[]{:S(2)}) collective-permute-start(f32[4,128,1024]{2,1,0:T(8,128)} %constant_dynamic-slice_fusion), channel_id=1, source_target_pairs={{0,4},{4,0},{8,12},{12,8},{1,5},{5,1},{9,13},{13,9},{2,6},{6,2},{1... | collective-permute-start | bytes 6291464 | tf_op jit(solution)/shard_map/ppermute | solution.py:8
  229.0 4.7 %copy-start.2 = (s32[256,1]{0,1:T(1,128)S(1)}, s32[256,1]{0,1:T(1,128)}, u32[]{:S(2)}) copy-start(s32[256,1]{0,1:T(1,128)} %param.12) | copy-start | bytes 3076
  229.0 29.6 %all-to-all-start.1 = ((bf16[4,128,1024]{2,1,0:T(8,128)(2,1)}), bf16[4,128,1024]{2,1,0:T(8,128)(2,1)S(1)}, u32[]{:S(2)}, u32[]{:S(2)}) async-start(bf16[4,128,1024]{2,1,0:T(8,128)(2,1)} %add_convert_fusion), calls=%async_computation.1 | async-start | bytes 2097152 | tf_op jit(solution)/shard_map/all_to_all | solution.py:50
Sparse Core Ops, SparseCore 0:
  117.6 22.6 all-reduce.2
  143.6 28.3 all-gather.1
where the time goes:
time: 267 us
  waiting for transfers between devices  122 us (46%)
  blocking collectives  99.4 us (37%)
  between operations  13.5 us (5%)
  matrix products  13.4 us (5%)
  other arithmetic  8.54 us (3%)
  starting transfers between devices  6.26 us (2%)
  local copies, waits for them, and re-layouts  3.32 us (1%)
    all_to_all x1, blocking collectives, local(): lax.all_to_all(doubled, 'expert', split_axis=0, concat_axis=0, tiled=True)  99.4 us
    ppermute x1, waiting for transfers between devices, swapped(): lax.ppermute(x, axis, [(i, i ^ 1 << distance) for i in range(lax.axis_siz...  46.2 us
    all_gather x1, waiting for transfers between devices, local(): lax.all_gather(activated, 'tensor', axis=1, tiled=True)  28.5 us
    all_to_all x1, waiting for transfers between devices, local(): lax.all_to_all(summed.astype(jnp.bfloat16), 'expert', split_axis=0, conca...  24.8 us
    psum x1, waiting for transfers between devices, local(): gate_act, up_act = lax.psum((gate_part, up_part), 'seq')  22.7 us
  transfers between devices with their start and end apart: 4, of which 4 were waited for; matrix products, arithmetic and copies ran while one was open for 0% of the time, Pallas kernels for 0%

commit v1 on v0

--- a/solution.py
+++ b/solution.py
@@ -8,7 +8,7 @@
     return lax.ppermute(x, axis, [(i, i ^ 1 << distance) for i in range(lax.axis_size(axis))])
 
 
-def local(tokens, gate_weight, up_weight, down_weight, expert_ids, codes, expert_home):
+def routed(tokens, gate_weight, up_weight, down_weight, expert_ids, codes, expert_home):
     tok_rows, columns_dev = tokens.shape
     experts = expert_home.shape[0]
     capacity = min(tok_rows, 2 * tok_rows // experts)
@@ -56,6 +56,89 @@
     return (weights[:, None] * gathered).astype(jnp.bfloat16)
 
 
+PAIR = [(0, 1), (1, 0), (2, 3), (3, 2)]
+ACROSS = [(1, 2), (2, 1)]
+OUTWARD = [(1, 0), (2, 3)]
+INWARD = [(0, 1), (3, 2)]
+FAR = [(1, 3), (2, 0)]
+
+
+def z_send(x, pairs):
+    return lax.ppermute(x, "expert", pairs)
+
+
+def half(x, index):
+    rows = x.shape[0] // 2
+    return lax.dynamic_slice_in_dim(x, index * rows, rows, 0)
+
+
+def in_order(own, other, index):
+    return jnp.where(index == 0, jnp.concatenate([own, other]), jnp.concatenate([other, own]))
+
+
+def gathered_pairs(tokens, gate_weight, up_weight, down_weight, expert_ids, codes, expert_home):
+    z, x, c = lax.axis_index("expert"), lax.axis_index("tensor"), lax.axis_index("seq")
+    inner = (z == 1) | (z == 2)
+    f32, bf16 = jnp.float32, jnp.bfloat16
+
+    other_columns = swapped(half(tokens, 1 - c), "seq", 0)
+    own_rows = jnp.concatenate([half(tokens, c), other_columns], axis=1)
+    quarter = half(own_rows, x)
+
+    from_pair = z_send(quarter, PAIR)
+    from_across = z_send(quarter, ACROSS)
+    weights = jnp.concatenate([gate_weight[0], up_weight[0]], axis=1)
+    weights = jnp.concatenate([weights, swapped(weights, "seq", 0)], axis=0)
+    down = down_weight[0]
+
+    near = jnp.where(inner, from_across, z_send(from_across, OUTWARD))
+    across_pair = z_send(from_pair, ACROSS)
+    far = jnp.where(inner, across_pair, z_send(across_pair, OUTWARD))
+
+    def with_tensor(part):
+        return in_order(part, swapped(part, "tensor", 0), x)
+
+    def hidden(rows):
+        acts = jnp.dot(rows, weights, preferred_element_type=f32)
+        gate_act, up_act = jnp.split(acts, 2, axis=1)
+        own = (jax.nn.silu(gate_act) * up_act).astype(bf16)
+        other = swapped(own, "tensor", 0)
+        both = jnp.where(
+            x == 0,
+            jnp.concatenate([own, other], axis=1),
+            jnp.concatenate([other, own], axis=1),
+        )
+        return in_order(both, swapped(both, "seq", 0), c)
+
+    def partial_out(rows):
+        return jnp.dot(hidden(rows), down, preferred_element_type=f32)
+
+    own_part = partial_out(own_rows)
+    pair_part = z_send(partial_out(with_tensor(from_pair)).astype(bf16), PAIR)
+    near_part = partial_out(with_tensor(near))
+    near_sum = near_part + z_send(near_part.astype(bf16), INWARD).astype(f32)
+    returned = z_send(near_sum.astype(bf16), ACROSS)
+    far_part = partial_out(with_tensor(far))
+    far_sum = far_part + z_send(far_part.astype(bf16), INWARD).astype(f32)
+    returned_far = z_send(far_sum.astype(bf16), FAR)
+
+    ids = expert_ids[:, 0]
+    home = jnp.where(ids == 0, expert_home[0], expert_home[1])
+    ours = (home == z // 2)[:, None]
+    local = (own_part + pair_part.astype(f32)).astype(bf16)
+    expert_out = jnp.where(ours, local, jnp.where(inner, returned, returned_far))
+    scale = codes[:, 0].astype(f32) / 1024.0
+    return (scale[:, None] * expert_out.astype(f32)).astype(bf16)
+
+
+def local(*arguments):
+    experts = arguments[-1].shape[0]
+    sizes = tuple(lax.axis_size(axis) for axis in ("expert", "tensor", "seq"))
+    if experts == 2 and sizes == (4, 2, 2):
+        return gathered_pairs(*arguments)
+    return routed(*arguments)
+
+
 def solution(mesh):
     in_specs = (
         P(("groups", "expert"), "seq"),

time: 267 us -> 131 us (0.49)
  blocking collectives: 99.4 us -> 0 us
  waiting for transfers between devices: 122 us -> 70.8 us
  starting transfers between devices: 6.26 us -> 24.7 us
  between operations: 13.5 us -> 0.37 us
  matrix products: 13.4 us -> 25.7 us
    all_to_all x1 -> x0, blocking collectives: 99.4 us -> none  [local(): lax.all_to_all(doubled, 'expert', split_axis=0, concat_axis=0, tiled=True)]
    ppermute x0 -> x10, waiting for transfers between devices: none -> 60.7 us  [z_send(): return lax.ppermute(x, 'expert', pairs)]
    ppermute x1 -> x13, waiting for transfers between devices: 46.2 us -> 10.1 us  [swapped(): lax.ppermute(x, axis, [(i, i ^ 1 << distance) for i in range(lax.axis_siz...]
    all_gather x1 -> x0, waiting for transfers between devices: 28.5 us -> none  [local(): lax.all_gather(activated, 'tensor', axis=1, tiled=True)]
    all_to_all x1 -> x0, waiting for transfers between devices: 24.8 us -> none  [local(): lax.all_to_all(summed.astype(jnp.bfloat16), 'expert', split_axis=0, conca...]
    psum x1 -> x0, waiting for transfers between devices: 22.7 us -> none  [local(): gate_act, up_act = lax.psum((gate_part, up_part), 'seq')]
    ppermute x0 -> x10, starting transfers between devices: none -> 13.9 us  [z_send(): return lax.ppermute(x, 'expert', pairs)]
    dot_general x5 -> x8, matrix products: 13.4 us -> 25.7 us  [the longest x4 22.5 us: hidden(): acts = jnp.dot(rows, weights, preferred_element_type=f32)]
  transfers between devices with their start and end apart: 4 -> 23, of which waited for: 4 -> 11; matrix products, arithmetic and copies ran while one was open for 0% -> 24% of each run, Pallas kernels for 0% -> 0%
where the time goes in v1:
time: 131 us; the launch traced here: 130 us
  waiting for transfers between devices  70.8 us (54%)
  matrix products  25.7 us (20%)
  starting transfers between devices  24.7 us (19%)
  other arithmetic  6.53 us (5%)
  local copies, waits for them, and re-layouts  2.01 us (2%)
    ppermute x10, waiting for transfers between devices, z_send(): return lax.ppermute(x, 'expert', pairs)  60.7 us
    dot_general x4, matrix products, hidden(): acts = jnp.dot(rows, weights, preferred_element_type=f32)  22.5 us
    ppermute x10, starting transfers between devices, z_send(): return lax.ppermute(x, 'expert', pairs)  13.9 us
    ppermute x13, starting transfers between devices, swapped(): lax.ppermute(x, axis, [(i, i ^ 1 << distance) for i in range(lax.axis_siz...  10.7 us
    ppermute x13, waiting for transfers between devices, swapped(): lax.ppermute(x, axis, [(i, i ^ 1 << distance) for i in range(lax.axis_siz...  10.1 us
    concatenate x1, other arithmetic, gathered_pairs(): weights = jnp.concatenate([gate_weight[0], up_weight[0]], axis=1)  3.35 us
    dot_general x4, matrix products, partial_out(): return jnp.dot(hidden(rows), down, preferred_element_type=f32)  3.2 us
  transfers between devices with their start and end apart: 23, of which 11 were waited for; matrix products, arithmetic and copies ran while one was open for 24% of the time, Pallas kernels for 0%

profile of v1, /device:TPU:0, one launch (start us, length us, event | category | flops | bytes accessed | tf_op | source)
XLA Modules:
  0.0 130.1 jit_solution(2173837592249562998)
XLA Ops:
  0.0 1.4 %constant_dynamic-slice_fusion = (bf16[128,2048]{1,0:T(8,128)(2,1)S(1)}, bf16[128,2048]{1,0:T(8,128)(2,1)S(1)}) fusion(bf16[256,2048]{1,0:T(8,128)(2,1)} %param.7, s32[]{:T(128)S(6)} %select_n.104, s32[]{:T(128)S(6)} %select_n.103), kind=kLoop, calls=%fused_computation.92 | loop fusion | bytes 2097160 | tf_op jit(solution)/shard_map/dynamic_slice | solution.py:72
  1.4 0.5 collective-permute-start
  1.9 3.4 %pad_maximum_fusion.1 = bf16[2048,768]{1,0:T(8,128)(2,1)} fusion(bf16[2048,384]{1,0:T(8,128)(2,1)S(1)} %bitcast.32, bf16[2048,384]{1,0:T(8,128)(2,1)} %bitcast.37), kind=kLoop, calls=%fused_computation.1 | loop fusion | flops 6291456 | bytes 6291456 | tf_op jit(solution)/shard_map/concatenate | solution.py:90
  5.3 0.4 collective-permute-start.1
  5.7 2.8 %collective-permute-start.4 = (bf16[64,4096]{1,0:T(8,128)(2,1)S(1)}, bf16[64,4096]{1,0:T(8,128)(2,1)}, u32[]{:S(2)}, u32[]{:S(2)}) collective-permute-start(bf16[64,4096]{1,0:T(8,128)(2,1)S(1)} %fusion.51), channel_id=1, source_target_pairs={{0,4},{4,0},{8,12},{12,8},{1,5},{5,1},{9,13},{13,9},{2,6},{6,2},{1... | collective-permute-start | bytes 1572872 | tf_op jit(solution)/shard_map/ppermute | solution.py:67
  8.5 1.4 %collective-permute-start.9 = (bf16[64,4096]{1,0:T(8,128)(2,1)S(1)}, bf16[64,4096]{1,0:T(8,128)(2,1)}, u32[]{:S(2)}, u32[]{:S(2)}) collective-permute-start(bf16[64,4096]{1,0:T(8,128)(2,1)S(1)} %fusion.51), channel_id=1, source_target_pairs={{4,8},{8,4},{5,9},{9,5},{6,10},{10,6},{7,11},{11,7},{20,24},{24,20... | collective-permute-start | bytes 1572872 | tf_op jit(solution)/shard_map/ppermute | solution.py:67
  9.9 11.1 %collective-permute-done.4 = bf16[64,4096]{1,0:T(8,128)(2,1)} collective-permute-done((bf16[64,4096]{1,0:T(8,128)(2,1)S(1)}, bf16[64,4096]{1,0:T(8,128)(2,1)}, u32[]{:S(2)}, u32[]{:S(2)}) %collective-permute-start.4) | collective-permute-done | bytes 524320 | tf_op jit(solution)/shard_map/ppermute | solution.py:67
  21.0 0.7 collective-permute-start.16
  21.7 1.3 collective-permute-start.10
  23.1 0.6 fusion.88
  23.7 1.7 %collective-permute-start.5 = (bf16[64,4096]{1,0:T(8,128)(2,1)}, bf16[64,4096]{1,0:T(8,128)(2,1)S(1)}, u32[]{:S(2)}, u32[]{:S(2)}) collective-permute-start(bf16[64,4096]{1,0:T(8,128)(2,1)} %collective-permute-done.4), channel_id=1, source_target_pairs={{0,2},{2,0},{1,3},{3,1},{4,6},{6,4},{5,7},{7,5},{8,10},{10,8},{9,1... | collective-permute-start | bytes 1572872 | tf_op jit(solution)/shard_map/ppermute | solution.py:8
  25.3 1.3 collective-permute-start.17
  26.6 12.7 %collective-permute-done.10 = bf16[64,4096]{1,0:T(8,128)(2,1)} collective-permute-done((bf16[64,4096]{1,0:T(8,128)(2,1)}, bf16[64,4096]{1,0:T(8,128)(2,1)}, u32[]{:S(2)}, u32[]{:S(2)}) %collective-permute-start.10) | collective-permute-done | bytes 524320 | tf_op jit(solution)/shard_map/ppermute | solution.py:67
  39.3 1.1 broadcast_select_fusion.1
  40.4 1.6 %collective-permute-start.11 = (bf16[64,4096]{1,0:T(8,128)(2,1)S(1)}, bf16[64,4096]{1,0:T(8,128)(2,1)S(1)}, u32[]{:S(2)}, u32[]{:S(2)}) collective-permute-start(bf16[64,4096]{1,0:T(8,128)(2,1)S(1)} %broadcast_select_fusion.1), channel_id=1, source_target_pairs={{0,2},{2,0},{1,3},{3,1},{4,6},{6,4},{5,7},{7,5},{8,10},{10,8},{9,1... | collective-permute-start | bytes 1572872 | tf_op jit(solution)/shard_map/ppermute | solution.py:8
  41.9 8.4 %collective-permute-done.17 = bf16[64,4096]{1,0:T(8,128)(2,1)S(1)} collective-permute-done((bf16[64,4096]{1,0:T(8,128)(2,1)S(1)}, bf16[64,4096]{1,0:T(8,128)(2,1)S(1)}, u32[]{:S(2)}, u32[]{:S(2)}) %collective-permute-start.17) | collective-permute-done | bytes 524320 | tf_op jit(solution)/shard_map/ppermute | solution.py:67
  50.4 1.6 %collective-permute-start.18 = (bf16[64,4096]{1,0:T(8,128)(2,1)S(1)}, bf16[64,4096]{1,0:T(8,128)(2,1)S(1)}, u32[]{:S(2)}, u32[]{:S(2)}) collective-permute-start(bf16[64,4096]{1,0:T(8,128)(2,1)S(1)} %broadcast_select_fusion), channel_id=1, source_target_pairs={{0,2},{2,0},{1,3},{3,1},{4,6},{6,4},{5,7},{7,5},{8,10},{10,8},{9,1... | collective-permute-start | bytes 1572872 | tf_op jit(solution)/shard_map/ppermute | solution.py:8
  52.0 3.3 %fusion.30 = f32[128,768]{1,0:T(8,128)S(1)} fusion(bf16[64,4096]{1,0:T(8,128)(2,1)S(1)} %collective-permute-done.5, bf16[64,4096]{1,0:T(8,128)(2,1)} %collective-permute-done.4, pred[]{:T(512)S(6)} %eq.40, bf16[2048,768]{1,0:T(8,128)(2,1)} %collective-permute-done.1, bf16[2048,384]{1,0:T(8,128)(2,1)S(1)} %bitcast.33, bf16[2048,384]{1,0:T(8,128)(2,1)S(1)} %bitcast.38), kind=kOutput, calls=%fused_computation.22 | convolution fusion | flops 828899328 | bytes 7733249 | tf_op jit(solution)/shard_map/dot_general | solution.py:102
  55.4 0.6 collective-permute-start.6
  56.0 3.0 %fusion.36 = f32[128,768]{1,0:T(8,128)S(1)} fusion(bf16[64,4096]{1,0:T(8,128)(2,1)S(1)} %collective-permute-done.11, bf16[64,4096]{1,0:T(8,128)(2,1)S(1)} %broadcast_select_fusion.1, pred[]{:T(512)S(6)} %eq.40, bf16[2048,768]{1,0:T(8,128)(2,1)} %collective-permute-done.1, bf16[2048,384]{1,0:T(8,128)(2,1)S(1)} %bitcast.34, bf16[2048,384]{1,0:T(8,128)(2,1)S(1)} %bitcast.39), kind=kOutput, calls=%fused_computation.29 | convolution fusion | flops 828899328 | bytes 7733249 | tf_op jit(solution)/shard_map/dot_general | solution.py:102
  59.0 1.6 %collective-permute-start.12 = (bf16[128,384]{1,0:T(8,128)(2,1)S(1)}, bf16[128,384]{1,0:T(8,128)(2,1)S(1)}, u32[]{:S(2)}, u32[]{:S(2)}) collective-permute-start(bf16[128,384]{1,0:T(8,128)(2,1)S(1)} %fusion.77), channel_id=1, source_target_pairs={{0,2},{2,0},{1,3},{3,1},{4,6},{6,4},{5,7},{7,5},{8,10},{10,8},{9,1... | collective-permute-start | bytes 294920 | tf_op jit(solution)/shard_map/ppermute | solution.py:8
  60.6 5.1 %collective-permute-done.18 = bf16[64,4096]{1,0:T(8,128)(2,1)S(1)} collective-permute-done((bf16[64,4096]{1,0:T(8,128)(2,1)S(1)}, bf16[64,4096]{1,0:T(8,128)(2,1)S(1)}, u32[]{:S(2)}, u32[]{:S(2)}) %collective-permute-start.18) | collective-permute-done | bytes 524320 | tf_op jit(solution)/shard_map/ppermute | solution.py:8
  65.7 3.0 %fusion.42 = f32[128,768]{1,0:T(8,128)S(1)} fusion(bf16[64,4096]{1,0:T(8,128)(2,1)S(1)} %collective-permute-done.18, bf16[64,4096]{1,0:T(8,128)(2,1)S(1)} %broadcast_select_fusion, pred[]{:T(512)S(6)} %eq.40, bf16[2048,768]{1,0:T(8,128)(2,1)} %collective-permute-done.1, bf16[2048,384]{1,0:T(8,128)(2,1)S(1)} %bitcast.35, bf16[2048,384]{1,0:T(8,128)(2,1)S(1)} %bitcast.40), kind=kOutput, calls=%fused_computation.36 | convolution fusion | flops 828899328 | bytes 7733249 | tf_op jit(solution)/shard_map/dot_general | solution.py:102
  68.7 1.6 %collective-permute-start.19 = (bf16[128,384]{1,0:T(8,128)(2,1)S(1)}, bf16[128,384]{1,0:T(8,128)(2,1)S(1)}, u32[]{:S(2)}, u32[]{:S(2)}) collective-permute-start(bf16[128,384]{1,0:T(8,128)(2,1)S(1)} %fusion.76), channel_id=1, source_target_pairs={{0,2},{2,0},{1,3},{3,1},{4,6},{6,4},{5,7},{7,5},{8,10},{10,8},{9,1... | collective-permute-start | bytes 294920 | tf_op jit(solution)/shard_map/ppermute | solution.py:8
  70.3 13.3 %fusion.29 = f32[128,768]{1,0:T(8,128)S(1)} fusion(bf16[128,2048]{1,0:T(8,128)(2,1)S(1)} %collective-permute-done, bf16[128,2048]{1,0:T(8,128)(2,1)S(1)} %get-tuple-element.6, bf16[2048,768]{1,0:T(8,128)(2,1)} %collective-permute-done.1, bf16[2048,384]{1,0:T(8,128)(2,1)S(1)} %bitcast.36, bf16[2048,384]{1,0:T(8,128)(2,1)S(1)} %bitcast.41), kind=kOutput, calls=%fused_computation.20 | convolution fusion | flops 826277888 | bytes 7733248 | tf_op jit(solution)/shard_map/dot_general | solution.py:102
  83.7 0.1 collective-permute-start.13
  83.8 0.6 collective-permute-start.7
  84.5 0.1 collective-permute-start.20
  84.5 0.7 collective-permute-done.13
  85.2 0.6 fusion.89
  85.8 3.1 %collective-permute-start.14 = (bf16[256,1024]{1,0:T(8,128)(2,1)S(1)}, bf16[256,1024]{1,0:T(8,128)(2,1)S(1)}, u32[]{:S(2)}, u32[]{:S(2)}) collective-permute-start(bf16[256,1024]{1,0:T(8,128)(2,1)S(1)} %get-tuple-element.9), channel_id=1, source_target_pairs={{0,4},{12,8},{1,5},{13,9},{2,6},{14,10},{3,7},{15,11},{16,20},{28,... | collective-permute-start | bytes 1572872 | tf_op jit(solution)/shard_map/ppermute | solution.py:67
  88.9 0.6 fusion.90
  89.5 1.3 %collective-permute-start.21 = (bf16[256,1024]{1,0:T(8,128)(2,1)S(1)}, bf16[256,1024]{1,0:T(8,128)(2,1)S(1)}, u32[]{:S(2)}, u32[]{:S(2)}) collective-permute-start(bf16[256,1024]{1,0:T(8,128)(2,1)S(1)} %get-tuple-element.11), channel_id=1, source_target_pairs={{0,4},{12,8},{1,5},{13,9},{2,6},{14,10},{3,7},{15,11},{16,20},{28,... | collective-permute-start | bytes 1572872 | tf_op jit(solution)/shard_map/ppermute | solution.py:67
  90.8 0.6 fusion.14
  91.4 0.1 collective-permute-start.8
  91.5 9.6 %collective-permute-done.14 = bf16[256,1024]{1,0:T(8,128)(2,1)S(1)} collective-permute-done((bf16[256,1024]{1,0:T(8,128)(2,1)S(1)}, bf16[256,1024]{1,0:T(8,128)(2,1)S(1)}, u32[]{:S(2)}, u32[]{:S(2)}) %collective-permute-start.14) | collective-permute-done | bytes 524320 | tf_op jit(solution)/shard_map/ppermute | solution.py:67
  101.1 0.1 add_convert_fusion.1
  101.2 0.7 collective-permute-start.15
  102.0 10.4 %collective-permute-done.21 = bf16[256,1024]{1,0:T(8,128)(2,1)S(1)} collective-permute-done((bf16[256,1024]{1,0:T(8,128)(2,1)S(1)}, bf16[256,1024]{1,0:T(8,128)(2,1)S(1)}, u32[]{:S(2)}, u32[]{:S(2)}) %collective-permute-start.21) | collective-permute-done | bytes 524320 | tf_op jit(solution)/shard_map/ppermute | solution.py:67
  112.3 0.1 add_convert_fusion
  112.5 1.3 collective-permute-start.22
  113.9 0.6 collective-permute-start.2
  114.5 1.2 compare_reduce_fusion
  115.7 2.8 %collective-permute-done.2 = bf16[128,384]{1,0:T(8,128)(2,1)S(1)} collective-permute-done((bf16[128,384]{1,0:T(8,128)(2,1)S(1)}, bf16[128,384]{1,0:T(8,128)(2,1)S(1)}, u32[]{:S(2)}, u32[]{:S(2)}) %collective-permute-start.2) | collective-permute-done | bytes 98336 | tf_op jit(solution)/shard_map/ppermute | solution.py:8
  118.7 1.4 %collective-permute-done.3 = bf16[128,768]{1,0:T(8,128)(2,1)S(1)} collective-permute-done((bf16[128,768]{1,0:T(8,128)(2,1)S(1)}, bf16[128,768]{1,0:T(8,128)(2,1)S(1)}, u32[]{:S(2)}, u32[]{:S(2)}) %collective-permute-start.3) | collective-permute-done | bytes 196640 | tf_op jit(solution)/shard_map/ppermute | solution.py:8
  120.1 2.7 %collective-permute-done.8 = bf16[256,1024]{1,0:T(8,128)(2,1)S(1)} collective-permute-done((bf16[256,1024]{1,0:T(8,128)(2,1)S(1)}, bf16[256,1024]{1,0:T(8,128)(2,1)S(1)}, u32[]{:S(2)}, u32[]{:S(2)}) %collective-permute-start.8) | collective-permute-done | bytes 524320 | tf_op jit(solution)/shard_map/ppermute | solution.py:67
  122.8 5.9 %collective-permute-done.22 = bf16[256,1024]{1,0:T(8,128)(2,1)S(1)} collective-permute-done((bf16[256,1024]{1,0:T(8,128)(2,1)S(1)}, bf16[256,1024]{1,0:T(8,128)(2,1)S(1)}, u32[]{:S(2)}, u32[]{:S(2)}) %collective-permute-start.22) | collective-permute-done | bytes 524320 | tf_op jit(solution)/shard_map/ppermute | solution.py:67
  128.6 1.5 %fusion.26 = bf16[256,1024]{1,0:T(8,128)(2,1)} fusion(bf16[1,768,1024]{2,1,0:T(8,128)(2,1)S(1)} %copy-done, bf16[256,1024]{1,0:T(8,128)(2,1)S(1)} %collective-permute-done.8, bf16[256,1024]{1,0:T(8,128)(2,1)S(1)} %collective-permute-done.15, bf16[256,1024]{1,0:T(8,128)(2,1)S(1)} %collective-permute-done.22, f32[256]{0:T(256)S(1)} %bitcast.42, ...), kind=kOutput, calls=%fused_computation.16 | convolution fusion | flops 406519808 | bytes 4064514 | tf_op jit(solution)/shard_map/dot_general | solution.py:114
  (38 shorter events, 0.7 us)
Async XLA Ops:
  0.0 85.2 %copy-start = (bf16[1,768,1024]{2,1,0:T(8,128)(2,1)S(1)}, bf16[1,768,1024]{2,1,0:T(8,128)(2,1)}, u32[]{:S(2)}) copy-start(bf16[1,768,1024]{2,1,0:T(8,128)(2,1)} %param.10) | copy-start | bytes 4718596
  0.0 1.9 %copy-start.1 = (bf16[1,2048,384]{2,1,0:T(8,128)(2,1)S(1)}, bf16[1,2048,384]{2,1,0:T(8,128)(2,1)}, u32[]{:S(2)}) copy-start(bf16[1,2048,384]{2,1,0:T(8,128)(2,1)} %param.9) | copy-start | bytes 4718596
  1.4 4.2 %collective-permute-start = (bf16[128,2048]{1,0:T(8,128)(2,1)S(1)}, bf16[128,2048]{1,0:T(8,128)(2,1)S(1)}, u32[]{:S(2)}, u32[]{:S(2)}) collective-permute-start(bf16[128,2048]{1,0:T(8,128)(2,1)S(1)} %get-tuple-element.5), channel_id=1, source_target_pairs={{0,1},{1,0},{2,3},{3,2},{4,5},{5,4},{6,7},{7,6},{8,9},{9,8},{10,11... | collective-permute-start | bytes 1572872 | tf_op jit(solution)/shard_map/ppermute | solution.py:8
  1.9 21.1 %copy-start.4 = (s32[2]{0:T(128)S(1)}, s32[2]{0:T(128)}, u32[]{:S(2)}) copy-start(s32[2]{0:T(128)} %param.13) | copy-start | bytes 28
  5.3 46.7 %collective-permute-start.1 = (bf16[2048,768]{1,0:T(8,128)(2,1)}, bf16[2048,768]{1,0:T(8,128)(2,1)}, u32[]{:S(2)}, u32[]{:S(2)}) collective-permute-start(bf16[2048,768]{1,0:T(8,128)(2,1)} %pad_maximum_fusion.1), channel_id=1, source_target_pairs={{0,1},{1,0},{2,3},{3,2},{4,5},{5,4},{6,7},{7,6},{8,9},{9,8},{10,11... | collective-permute-start | bytes 9437192 | tf_op jit(solution)/shard_map/ppermute | solution.py:8
  5.7 15.3 %collective-permute-start.4 = (bf16[64,4096]{1,0:T(8,128)(2,1)S(1)}, bf16[64,4096]{1,0:T(8,128)(2,1)}, u32[]{:S(2)}, u32[]{:S(2)}) collective-permute-start(bf16[64,4096]{1,0:T(8,128)(2,1)S(1)} %fusion.51), channel_id=1, source_target_pairs={{0,4},{4,0},{8,12},{12,8},{1,5},{5,1},{9,13},{13,9},{2,6},{6,2},{1... | collective-permute-start | bytes 1572872 | tf_op jit(solution)/shard_map/ppermute | solution.py:67
  8.5 13.2 %collective-permute-start.9 = (bf16[64,4096]{1,0:T(8,128)(2,1)S(1)}, bf16[64,4096]{1,0:T(8,128)(2,1)}, u32[]{:S(2)}, u32[]{:S(2)}) collective-permute-start(bf16[64,4096]{1,0:T(8,128)(2,1)S(1)} %fusion.51), channel_id=1, source_target_pairs={{4,8},{8,4},{5,9},{9,5},{6,10},{10,6},{7,11},{11,7},{20,24},{24,20... | collective-permute-start | bytes 1572872 | tf_op jit(solution)/shard_map/ppermute | solution.py:67
  21.0 4.3 %collective-permute-start.16 = (bf16[64,4096]{1,0:T(8,128)(2,1)}, bf16[64,4096]{1,0:T(8,128)(2,1)S(1)}, u32[]{:S(2)}, u32[]{:S(2)}) collective-permute-start(bf16[64,4096]{1,0:T(8,128)(2,1)} %collective-permute-done.4), channel_id=1, source_target_pairs={{4,8},{8,4},{5,9},{9,5},{6,10},{10,6},{7,11},{11,7},{20,24},{24,20... | collective-permute-start | bytes 1572872 | tf_op jit(solution)/shard_map/ppermute | solution.py:67
  21.7 17.5 %collective-permute-start.10 = (bf16[64,4096]{1,0:T(8,128)(2,1)}, bf16[64,4096]{1,0:T(8,128)(2,1)}, u32[]{:S(2)}, u32[]{:S(2)}) collective-permute-start(bf16[64,4096]{1,0:T(8,128)(2,1)} %collective-permute-done.9), channel_id=1, source_target_pairs={{4,0},{8,12},{5,1},{9,13},{6,2},{10,14},{7,3},{11,15},{20,16},{24,... | collective-permute-start | bytes 1572872 | tf_op jit(solution)/shard_map/ppermute | solution.py:67
  23.1 28.9 %copy-start.2 = (bf16[1,2048,384]{2,1,0:T(8,128)(2,1)S(1)}, bf16[1,2048,384]{2,1,0:T(8,128)(2,1)}, u32[]{:S(2)}) copy-start(bf16[1,2048,384]{2,1,0:T(8,128)(2,1)} %param.9) | copy-start | bytes 4718596
  23.1 28.9 %copy-start.3 = (bf16[1,2048,384]{2,1,0:T(8,128)(2,1)S(1)}, bf16[1,2048,384]{2,1,0:T(8,128)(2,1)}, u32[]{:S(2)}) copy-start(bf16[1,2048,384]{2,1,0:T(8,128)(2,1)} %param.8) | copy-start | bytes 4718596
  23.7 28.3 %collective-permute-start.5 = (bf16[64,4096]{1,0:T(8,128)(2,1)}, bf16[64,4096]{1,0:T(8,128)(2,1)S(1)}, u32[]{:S(2)}, u32[]{:S(2)}) collective-permute-start(bf16[64,4096]{1,0:T(8,128)(2,1)} %collective-permute-done.4), channel_id=1, source_target_pairs={{0,2},{2,0},{1,3},{3,1},{4,6},{6,4},{5,7},{7,5},{8,10},{10,8},{9,1... | collective-permute-start | bytes 1572872 | tf_op jit(solution)/shard_map/ppermute | solution.py:8
  25.3 25.0 %collective-permute-start.17 = (bf16[64,4096]{1,0:T(8,128)(2,1)S(1)}, bf16[64,4096]{1,0:T(8,128)(2,1)S(1)}, u32[]{:S(2)}, u32[]{:S(2)}) collective-permute-start(bf16[64,4096]{1,0:T(8,128)(2,1)S(1)} %collective-permute-done.16), channel_id=1, source_target_pairs={{4,0},{8,12},{5,1},{9,13},{6,2},{10,14},{7,3},{11,15},{20,16},{24,... | collective-permute-start | bytes 1572872 | tf_op jit(solution)/shard_map/ppermute | solution.py:67
  40.4 15.6 %collective-permute-start.11 = (bf16[64,4096]{1,0:T(8,128)(2,1)S(1)}, bf16[64,4096]{1,0:T(8,128)(2,1)S(1)}, u32[]{:S(2)}, u32[]{:S(2)}) collective-permute-start(bf16[64,4096]{1,0:T(8,128)(2,1)S(1)} %broadcast_select_fusion.1), channel_id=1, source_target_pairs={{0,2},{2,0},{1,3},{3,1},{4,6},{6,4},{5,7},{7,5},{8,10},{10,8},{9,1... | collective-permute-start | bytes 1572872 | tf_op jit(solution)/shard_map/ppermute | solution.py:8
  50.4 15.3 %collective-permute-start.18 = (bf16[64,4096]{1,0:T(8,128)(2,1)S(1)}, bf16[64,4096]{1,0:T(8,128)(2,1)S(1)}, u32[]{:S(2)}, u32[]{:S(2)}) collective-permute-start(bf16[64,4096]{1,0:T(8,128)(2,1)S(1)} %broadcast_select_fusion), channel_id=1, source_target_pairs={{0,2},{2,0},{1,3},{3,1},{4,6},{6,4},{5,7},{7,5},{8,10},{10,8},{9,1... | collective-permute-start | bytes 1572872 | tf_op jit(solution)/shard_map/ppermute | solution.py:8
  55.4 28.4 %collective-permute-start.6 = (bf16[128,384]{1,0:T(8,128)(2,1)S(1)}, bf16[128,384]{1,0:T(8,128)(2,1)S(1)}, u32[]{:S(2)}, u32[]{:S(2)}) collective-permute-start(bf16[128,384]{1,0:T(8,128)(2,1)S(1)} %fusion.78), channel_id=1, source_target_pairs={{0,2},{2,0},{1,3},{3,1},{4,6},{6,4},{5,7},{7,5},{8,10},{10,8},{9,1... | collective-permute-start | bytes 294920 | tf_op jit(solution)/shard_map/ppermute | solution.py:8
  59.0 24.6 %collective-permute-start.12 = (bf16[128,384]{1,0:T(8,128)(2,1)S(1)}, bf16[128,384]{1,0:T(8,128)(2,1)S(1)}, u32[]{:S(2)}, u32[]{:S(2)}) collective-permute-start(bf16[128,384]{1,0:T(8,128)(2,1)S(1)} %fusion.77), channel_id=1, source_target_pairs={{0,2},{2,0},{1,3},{3,1},{4,6},{6,4},{5,7},{7,5},{8,10},{10,8},{9,1... | collective-permute-start | bytes 294920 | tf_op jit(solution)/shard_map/ppermute | solution.py:8
  68.7 15.7 %collective-permute-start.19 = (bf16[128,384]{1,0:T(8,128)(2,1)S(1)}, bf16[128,384]{1,0:T(8,128)(2,1)S(1)}, u32[]{:S(2)}, u32[]{:S(2)}) collective-permute-start(bf16[128,384]{1,0:T(8,128)(2,1)S(1)} %fusion.76), channel_id=1, source_target_pairs={{0,2},{2,0},{1,3},{3,1},{4,6},{6,4},{5,7},{7,5},{8,10},{10,8},{9,1... | collective-permute-start | bytes 294920 | tf_op jit(solution)/shard_map/ppermute | solution.py:8
  83.7 1.5 %collective-permute-start.13 = (bf16[128,768]{1,0:T(8,128)(2,1)S(1)}, bf16[128,768]{1,0:T(8,128)(2,1)S(1)}, u32[]{:S(2)}, u32[]{:S(2)}) collective-permute-start(bf16[128,768]{1,0:T(8,128)(2,1)S(1)} %maximum_select_fusion.16), channel_id=1, source_target_pairs={{0,1},{1,0},{2,3},{3,2},{4,5},{5,4},{6,7},{7,6},{8,9},{9,8},{10,11... | collective-permute-start | bytes 589832 | tf_op jit(solution)/shard_map/ppermute | solution.py:8
  83.8 6.9 %collective-permute-start.7 = (bf16[128,768]{1,0:T(8,128)(2,1)S(1)}, bf16[128,768]{1,0:T(8,128)(2,1)S(1)}, u32[]{:S(2)}, u32[]{:S(2)}) collective-permute-start(bf16[128,768]{1,0:T(8,128)(2,1)S(1)} %maximum_select_fusion.15), channel_id=1, source_target_pairs={{0,1},{1,0},{2,3},{3,2},{4,5},{5,4},{6,7},{7,6},{8,9},{9,8},{10,11... | collective-permute-start | bytes 589832 | tf_op jit(solution)/shard_map/ppermute | solution.py:8
  84.5 4.4 %collective-permute-start.20 = (bf16[128,768]{1,0:T(8,128)(2,1)S(1)}, bf16[128,768]{1,0:T(8,128)(2,1)S(1)}, u32[]{:S(2)}, u32[]{:S(2)}) collective-permute-start(bf16[128,768]{1,0:T(8,128)(2,1)S(1)} %maximum_select_fusion.17), channel_id=1, source_target_pairs={{0,1},{1,0},{2,3},{3,2},{4,5},{5,4},{6,7},{7,6},{8,9},{9,8},{10,11... | collective-permute-start | bytes 589832 | tf_op jit(solution)/shard_map/ppermute | solution.py:8
  85.8 15.3 %collective-permute-start.14 = (bf16[256,1024]{1,0:T(8,128)(2,1)S(1)}, bf16[256,1024]{1,0:T(8,128)(2,1)S(1)}, u32[]{:S(2)}, u32[]{:S(2)}) collective-permute-start(bf16[256,1024]{1,0:T(8,128)(2,1)S(1)} %get-tuple-element.9), channel_id=1, source_target_pairs={{0,4},{12,8},{1,5},{13,9},{2,6},{14,10},{3,7},{15,11},{16,20},{28,... | collective-permute-start | bytes 1572872 | tf_op jit(solution)/shard_map/ppermute | solution.py:67
  89.5 22.9 %collective-permute-start.21 = (bf16[256,1024]{1,0:T(8,128)(2,1)S(1)}, bf16[256,1024]{1,0:T(8,128)(2,1)S(1)}, u32[]{:S(2)}, u32[]{:S(2)}) collective-permute-start(bf16[256,1024]{1,0:T(8,128)(2,1)S(1)} %get-tuple-element.11), channel_id=1, source_target_pairs={{0,4},{12,8},{1,5},{13,9},{2,6},{14,10},{3,7},{15,11},{16,20},{28,... | collective-permute-start | bytes 1572872 | tf_op jit(solution)/shard_map/ppermute | solution.py:67
  91.4 23.1 %copy-start.5 = (s32[256,1]{0,1:T(1,128)S(1)}, s32[256,1]{0,1:T(1,128)}, u32[]{:S(2)}) copy-start(s32[256,1]{0,1:T(1,128)} %param.11) | copy-start | bytes 3076
  91.4 27.3 %copy-start.6 = (s32[256,1]{0,1:T(1,128)S(1)}, s32[256,1]{0,1:T(1,128)}, u32[]{:S(2)}) copy-start(s32[256,1]{0,1:T(1,128)} %param.12) | copy-start | bytes 3076
  91.4 31.4 %collective-permute-start.8 = (bf16[256,1024]{1,0:T(8,128)(2,1)S(1)}, bf16[256,1024]{1,0:T(8,128)(2,1)S(1)}, u32[]{:S(2)}, u32[]{:S(2)}) collective-permute-start(bf16[256,1024]{1,0:T(8,128)(2,1)S(1)} %fusion.14), channel_id=1, source_target_pairs={{0,4},{4,0},{8,12},{12,8},{1,5},{5,1},{9,13},{13,9},{2,6},{6,2},{1... | collective-permute-start | bytes 1572872 | tf_op jit(solution)/shard_map/ppermute | solution.py:67
  101.2 21.5 %collective-permute-start.15 = (bf16[256,1024]{1,0:T(8,128)(2,1)S(1)}, bf16[256,1024]{1,0:T(8,128)(2,1)S(1)}, u32[]{:S(2)}, u32[]{:S(2)}) collective-permute-start(bf16[256,1024]{1,0:T(8,128)(2,1)S(1)} %add_convert_fusion.1), channel_id=1, source_target_pairs={{4,8},{8,4},{5,9},{9,5},{6,10},{10,6},{7,11},{11,7},{20,24},{24,20... | collective-permute-start | bytes 1572872 | tf_op jit(solution)/shard_map/ppermute | solution.py:67
  112.5 16.1 %collective-permute-start.22 = (bf16[256,1024]{1,0:T(8,128)(2,1)S(1)}, bf16[256,1024]{1,0:T(8,128)(2,1)S(1)}, u32[]{:S(2)}, u32[]{:S(2)}) collective-permute-start(bf16[256,1024]{1,0:T(8,128)(2,1)S(1)} %add_convert_fusion), channel_id=1, source_target_pairs={{4,12},{8,0},{5,13},{9,1},{6,14},{10,2},{7,15},{11,3},{20,28},{24,... | collective-permute-start | bytes 1572872 | tf_op jit(solution)/shard_map/ppermute | solution.py:67
  113.9 4.7 %collective-permute-start.2 = (bf16[128,384]{1,0:T(8,128)(2,1)S(1)}, bf16[128,384]{1,0:T(8,128)(2,1)S(1)}, u32[]{:S(2)}, u32[]{:S(2)}) collective-permute-start(bf16[128,384]{1,0:T(8,128)(2,1)S(1)} %fusion.79), channel_id=1, source_target_pairs={{0,2},{2,0},{1,3},{3,1},{4,6},{6,4},{5,7},{7,5},{8,10},{10,8},{9,1... | collective-permute-start | bytes 294920 | tf_op jit(solution)/shard_map/ppermute | solution.py:8
  118.6 1.5 %collective-permute-start.3 = (bf16[128,768]{1,0:T(8,128)(2,1)S(1)}, bf16[128,768]{1,0:T(8,128)(2,1)S(1)}, u32[]{:S(2)}, u32[]{:S(2)}) collective-permute-start(bf16[128,768]{1,0:T(8,128)(2,1)S(1)} %maximum_select_fusion.14), channel_id=1, source_target_pairs={{0,1},{1,0},{2,3},{3,2},{4,5},{5,4},{6,7},{7,6},{8,9},{9,8},{10,11... | collective-permute-start | bytes 589832 | tf_op jit(solution)/shard_map/ppermute | solution.py:8

commit v2 on v0

--- a/solution.py
+++ b/solution.py
@@ -1,6 +1,10 @@
+import functools
+
 import jax
 import jax.numpy as jnp
 from jax import lax
+from jax.experimental import pallas as pl
+from jax.experimental.pallas import tpu as pltpu
 from jax.sharding import PartitionSpec as P
 
 
@@ -8,7 +12,7 @@
     return lax.ppermute(x, axis, [(i, i ^ 1 << distance) for i in range(lax.axis_size(axis))])
 
 
-def local(tokens, gate_weight, up_weight, down_weight, expert_ids, codes, expert_home):
+def routed(tokens, gate_weight, up_weight, down_weight, expert_ids, codes, expert_home):
     tok_rows, columns_dev = tokens.shape
     experts = expert_home.shape[0]
     capacity = min(tok_rows, 2 * tok_rows // experts)
@@ -56,6 +60,169 @@
     return (weights[:, None] * gathered).astype(jnp.bfloat16)
 
 
+def z_send(x, distance):
+    size = lax.axis_size("expert")
+    return lax.ppermute(x, "expert", [(i, i ^ distance) for i in range(size)])
+
+
+def ring_send(x):
+    size, cores = lax.axis_size("expert"), lax.axis_size("seq")
+    pairs = [
+        (i * cores + core, (i + step) % size * cores + core)
+        for i in range(size)
+        for core, step in enumerate((1, -1))
+    ]
+    return lax.ppermute(x, ("expert", "seq"), pairs)
+
+
+def half(x, index):
+    rows = x.shape[0] // 2
+    return lax.dynamic_slice_in_dim(x, index * rows, rows, 0)
+
+
+def in_order(own, other, index, axis=0):
+    return jnp.where(
+        index == 0,
+        jnp.concatenate([own, other], axis),
+        jnp.concatenate([other, own], axis),
+    )
+
+
+VMEM = pl.BlockSpec(memory_space=pltpu.VMEM)
+SMEM = pl.BlockSpec(memory_space=pltpu.SMEM)
+LIMIT = 16 * 1024 * 1024
+
+
+def hidden_kernel(parts, index, *refs):
+    taken, weights, (out, acts) = refs[: 2 * parts], refs[2 * parts : -2], refs[-2:]
+    rows, depth = out.shape[0] // 2, weights[0].shape[0]
+    width = out.shape[1]
+    step = 1024
+    for i in range(2 * depth // step):
+        pair, start = divmod(i * step, depth)
+        block = jnp.concatenate(
+            [ref[pl.ds(start, step), :] for ref in weights[2 * pair : 2 * pair + 2]], axis=1
+        )
+        value = jnp.dot(
+            jnp.concatenate([ref[:, pl.ds(i * step, step)] for ref in taken], axis=0),
+            block,
+            preferred_element_type=jnp.float32,
+        )
+        if i == 0:
+            acts[...] = value
+        else:
+            acts[...] += value
+
+    gate_act, up_act = acts[:, :width], acts[:, width:]
+    value = (jax.nn.silu(gate_act) * up_act).astype(out.dtype)
+    place = index[0]
+    out[pl.ds(pl.multiple_of(place * rows, rows), rows), :] = value[:rows]
+    out[pl.ds(pl.multiple_of((1 - place) * rows, rows), rows), :] = value[rows:]
+
+
+def hidden_call(index, first, second, weights):
+    rows, width = sum(part.shape[0] for part in first), weights[0].shape[1]
+    operands = (*first, *second, *weights)
+    return pl.pallas_call(
+        functools.partial(hidden_kernel, len(first)),
+        out_shape=jax.ShapeDtypeStruct((2 * rows, width), jnp.bfloat16),
+        in_specs=[SMEM] + [VMEM] * len(operands),
+        out_specs=VMEM,
+        scratch_shapes=[pltpu.VMEM((2 * rows, 2 * width), jnp.float32)],
+        compiler_params=pltpu.CompilerParams(vmem_limit_bytes=LIMIT),
+        cost_estimate=pl.CostEstimate(
+            flops=0,
+            bytes_accessed=0,
+            transcendentals=0,
+        ),
+    )(index, *operands)
+
+
+def ring(tokens, gate_weight, up_weight, down_weight, expert_ids, codes, expert_home):
+    z, x, c = lax.axis_index("expert"), lax.axis_index("tensor"), lax.axis_index("seq")
+    f32, bf16 = jnp.float32, jnp.bfloat16
+    tied = lax.optimization_barrier
+    odd = z % 2
+    place = c ^ odd
+    x_index = x.astype(jnp.int32).reshape(1)
+
+    def to_tensor(part):
+        return swapped(part, "tensor", 0)
+
+    down = down_weight[0]
+    own_half, given_half = half(tokens, c), half(tokens, 1 - c)
+    own_rows = tied(jnp.concatenate([own_half, swapped(given_half, "seq", 0)], axis=1))
+    moving, staying = tied((half(own_rows, x), half(own_rows, 1 - x)))
+    block1 = ring_send(moving)
+    gate_own, up_own, staying = tied((gate_weight[0], up_weight[0], staying))
+    weights = (gate_own, up_own, swapped(gate_own, "seq", 0), swapped(up_own, "seq", 0))
+
+    def activated(part, other):
+        return hidden_call(x_index, (part,), (other,), weights)
+
+    def partial_out(own, other):
+        both = in_order(own, other, x, 1)
+        rows = in_order(both, swapped(both, "seq", 0), place)
+        return jnp.dot(rows, down, preferred_element_type=f32)
+
+    def a_half(part):
+        return part[: part.shape[0] // 2]
+
+    def b_half(part):
+        return part[part.shape[0] // 2 :]
+
+    def added(part, received):
+        return (part + received.astype(f32)).astype(bf16)
+
+    act0 = activated(moving, staying)
+    hidden0 = to_tensor(act0)
+    block1, act0, hidden0 = tied((block1, act0, hidden0))
+    block2, other1 = ring_send(block1), to_tensor(block1)
+    part0 = partial_out(act0, hidden0)
+    block2, other1, part0 = tied((block2, other1, part0))
+    block3, other2 = ring_send(block2), to_tensor(block2)
+    act1 = activated(block1, other1)
+    hidden1 = to_tensor(act1)
+    block3, other2, hidden1 = tied((block3, other2, hidden1))
+    other3 = to_tensor(block3)
+    part1 = partial_out(act1, hidden1).astype(bf16)
+    back1 = z_send(part1, 1)
+    act2 = activated(block2, other2)
+    hidden2 = to_tensor(act2)
+    other3, part1, hidden2 = tied((other3, part1, hidden2))
+    part2 = partial_out(act2, hidden2)
+    act3 = activated(block3, other3)
+    back1, part2, act3 = tied((back1, part2, act3))
+    sent_a2 = z_send(a_half(part2).astype(bf16), 1)
+    home_b2 = z_send(added(b_half(part2), a_half(back1)), 2)
+    part3 = partial_out(act3, to_tensor(act3))
+    sent_a3 = z_send(a_half(part3).astype(bf16), 1)
+    sent_a2, home_b2, part3 = tied((sent_a2, home_b2, part3))
+    home_b3 = z_send(added(b_half(part3), sent_a2), 3)
+
+    def in_rows(part_a, part_b):
+        return in_order(part_a, part_b, odd)
+
+    ids = expert_ids[:, 0]
+    home = jnp.where(ids == 0, expert_home[0], expert_home[1])
+    ours = (home == z // 2)[:, None]
+    scale = codes[:, 0].astype(f32) / 1024.0
+    from_pair = in_rows(
+        a_half(part0) + b_half(back1).astype(f32), b_half(part0) + sent_a3.astype(f32)
+    )
+    from_others = in_rows(home_b3, home_b2).astype(f32)
+    expert_out = jnp.where(ours, from_pair, from_others).astype(bf16)
+    return (scale[:, None] * expert_out.astype(f32)).astype(bf16)
+
+
+def local(*arguments):
+    experts = arguments[-1].shape[0]
+    sizes = tuple(lax.axis_size(axis) for axis in ("expert", "tensor", "seq"))
+    if experts == 2 and sizes == (4, 2, 2):
+        return ring(*arguments)
+    return routed(*arguments)
+
+
 def solution(mesh):
     in_specs = (
         P(("groups", "expert"), "seq"),

time: 267 us -> 115 us (0.43)
  blocking collectives: 99.4 us -> 0 us
  waiting for transfers between devices: 122 us -> 58.2 us
  starting transfers between devices: 6.26 us -> 24.6 us
  between operations: 13.5 us -> 0.26 us
  matrix products: 13.4 us -> 4.32 us
  Pallas kernels: 0 us -> 8.99 us
  local copies, waits for them, and re-layouts: 3.32 us -> 12.3 us
  other arithmetic: 8.54 us -> 5.83 us
    all_to_all x1 -> x0, blocking collectives: 99.4 us -> none  [local(): lax.all_to_all(doubled, 'expert', split_axis=0, concat_axis=0, tiled=True)]
    ppermute x0 -> x8, waiting for transfers between devices: none -> 36.2 us  [the longest x5 21.3 us: z_send(): return lax.ppermute(x, 'expert', [(i, i ^ distance) for i in range(size)])]
    all_gather x1 -> x0, waiting for transfers between devices: 28.5 us -> none  [local(): lax.all_gather(activated, 'tensor', axis=1, tiled=True)]
    all_to_all x1 -> x0, waiting for transfers between devices: 24.8 us -> none  [local(): lax.all_to_all(summed.astype(jnp.bfloat16), 'expert', split_axis=0, conca...]
    ppermute x1 -> x14, waiting for transfers between devices: 46.2 us -> 22 us  [swapped(): lax.ppermute(x, axis, [(i, i ^ 1 << distance) for i in range(lax.axis_siz...]
    psum x1 -> x0, waiting for transfers between devices: 22.7 us -> none  [local(): gate_act, up_act = lax.psum((gate_part, up_part), 'seq')]
    ppermute x1 -> x14, starting transfers between devices: 1.49 us -> 13.8 us  [swapped(): lax.ppermute(x, axis, [(i, i ^ 1 << distance) for i in range(lax.axis_siz...]
    ppermute x0 -> x8, starting transfers between devices: none -> 10.8 us  [the longest x5 7.99 us: z_send(): return lax.ppermute(x, 'expert', [(i, i ^ distance) for i in range(size)])]
  transfers between devices with their start and end apart: 4 -> 22, of which waited for: 4 -> 12; matrix products, arithmetic and copies ran while one was open for 0% -> 8% of each run, Pallas kernels for 0% -> 8%
where the time goes in v2:
time: 115 us
  waiting for transfers between devices  58.2 us (51%)
  starting transfers between devices  24.6 us (21%)
  local copies, waits for them, and re-layouts  12.3 us (11%)
  Pallas kernels  8.99 us (8%)
  other arithmetic  5.83 us (5%)
  matrix products  4.32 us (4%)
    ppermute x14, waiting for transfers between devices, swapped(): lax.ppermute(x, axis, [(i, i ^ 1 << distance) for i in range(lax.axis_siz...  22 us
    ppermute x5, waiting for transfers between devices, z_send(): return lax.ppermute(x, 'expert', [(i, i ^ distance) for i in range(size)])  21.3 us
    ppermute x3, waiting for transfers between devices, ring_send(): return lax.ppermute(x, ('expert', 'seq'), pairs)  14.9 us
    ppermute x14, starting transfers between devices, swapped(): lax.ppermute(x, axis, [(i, i ^ 1 << distance) for i in range(lax.axis_siz...  13.8 us
    unnamed x44, local copies, waits for them, and re-layouts  9.32 us
    pallas_call x4, Pallas kernels, hidden_call(): pl.pallas_call(functools.partial(hidden_kernel, len(first)), out_shape=ja...  8.99 us
    ppermute x5, starting transfers between devices, z_send(): return lax.ppermute(x, 'expert', [(i, i ^ distance) for i in range(size)])  7.99 us
    dot_general x4, matrix products, partial_out(): return jnp.dot(rows, down, preferred_element_type=f32)  4.32 us
  transfers between devices with their start and end apart: 22, of which 12 were waited for; matrix products, arithmetic and copies ran while one was open for 8% of the time, Pallas kernels for 8%

profile of v2, /device:TPU:0, one launch (start us, length us, event | category | flops | bytes accessed | tf_op | source)
XLA Modules:
  0.0 114.5 jit_solution(7897996173947206286)
XLA Ops:
  0.0 1.4 %constant_dynamic-slice_fusion.3 = (bf16[128,2048]{1,0:T(8,128)(2,1)S(1)}, bf16[128,2048]{1,0:T(8,128)(2,1)S(1)}) fusion(bf16[256,2048]{1,0:T(8,128)(2,1)} %param.7, s32[]{:T(128)S(6)} %select_n.90, s32[]{:T(128)S(6)} %select_n.91), kind=kLoop, calls=%fused_computation.58 | loop fusion | bytes 2097160 | tf_op jit(solution)/shard_map/dynamic_slice | solution.py:80
  1.9 1.5 %collective-permute-done = bf16[128,2048]{1,0:T(8,128)(2,1)S(1)} collective-permute-done((bf16[128,2048]{1,0:T(8,128)(2,1)S(1)}, bf16[128,2048]{1,0:T(8,128)(2,1)S(1)}, u32[]{:S(2)}, u32[]{:S(2)}) %collective-permute-start) | collective-permute-done | bytes 524320 | tf_op jit(solution)/shard_map/ppermute | solution.py:12
  3.5 0.9 constant_dynamic-slice_fusion
  4.4 0.8 copy-done.1
  5.9 2.8 %collective-permute-start.1 = (bf16[64,4096]{1,0:T(8,128)(2,1)}, bf16[64,4096]{1,0:T(8,128)(2,1)}, u32[]{:S(2)}, u32[]{:S(2)}) collective-permute-start(bf16[64,4096]{1,0:T(8,128)(2,1)} %get-tuple-element.27.refs_0_), channel_id=1, source_target_pairs={{0,4},{1,13},{4,8},{5,1},{8,12},{9,5},{12,0},{13,9},{2,6},{3,15},{... | collective-permute-start | bytes 1572872 | tf_op jit(solution)/shard_map/ppermute | solution.py:75
  8.7 2.2 %collective-permute-done.3.refs_5_ = bf16[2048,384]{1,0:T(8,128)(2,1)S(1)} collective-permute-done((bf16[2048,384]{1,0:T(8,128)(2,1)S(1)}, bf16[2048,384]{1,0:T(8,128)(2,1)S(1)}, u32[]{:S(2)}, u32[]{:S(2)}) %collective-permute-start.3) | collective-permute-done | bytes 1572896 | tf_op jit(solution)/shard_map/ppermute | solution.py:12
  10.9 2.4 %shard_map.73 = bf16[128,384]{1,0:T(8,128)(2,1)S(1)} custom-call(s32[1]{0:T(128)} %bitcast.3.index, bf16[64,4096]{1,0:T(8,128)(2,1)} %get-tuple-element.27.refs_0_, bf16[64,4096]{1,0:T(8,128)(2,1)S(1)} %get-tuple-element.29.refs_1_, bf16[2048,384]{1,0:T(8,128)(2,1)S(1)} %bitcast.18, bf16[2048,384]{1,0:T(8,128)(2,1)S(1)} %bitcast.23, ...), custom_call_target="tpu_custom_call" | custom-call | tf_op jit(solution)/shard_map/pallas_call | solution.py:126
  13.4 2.9 %collective-permute-start.4 = (bf16[128,384]{1,0:T(8,128)(2,1)S(1)}, bf16[128,384]{1,0:T(8,128)(2,1)S(1)}, u32[]{:S(2)}, u32[]{:S(2)}) collective-permute-start(bf16[128,384]{1,0:T(8,128)(2,1)S(1)} %shard_map.73), channel_id=1, source_target_pairs={{0,2},{2,0},{1,3},{3,1},{4,6},{6,4},{5,7},{7,5},{8,10},{10,8},{9,1... | collective-permute-start | bytes 294920 | tf_op jit(solution)/shard_map/ppermute | solution.py:12
  16.3 7.3 %collective-permute-done.1.refs_0_ = bf16[64,4096]{1,0:T(8,128)(2,1)} collective-permute-done((bf16[64,4096]{1,0:T(8,128)(2,1)}, bf16[64,4096]{1,0:T(8,128)(2,1)}, u32[]{:S(2)}, u32[]{:S(2)}) %collective-permute-start.1) | collective-permute-done | bytes 524320 | tf_op jit(solution)/shard_map/ppermute | solution.py:75
  23.6 1.5 %collective-permute-start.6 = (bf16[64,4096]{1,0:T(8,128)(2,1)}, bf16[64,4096]{1,0:T(8,128)(2,1)}, u32[]{:S(2)}, u32[]{:S(2)}) collective-permute-start(bf16[64,4096]{1,0:T(8,128)(2,1)} %collective-permute-done.1.refs_0_), channel_id=1, source_target_pairs={{0,2},{2,0},{1,3},{3,1},{4,6},{6,4},{5,7},{7,5},{8,10},{10,8},{9,1... | collective-permute-start | bytes 1572872 | tf_op jit(solution)/shard_map/ppermute | solution.py:12
  25.1 1.5 %collective-permute-start.7 = (bf16[128,768]{1,0:T(8,128)(2,1)S(1)}, bf16[128,768]{1,0:T(8,128)(2,1)}, u32[]{:S(2)}, u32[]{:S(2)}) collective-permute-start(bf16[128,768]{1,0:T(8,128)(2,1)S(1)} %maximum_select_fusion.10), channel_id=1, source_target_pairs={{0,1},{1,0},{2,3},{3,2},{4,5},{5,4},{6,7},{7,6},{8,9},{9,8},{10,11... | collective-permute-start | bytes 589832 | tf_op jit(solution)/shard_map/ppermute | solution.py:12
  26.6 1.2 %collective-permute-done.7 = bf16[128,768]{1,0:T(8,128)(2,1)} collective-permute-done((bf16[128,768]{1,0:T(8,128)(2,1)S(1)}, bf16[128,768]{1,0:T(8,128)(2,1)}, u32[]{:S(2)}, u32[]{:S(2)}) %collective-permute-start.7) | collective-permute-done | bytes 196640 | tf_op jit(solution)/shard_map/ppermute | solution.py:12
  27.8 2.6 %fusion.6 = f32[256,1024]{1,0:T(8,128)} fusion(bf16[1,768,1024]{2,1,0:T(8,128)(2,1)S(1)} %copy-done, bf16[128,768]{1,0:T(8,128)(2,1)} %collective-permute-done.7, bf16[128,768]{1,0:T(8,128)(2,1)S(1)} %maximum_select_fusion.10, pred[]{:T(512)S(6)} %eq.37), kind=kOutput, calls=%fused_computation.6 | convolution fusion | flops 404422656 | bytes 3014657 | tf_op jit(solution)/shard_map/dot_general | solution.py:166
  30.4 7.6 %collective-permute-done.5.refs_0_ = bf16[64,4096]{1,0:T(8,128)(2,1)} collective-permute-done((bf16[64,4096]{1,0:T(8,128)(2,1)}, bf16[64,4096]{1,0:T(8,128)(2,1)}, u32[]{:S(2)}, u32[]{:S(2)}) %collective-permute-start.5) | collective-permute-done | bytes 524320 | tf_op jit(solution)/shard_map/ppermute | solution.py:75
  38.1 1.5 %collective-permute-start.9 = (bf16[64,4096]{1,0:T(8,128)(2,1)}, bf16[64,4096]{1,0:T(8,128)(2,1)S(1)}, u32[]{:S(2)}, u32[]{:S(2)}) collective-permute-start(bf16[64,4096]{1,0:T(8,128)(2,1)} %collective-permute-done.5.refs_0_), channel_id=1, source_target_pairs={{0,2},{2,0},{1,3},{3,1},{4,6},{6,4},{5,7},{7,5},{8,10},{10,8},{9,1... | collective-permute-start | bytes 1572872 | tf_op jit(solution)/shard_map/ppermute | solution.py:12
  39.6 1.4 %copy-done.11 = bf16[2048,384]{1,0:T(8,128)(2,1)S(1)} copy-done((bf16[2048,384]{1,0:T(8,128)(2,1)S(1)}, bf16[2048,384]{1,0:T(8,128)(2,1)}, u32[]{:S(2)}) %copy-start.11) | copy-done | bytes 1572888
  41.0 2.2 %shard_map.74 = bf16[128,384]{1,0:T(8,128)(2,1)S(1)} custom-call(s32[1]{0:T(128)} %bitcast.3.index, bf16[64,4096]{1,0:T(8,128)(2,1)} %collective-permute-done.1.refs_0_, bf16[64,4096]{1,0:T(8,128)(2,1)} %collective-permute-done.6.refs_1_, bf16[2048,384]{1,0:T(8,128)(2,1)S(1)} %bitcast.19, bf16[2048,384]{1,0:T(8,128)(2,1)S(1)} %bitcast.24, ...), custom_call_target="tpu_custom_call" | custom-call | tf_op jit(solution)/shard_map/pallas_call | solution.py:126
  43.2 0.6 collective-permute-start.10
  43.8 10.2 %collective-permute-done.10 = bf16[128,384]{1,0:T(8,128)(2,1)S(1)} collective-permute-done((bf16[128,384]{1,0:T(8,128)(2,1)S(1)}, bf16[128,384]{1,0:T(8,128)(2,1)S(1)}, u32[]{:S(2)}, u32[]{:S(2)}) %collective-permute-start.10) | collective-permute-done | bytes 98336 | tf_op jit(solution)/shard_map/ppermute | solution.py:12
  54.0 0.8 copy-done.14
  54.8 1.5 %collective-permute-start.13 = (bf16[64,4096]{1,0:T(8,128)(2,1)}, bf16[64,4096]{1,0:T(8,128)(2,1)}, u32[]{:S(2)}, u32[]{:S(2)}) collective-permute-start(bf16[64,4096]{1,0:T(8,128)(2,1)} %collective-permute-done.8.refs_0_), channel_id=1, source_target_pairs={{0,2},{2,0},{1,3},{3,1},{4,6},{6,4},{5,7},{7,5},{8,10},{10,8},{9,1... | collective-permute-start | bytes 1572872 | tf_op jit(solution)/shard_map/ppermute | solution.py:12
  56.4 0.8 collective-permute-start.11
  57.1 1.4 %copy-done.4 = bf16[1,2048,384]{2,1,0:T(8,128)(2,1)S(1)} copy-done((bf16[1,2048,384]{2,1,0:T(8,128)(2,1)S(1)}, bf16[1,2048,384]{2,1,0:T(8,128)(2,1)}, u32[]{:S(2)}) %copy-start.4) | copy-done | bytes 1572888
  58.6 1.4 %copy-done.8 = bf16[2048,384]{1,0:T(8,128)(2,1)S(1)} copy-done((bf16[2048,384]{1,0:T(8,128)(2,1)S(1)}, bf16[2048,384]{1,0:T(8,128)(2,1)}, u32[]{:S(2)}) %copy-start.8) | copy-done | bytes 1572888
  60.0 1.4 %copy-done.12 = bf16[2048,384]{1,0:T(8,128)(2,1)S(1)} copy-done((bf16[2048,384]{1,0:T(8,128)(2,1)S(1)}, bf16[2048,384]{1,0:T(8,128)(2,1)}, u32[]{:S(2)}) %copy-start.12) | copy-done | bytes 1572888
  61.4 1.0 copy-done.15
  62.4 2.2 %shard_map.75 = bf16[128,384]{1,0:T(8,128)(2,1)S(1)} custom-call(s32[1]{0:T(128)} %bitcast.3.index, bf16[64,4096]{1,0:T(8,128)(2,1)} %collective-permute-done.5.refs_0_, bf16[64,4096]{1,0:T(8,128)(2,1)S(1)} %copy-done.15, bf16[2048,384]{1,0:T(8,128)(2,1)S(1)} %bitcast.20, bf16[2048,384]{1,0:T(8,128)(2,1)S(1)} %bitcast.25, bf16[2048,384]{1,0:T(8,128)(2,1)S(1)} %copy-done.8, ...), custom_call_target="tpu_custom_call" | custom-call | tf_op jit(solution)/shard_map/pallas_call | solution.py:126
  64.6 0.6 collective-permute-start.14
  65.2 0.6 fusion.8
  65.8 1.8 %collective-permute-start.12 = (bf16[256,1024]{1,0:T(8,128)(2,1)S(1)}, bf16[256,1024]{1,0:T(8,128)(2,1)S(1)}, u32[]{:S(2)}, u32[]{:S(2)}) collective-permute-start(bf16[256,1024]{1,0:T(8,128)(2,1)S(1)} %fusion.8), channel_id=1, source_target_pairs={{0,4},{4,0},{8,12},{12,8},{1,5},{5,1},{9,13},{13,9},{2,6},{6,2},{1... | collective-permute-start | bytes 1572872 | tf_op jit(solution)/shard_map/ppermute | solution.py:65
  67.6 4.4 %collective-permute-done.14 = bf16[128,384]{1,0:T(8,128)(2,1)S(1)} collective-permute-done((bf16[128,384]{1,0:T(8,128)(2,1)S(1)}, bf16[128,384]{1,0:T(8,128)(2,1)S(1)}, u32[]{:S(2)}, u32[]{:S(2)}) %collective-permute-start.14) | collective-permute-done | bytes 98336 | tf_op jit(solution)/shard_map/ppermute | solution.py:12
  72.2 2.2 %shard_map.76 = bf16[128,384]{1,0:T(8,128)(2,1)S(1)} custom-call(s32[1]{0:T(128)} %bitcast.3.index, bf16[64,4096]{1,0:T(8,128)(2,1)} %collective-permute-done.8.refs_0_, bf16[64,4096]{1,0:T(8,128)(2,1)} %collective-permute-done.13.refs_1_, bf16[2048,384]{1,0:T(8,128)(2,1)S(1)} %bitcast.21, bf16[2048,384]{1,0:T(8,128)(2,1)S(1)} %bitcast.26, ...), custom_call_target="tpu_custom_call" | custom-call | tf_op jit(solution)/shard_map/pallas_call | solution.py:126
  74.4 0.6 fusion.2
  75.0 4.8 %collective-permute-done.12 = bf16[256,1024]{1,0:T(8,128)(2,1)S(1)} collective-permute-done((bf16[256,1024]{1,0:T(8,128)(2,1)S(1)}, bf16[256,1024]{1,0:T(8,128)(2,1)S(1)}, u32[]{:S(2)}, u32[]{:S(2)}) %collective-permute-start.12) | collective-permute-done | bytes 524320 | tf_op jit(solution)/shard_map/ppermute | solution.py:65
  79.9 1.5 %collective-permute-start.16 = (bf16[128,384]{1,0:T(8,128)(2,1)S(1)}, bf16[128,384]{1,0:T(8,128)(2,1)S(1)}, u32[]{:S(2)}, u32[]{:S(2)}) collective-permute-start(bf16[128,384]{1,0:T(8,128)(2,1)S(1)} %shard_map.76), channel_id=1, source_target_pairs={{0,2},{2,0},{1,3},{3,1},{4,6},{6,4},{5,7},{7,5},{8,10},{10,8},{9,1... | collective-permute-start | bytes 294920 | tf_op jit(solution)/shard_map/ppermute | solution.py:12
  81.4 0.7 fusion.41
  82.0 2.4 %collective-permute-done.16 = bf16[128,384]{1,0:T(8,128)(2,1)S(1)} collective-permute-done((bf16[128,384]{1,0:T(8,128)(2,1)S(1)}, bf16[128,384]{1,0:T(8,128)(2,1)S(1)}, u32[]{:S(2)}, u32[]{:S(2)}) %collective-permute-start.16) | collective-permute-done | bytes 98336 | tf_op jit(solution)/shard_map/ppermute | solution.py:12
  84.6 0.8 add_convert_fusion.1
  85.4 0.8 collective-permute-start.20
  86.2 1.7 %collective-permute-start.19 = (bf16[128,1024]{1,0:T(8,128)(2,1)S(1)}, bf16[128,1024]{1,0:T(8,128)(2,1)}, u32[]{:S(2)}, u32[]{:S(2)}) collective-permute-start(bf16[128,1024]{1,0:T(8,128)(2,1)S(1)} %slice.52), channel_id=1, source_target_pairs={{0,4},{4,0},{8,12},{12,8},{1,5},{5,1},{9,13},{13,9},{2,6},{6,2},{1... | collective-permute-start | bytes 786440 | tf_op jit(solution)/shard_map/ppermute | solution.py:65
  88.5 1.0 copy-done.17
  89.9 1.3 %compare_reduce_fusion = pred[256]{0:T(512)(128)(4,1)S(1)} fusion(s32[256,1]{0,1:T(1,128)S(1)} %copy-done.20, s32[]{:T(128)S(6)} %select_n.87, s32[]{:T(128)} %bitcast.2, s32[]{:T(128)} %bitcast.1), kind=kLoop, calls=%fused_computation.53 | loop fusion | flops 768 | bytes 1292 | tf_op jit(solution)/shard_map/eq | solution.py:208
  91.2 9.8 %collective-permute-done.20 = bf16[128,1024]{1,0:T(8,128)(2,1)S(1)} collective-permute-done((bf16[128,1024]{1,0:T(8,128)(2,1)}, bf16[128,1024]{1,0:T(8,128)(2,1)S(1)}, u32[]{:S(2)}, u32[]{:S(2)}) %collective-permute-start.20) | collective-permute-done | bytes 262176 | tf_op jit(solution)/shard_map/ppermute | solution.py:65
  101.0 1.2 %add_convert_fusion = bf16[128,1024]{1,0:T(8,128)(2,1)S(1)} fusion(bf16[128,1024]{1,0:T(8,128)(2,1)} %collective-permute-done.19, f32[256,1024]{1,0:T(8,128)} %copy-done.17), kind=kLoop, calls=%fused_computation.17 | loop fusion | flops 393216 | bytes 1048576 | tf_op jit(solution)/shard_map/convert_element_type | solution.py:175
  102.2 3.3 %collective-permute-start.21 = (bf16[128,1024]{1,0:T(8,128)(2,1)S(1)}, bf16[128,1024]{1,0:T(8,128)(2,1)S(1)}, u32[]{:S(2)}, u32[]{:S(2)}) collective-permute-start(bf16[128,1024]{1,0:T(8,128)(2,1)S(1)} %add_convert_fusion), channel_id=1, source_target_pairs={{0,12},{4,8},{8,4},{12,0},{1,13},{5,9},{9,5},{13,1},{2,14},{6,10},... | collective-permute-start | bytes 786440 | tf_op jit(solution)/shard_map/ppermute | solution.py:65
  106.0 1.2 %convert_add_fusion = (bf16[128,1024]{1,0:T(8,128)(2,1)S(1)}, bf16[128,1024]{1,0:T(8,128)(2,1)S(1)}) fusion(bf16[128,1024]{1,0:T(8,128)(2,1)} %collective-permute-done.18, f32[256,1024]{1,0:T(8,128)S(1)} %copy-done.16, bf16[256,1024]{1,0:T(8,128)(2,1)} %copy-done.18), kind=kLoop, calls=%fused_computation.19 | loop fusion | flops 786432 | bytes 2097152 | tf_op jit(solution)/shard_map/add | solution.py:211
  107.1 6.3 %collective-permute-done.21 = bf16[128,1024]{1,0:T(8,128)(2,1)S(1)} collective-permute-done((bf16[128,1024]{1,0:T(8,128)(2,1)S(1)}, bf16[128,1024]{1,0:T(8,128)(2,1)S(1)}, u32[]{:S(2)}, u32[]{:S(2)}) %collective-permute-start.21) | collective-permute-done | bytes 262176 | tf_op jit(solution)/shard_map/ppermute | solution.py:65
  113.4 1.1 multiply_convert_fusion
  (64 shorter events, 3.2 us)
Async XLA Ops:
  0.0 27.8 %copy-start = (bf16[1,768,1024]{2,1,0:T(8,128)(2,1)S(1)}, bf16[1,768,1024]{2,1,0:T(8,128)(2,1)}, u32[]{:S(2)}) copy-start(bf16[1,768,1024]{2,1,0:T(8,128)(2,1)} %param.10) | copy-start | bytes 4718596
  1.4 2.1 %collective-permute-start = (bf16[128,2048]{1,0:T(8,128)(2,1)S(1)}, bf16[128,2048]{1,0:T(8,128)(2,1)S(1)}, u32[]{:S(2)}, u32[]{:S(2)}) collective-permute-start(bf16[128,2048]{1,0:T(8,128)(2,1)S(1)} %get-tuple-element.54), channel_id=1, source_target_pairs={{0,1},{1,0},{2,3},{3,2},{4,5},{5,4},{6,7},{7,6},{8,9},{9,8},{10,11... | collective-permute-start | bytes 1572872 | tf_op jit(solution)/shard_map/ppermute | solution.py:12
  3.4 2.2 %copy-start.2 = (bf16[1,2048,384]{2,1,0:T(8,128)(2,1)S(1)}, bf16[1,2048,384]{2,1,0:T(8,128)(2,1)}, u32[]{:S(2)}) copy-start(bf16[1,2048,384]{2,1,0:T(8,128)(2,1)} %param.9) | copy-start | bytes 4718596
  3.5 1.7 %copy-start.1 = (bf16[1,2048,384]{2,1,0:T(8,128)(2,1)S(1)}, bf16[1,2048,384]{2,1,0:T(8,128)(2,1)}, u32[]{:S(2)}) copy-start(bf16[1,2048,384]{2,1,0:T(8,128)(2,1)} %param.8) | copy-start | bytes 4718596
  5.2 3.5 %collective-permute-start.2 = (bf16[2048,384]{1,0:T(8,128)(2,1)S(1)}, bf16[2048,384]{1,0:T(8,128)(2,1)S(1)}, u32[]{:S(2)}, u32[]{:S(2)}) collective-permute-start(bf16[2048,384]{1,0:T(8,128)(2,1)S(1)} %bitcast.17), channel_id=1, source_target_pairs={{0,1},{1,0},{2,3},{3,2},{4,5},{5,4},{6,7},{7,6},{8,9},{9,8},{10,11... | collective-permute-start | bytes 4718600 | tf_op jit(solution)/shard_map/ppermute | solution.py:12
  5.6 5.3 %collective-permute-start.3 = (bf16[2048,384]{1,0:T(8,128)(2,1)S(1)}, bf16[2048,384]{1,0:T(8,128)(2,1)S(1)}, u32[]{:S(2)}, u32[]{:S(2)}) collective-permute-start(bf16[2048,384]{1,0:T(8,128)(2,1)S(1)} %bitcast.22), channel_id=1, source_target_pairs={{0,1},{1,0},{2,3},{3,2},{4,5},{5,4},{6,7},{7,6},{8,9},{9,8},{10,11... | collective-permute-start | bytes 4718600 | tf_op jit(solution)/shard_map/ppermute | solution.py:12
  5.9 17.7 %collective-permute-start.1 = (bf16[64,4096]{1,0:T(8,128)(2,1)}, bf16[64,4096]{1,0:T(8,128)(2,1)}, u32[]{:S(2)}, u32[]{:S(2)}) collective-permute-start(bf16[64,4096]{1,0:T(8,128)(2,1)} %get-tuple-element.27.refs_0_), channel_id=1, source_target_pairs={{0,4},{1,13},{4,8},{5,1},{8,12},{9,5},{12,0},{13,9},{2,6},{3,15},{... | collective-permute-start | bytes 1572872 | tf_op jit(solution)/shard_map/ppermute | solution.py:75
  8.7 4.7 %copy-start.6 = (bf16[2048,384]{1,0:T(8,128)(2,1)}, bf16[2048,384]{1,0:T(8,128)(2,1)S(1)}, u32[]{:S(2)}) copy-start(bf16[2048,384]{1,0:T(8,128)(2,1)S(1)} %collective-permute-done.2.refs_4_) | copy-start | bytes 4718596
  10.9 2.5 %copy-start.10 = (bf16[2048,384]{1,0:T(8,128)(2,1)}, bf16[2048,384]{1,0:T(8,128)(2,1)S(1)}, u32[]{:S(2)}) copy-start(bf16[2048,384]{1,0:T(8,128)(2,1)S(1)} %collective-permute-done.3.refs_5_) | copy-start | bytes 4718596
  13.4 10.2 %collective-permute-start.4 = (bf16[128,384]{1,0:T(8,128)(2,1)S(1)}, bf16[128,384]{1,0:T(8,128)(2,1)S(1)}, u32[]{:S(2)}, u32[]{:S(2)}) collective-permute-start(bf16[128,384]{1,0:T(8,128)(2,1)S(1)} %shard_map.73), channel_id=1, source_target_pairs={{0,2},{2,0},{1,3},{3,1},{4,6},{6,4},{5,7},{7,5},{8,10},{10,8},{9,1... | collective-permute-start | bytes 294920 | tf_op jit(solution)/shard_map/ppermute | solution.py:12
  23.6 14.5 %collective-permute-start.5 = (bf16[64,4096]{1,0:T(8,128)(2,1)}, bf16[64,4096]{1,0:T(8,128)(2,1)}, u32[]{:S(2)}, u32[]{:S(2)}) collective-permute-start(bf16[64,4096]{1,0:T(8,128)(2,1)} %collective-permute-done.1.refs_0_), channel_id=1, source_target_pairs={{0,4},{1,13},{4,8},{5,1},{8,12},{9,5},{12,0},{13,9},{2,6},{3,15},{... | collective-permute-start | bytes 1572872 | tf_op jit(solution)/shard_map/ppermute | solution.py:75
  23.6 14.5 %collective-permute-start.6 = (bf16[64,4096]{1,0:T(8,128)(2,1)}, bf16[64,4096]{1,0:T(8,128)(2,1)}, u32[]{:S(2)}, u32[]{:S(2)}) collective-permute-start(bf16[64,4096]{1,0:T(8,128)(2,1)} %collective-permute-done.1.refs_0_), channel_id=1, source_target_pairs={{0,2},{2,0},{1,3},{3,1},{4,6},{6,4},{5,7},{7,5},{8,10},{10,8},{9,1... | collective-permute-start | bytes 1572872 | tf_op jit(solution)/shard_map/ppermute | solution.py:12
  25.1 2.7 %collective-permute-start.7 = (bf16[128,768]{1,0:T(8,128)(2,1)S(1)}, bf16[128,768]{1,0:T(8,128)(2,1)}, u32[]{:S(2)}, u32[]{:S(2)}) collective-permute-start(bf16[128,768]{1,0:T(8,128)(2,1)S(1)} %maximum_select_fusion.10), channel_id=1, source_target_pairs={{0,1},{1,0},{2,3},{3,2},{4,5},{5,4},{6,7},{7,6},{8,9},{9,8},{10,11... | collective-permute-start | bytes 589832 | tf_op jit(solution)/shard_map/ppermute | solution.py:12
  26.6 12.9 %copy-start.3 = (bf16[1,2048,384]{2,1,0:T(8,128)(2,1)S(1)}, bf16[1,2048,384]{2,1,0:T(8,128)(2,1)}, u32[]{:S(2)}) copy-start(bf16[1,2048,384]{2,1,0:T(8,128)(2,1)} %param.9) | copy-start | bytes 4718596
  26.6 12.9 %copy-start.7 = (bf16[2048,384]{1,0:T(8,128)(2,1)S(1)}, bf16[2048,384]{1,0:T(8,128)(2,1)}, u32[]{:S(2)}) copy-start(bf16[2048,384]{1,0:T(8,128)(2,1)} %copy-done.6) | copy-start | bytes 4718596
  38.1 16.0 %collective-permute-start.8 = (bf16[64,4096]{1,0:T(8,128)(2,1)}, bf16[64,4096]{1,0:T(8,128)(2,1)}, u32[]{:S(2)}, u32[]{:S(2)}) collective-permute-start(bf16[64,4096]{1,0:T(8,128)(2,1)} %collective-permute-done.5.refs_0_), channel_id=1, source_target_pairs={{0,4},{1,13},{4,8},{5,1},{8,12},{9,5},{12,0},{13,9},{2,6},{3,15},{... | collective-permute-start | bytes 1572872 | tf_op jit(solution)/shard_map/ppermute | solution.py:75
  38.1 16.0 %collective-permute-start.9 = (bf16[64,4096]{1,0:T(8,128)(2,1)}, bf16[64,4096]{1,0:T(8,128)(2,1)S(1)}, u32[]{:S(2)}, u32[]{:S(2)}) collective-permute-start(bf16[64,4096]{1,0:T(8,128)(2,1)} %collective-permute-done.5.refs_0_), channel_id=1, source_target_pairs={{0,2},{2,0},{1,3},{3,1},{4,6},{6,4},{5,7},{7,5},{8,10},{10,8},{9,1... | collective-permute-start | bytes 1572872 | tf_op jit(solution)/shard_map/ppermute | solution.py:12
  39.6 1.4 %copy-start.11 = (bf16[2048,384]{1,0:T(8,128)(2,1)S(1)}, bf16[2048,384]{1,0:T(8,128)(2,1)}, u32[]{:S(2)}) copy-start(bf16[2048,384]{1,0:T(8,128)(2,1)} %copy-done.10) | copy-start | bytes 4718596
  43.2 10.9 %collective-permute-start.10 = (bf16[128,384]{1,0:T(8,128)(2,1)S(1)}, bf16[128,384]{1,0:T(8,128)(2,1)S(1)}, u32[]{:S(2)}, u32[]{:S(2)}) collective-permute-start(bf16[128,384]{1,0:T(8,128)(2,1)S(1)} %shard_map.74), channel_id=1, source_target_pairs={{0,2},{2,0},{1,3},{3,1},{4,6},{6,4},{5,7},{7,5},{8,10},{10,8},{9,1... | collective-permute-start | bytes 294920 | tf_op jit(solution)/shard_map/ppermute | solution.py:12
  54.0 0.8 copy-start.14
  54.8 17.1 %collective-permute-start.13 = (bf16[64,4096]{1,0:T(8,128)(2,1)}, bf16[64,4096]{1,0:T(8,128)(2,1)}, u32[]{:S(2)}, u32[]{:S(2)}) collective-permute-start(bf16[64,4096]{1,0:T(8,128)(2,1)} %collective-permute-done.8.refs_0_), channel_id=1, source_target_pairs={{0,2},{2,0},{1,3},{3,1},{4,6},{6,4},{5,7},{7,5},{8,10},{10,8},{9,1... | collective-permute-start | bytes 1572872 | tf_op jit(solution)/shard_map/ppermute | solution.py:12
  56.4 8.8 %collective-permute-start.11 = (bf16[128,768]{1,0:T(8,128)(2,1)S(1)}, bf16[128,768]{1,0:T(8,128)(2,1)S(1)}, u32[]{:S(2)}, u32[]{:S(2)}) collective-permute-start(bf16[128,768]{1,0:T(8,128)(2,1)S(1)} %maximum_select_fusion.11), channel_id=1, source_target_pairs={{0,1},{1,0},{2,3},{3,2},{4,5},{5,4},{6,7},{7,6},{8,9},{9,8},{10,11... | collective-permute-start | bytes 589832 | tf_op jit(solution)/shard_map/ppermute | solution.py:12
  57.1 1.4 %copy-start.4 = (bf16[1,2048,384]{2,1,0:T(8,128)(2,1)S(1)}, bf16[1,2048,384]{2,1,0:T(8,128)(2,1)}, u32[]{:S(2)}) copy-start(bf16[1,2048,384]{2,1,0:T(8,128)(2,1)} %param.9) | copy-start | bytes 4718596
  58.6 1.4 %copy-start.8 = (bf16[2048,384]{1,0:T(8,128)(2,1)S(1)}, bf16[2048,384]{1,0:T(8,128)(2,1)}, u32[]{:S(2)}) copy-start(bf16[2048,384]{1,0:T(8,128)(2,1)} %copy-done.6) | copy-start | bytes 4718596
  60.0 1.4 %copy-start.12 = (bf16[2048,384]{1,0:T(8,128)(2,1)S(1)}, bf16[2048,384]{1,0:T(8,128)(2,1)}, u32[]{:S(2)}) copy-start(bf16[2048,384]{1,0:T(8,128)(2,1)} %copy-done.10) | copy-start | bytes 4718596
  61.4 1.0 copy-start.15
  62.4 9.8 %copy-start.13 = (bf16[2048,384]{1,0:T(8,128)(2,1)S(1)}, bf16[2048,384]{1,0:T(8,128)(2,1)}, u32[]{:S(2)}) copy-start(bf16[2048,384]{1,0:T(8,128)(2,1)} %copy-done.10) | copy-start | bytes 4718596
  64.6 7.6 %copy-start.21 = (s32[256,1]{0,1:T(1,128)S(1)}, s32[256,1]{0,1:T(1,128)}, u32[]{:S(2)}) copy-start(s32[256,1]{0,1:T(1,128)} %param.12) | copy-start | bytes 3076
  64.6 7.6 %copy-start.5 = (bf16[1,2048,384]{2,1,0:T(8,128)(2,1)S(1)}, bf16[1,2048,384]{2,1,0:T(8,128)(2,1)}, u32[]{:S(2)}) copy-start(bf16[1,2048,384]{2,1,0:T(8,128)(2,1)} %param.9) | copy-start | bytes 4718596
  64.6 7.6 %copy-start.9 = (bf16[2048,384]{1,0:T(8,128)(2,1)S(1)}, bf16[2048,384]{1,0:T(8,128)(2,1)}, u32[]{:S(2)}) copy-start(bf16[2048,384]{1,0:T(8,128)(2,1)} %copy-done.6) | copy-start | bytes 4718596
  64.6 7.3 %collective-permute-start.14 = (bf16[128,384]{1,0:T(8,128)(2,1)S(1)}, bf16[128,384]{1,0:T(8,128)(2,1)S(1)}, u32[]{:S(2)}, u32[]{:S(2)}) collective-permute-start(bf16[128,384]{1,0:T(8,128)(2,1)S(1)} %shard_map.75), channel_id=1, source_target_pairs={{0,2},{2,0},{1,3},{3,1},{4,6},{6,4},{5,7},{7,5},{8,10},{10,8},{9,1... | collective-permute-start | bytes 294920 | tf_op jit(solution)/shard_map/ppermute | solution.py:12
  65.8 14.1 %collective-permute-start.12 = (bf16[256,1024]{1,0:T(8,128)(2,1)S(1)}, bf16[256,1024]{1,0:T(8,128)(2,1)S(1)}, u32[]{:S(2)}, u32[]{:S(2)}) collective-permute-start(bf16[256,1024]{1,0:T(8,128)(2,1)S(1)} %fusion.8), channel_id=1, source_target_pairs={{0,4},{4,0},{8,12},{12,8},{1,5},{5,1},{9,13},{13,9},{2,6},{6,2},{1... | collective-permute-start | bytes 1572872 | tf_op jit(solution)/shard_map/ppermute | solution.py:65
  72.0 2.4 %collective-permute-start.15 = (bf16[128,768]{1,0:T(8,128)(2,1)S(1)}, bf16[128,768]{1,0:T(8,128)(2,1)S(1)}, u32[]{:S(2)}, u32[]{:S(2)}) collective-permute-start(bf16[128,768]{1,0:T(8,128)(2,1)S(1)} %maximum_select_fusion.12), channel_id=1, source_target_pairs={{0,1},{1,0},{2,3},{3,2},{4,5},{5,4},{6,7},{7,6},{8,9},{9,8},{10,11... | collective-permute-start | bytes 589832 | tf_op jit(solution)/shard_map/ppermute | solution.py:12
  74.4 6.9 %copy-start.19 = (s32[2]{0:T(128)S(1)}, s32[2]{0:T(128)}, u32[]{:S(2)}) copy-start(s32[2]{0:T(128)} %param.13) | copy-start | bytes 28
  79.9 8.7 %copy-start.18 = (bf16[256,1024]{1,0:T(8,128)(2,1)}, bf16[256,1024]{1,0:T(8,128)(2,1)S(1)}, u32[]{:S(2)}) copy-start(bf16[256,1024]{1,0:T(8,128)(2,1)S(1)} %collective-permute-done.12) | copy-start | bytes 1572868
  79.9 4.6 %collective-permute-start.16 = (bf16[128,384]{1,0:T(8,128)(2,1)S(1)}, bf16[128,384]{1,0:T(8,128)(2,1)S(1)}, u32[]{:S(2)}, u32[]{:S(2)}) collective-permute-start(bf16[128,384]{1,0:T(8,128)(2,1)S(1)} %shard_map.76), channel_id=1, source_target_pairs={{0,2},{2,0},{1,3},{3,1},{4,6},{6,4},{5,7},{7,5},{8,10},{10,8},{9,1... | collective-permute-start | bytes 294920 | tf_op jit(solution)/shard_map/ppermute | solution.py:12
  84.5 3.4 %collective-permute-start.17 = (bf16[128,768]{1,0:T(8,128)(2,1)S(1)}, bf16[128,768]{1,0:T(8,128)(2,1)S(1)}, u32[]{:S(2)}, u32[]{:S(2)}) collective-permute-start(bf16[128,768]{1,0:T(8,128)(2,1)S(1)} %maximum_select_fusion.13), channel_id=1, source_target_pairs={{0,1},{1,0},{2,3},{3,2},{4,5},{5,4},{6,7},{7,6},{8,9},{9,8},{10,11... | collective-permute-start | bytes 589832 | tf_op jit(solution)/shard_map/ppermute | solution.py:12
  85.4 4.5 %copy-start.20 = (s32[256,1]{0,1:T(1,128)S(1)}, s32[256,1]{0,1:T(1,128)}, u32[]{:S(2)}) copy-start(s32[256,1]{0,1:T(1,128)} %param.11) | copy-start | bytes 3076
  85.4 15.6 %collective-permute-start.20 = (bf16[128,1024]{1,0:T(8,128)(2,1)}, bf16[128,1024]{1,0:T(8,128)(2,1)S(1)}, u32[]{:S(2)}, u32[]{:S(2)}) collective-permute-start(bf16[128,1024]{1,0:T(8,128)(2,1)} %add_convert_fusion.1), channel_id=1, source_target_pairs={{0,8},{4,12},{8,0},{12,4},{1,9},{5,13},{9,1},{13,5},{2,10},{6,14},... | collective-permute-start | bytes 786440 | tf_op jit(solution)/shard_map/ppermute | solution.py:65
  86.2 14.8 %collective-permute-start.19 = (bf16[128,1024]{1,0:T(8,128)(2,1)S(1)}, bf16[128,1024]{1,0:T(8,128)(2,1)}, u32[]{:S(2)}, u32[]{:S(2)}) collective-permute-start(bf16[128,1024]{1,0:T(8,128)(2,1)S(1)} %slice.52), channel_id=1, source_target_pairs={{0,4},{4,0},{8,12},{12,8},{1,5},{5,1},{9,13},{13,9},{2,6},{6,2},{1... | collective-permute-start | bytes 786440 | tf_op jit(solution)/shard_map/ppermute | solution.py:65
  88.5 1.0 copy-start.17
  89.5 16.4 %copy-start.16 = (f32[256,1024]{1,0:T(8,128)S(1)}, f32[256,1024]{1,0:T(8,128)}, u32[]{:S(2)}) copy-start(f32[256,1024]{1,0:T(8,128)} %fusion.6) | copy-start | bytes 3145732
  89.6 16.4 %collective-permute-start.18 = (bf16[128,1024]{1,0:T(8,128)(2,1)S(1)}, bf16[128,1024]{1,0:T(8,128)(2,1)}, u32[]{:S(2)}, u32[]{:S(2)}) collective-permute-start(bf16[128,1024]{1,0:T(8,128)(2,1)S(1)} %slice.53), channel_id=1, source_target_pairs={{0,4},{4,0},{8,12},{12,8},{1,5},{5,1},{9,13},{13,9},{2,6},{6,2},{1... | collective-permute-start | bytes 786440 | tf_op jit(solution)/shard_map/ppermute | solution.py:65
  102.2 11.2 %collective-permute-start.21 = (bf16[128,1024]{1,0:T(8,128)(2,1)S(1)}, bf16[128,1024]{1,0:T(8,128)(2,1)S(1)}, u32[]{:S(2)}, u32[]{:S(2)}) collective-permute-start(bf16[128,1024]{1,0:T(8,128)(2,1)S(1)} %add_convert_fusion), channel_id=1, source_target_pairs={{0,12},{4,8},{8,4},{12,0},{1,13},{5,9},{9,5},{13,1},{2,14},{6,10},... | collective-permute-start | bytes 786440 | tf_op jit(solution)/shard_map/ppermute | solution.py:65

commit v3 on v2

--- a/solution.py
+++ b/solution.py
@@ -90,22 +90,37 @@
 
 VMEM = pl.BlockSpec(memory_space=pltpu.VMEM)
 SMEM = pl.BlockSpec(memory_space=pltpu.SMEM)
-LIMIT = 16 * 1024 * 1024
+LIMIT = 48 * 1024 * 1024
 
 
 def hidden_kernel(parts, index, *refs):
-    taken, weights, (out, acts) = refs[: 2 * parts], refs[2 * parts : -2], refs[-2:]
-    rows, depth = out.shape[0] // 2, weights[0].shape[0]
+    taken, weights = refs[:parts], refs[parts : parts + 4]
+    out, rows, blocks, acts, part_sems, block_sems = refs[parts + 4 :]
+    share, depth = rows.shape[0] // parts, weights[0].shape[0]
     width = out.shape[1]
-    step = 1024
-    for i in range(2 * depth // step):
-        pair, start = divmod(i * step, depth)
-        block = jnp.concatenate(
-            [ref[pl.ds(start, step), :] for ref in weights[2 * pair : 2 * pair + 2]], axis=1
-        )
+    step = depth // 2
+
+    def part_copy(i):
+        target = rows.at[pl.ds(i * share, share), :]
+        return pltpu.make_async_copy(taken[i], target, part_sems.at[i])
+
+    def block_copy(i, half):
+        source = weights[2 * (i // 2) + half].at[pl.ds(i % 2 * step, step), :]
+        return pltpu.make_async_copy(source, blocks.at[i, half], block_sems.at[i, half])
+
+    for i in range(parts):
+        part_copy(i).start()
+    for i in range(4):
+        for half in range(2):
+            block_copy(i, half).start()
+    for i in range(parts):
+        part_copy(i).wait()
+    for i in range(4):
+        for half in range(2):
+            block_copy(i, half).wait()
         value = jnp.dot(
-            jnp.concatenate([ref[:, pl.ds(i * step, step)] for ref in taken], axis=0),
-            block,
+            rows[:, i * step : (i + 1) * step],
+            jnp.concatenate([blocks[i, 0], blocks[i, 1]], axis=1),
             preferred_element_type=jnp.float32,
         )
         if i == 0:
@@ -115,27 +130,29 @@
 
     gate_act, up_act = acts[:, :width], acts[:, width:]
     value = (jax.nn.silu(gate_act) * up_act).astype(out.dtype)
-    place = index[0]
-    out[pl.ds(pl.multiple_of(place * rows, rows), rows), :] = value[:rows]
-    out[pl.ds(pl.multiple_of((1 - place) * rows, rows), rows), :] = value[rows:]
-
-
-def hidden_call(index, first, second, weights):
-    rows, width = sum(part.shape[0] for part in first), weights[0].shape[1]
-    operands = (*first, *second, *weights)
+    out[pl.ds(pl.multiple_of(index[0] * share, share), share), :] = value[:share]
+    out[pl.ds(pl.multiple_of((1 - index[0]) * share, share), share), :] = value[share:]
+
+
+def hidden_call(index, parts, weights):
+    depth, width = weights[0].shape
+    rows = sum(part.shape[0] for part in parts)
+    held = pl.BlockSpec(memory_space=pltpu.HBM)
     return pl.pallas_call(
-        functools.partial(hidden_kernel, len(first)),
-        out_shape=jax.ShapeDtypeStruct((2 * rows, width), jnp.bfloat16),
-        in_specs=[SMEM] + [VMEM] * len(operands),
+        functools.partial(hidden_kernel, len(parts)),
+        out_shape=jax.ShapeDtypeStruct((rows, width), jnp.bfloat16),
+        in_specs=[SMEM] + [held] * (len(parts) + 4),
         out_specs=VMEM,
-        scratch_shapes=[pltpu.VMEM((2 * rows, 2 * width), jnp.float32)],
+        scratch_shapes=[
+            pltpu.VMEM((rows, 2 * depth), jnp.bfloat16),
+            pltpu.VMEM((4, 2, depth // 2, width), jnp.bfloat16),
+            pltpu.VMEM((rows, 2 * width), jnp.float32),
+            pltpu.SemaphoreType.DMA((len(parts),)),
+            pltpu.SemaphoreType.DMA((4, 2)),
+        ],
         compiler_params=pltpu.CompilerParams(vmem_limit_bytes=LIMIT),
-        cost_estimate=pl.CostEstimate(
-            flops=0,
-            bytes_accessed=0,
-            transcendentals=0,
-        ),
-    )(index, *operands)
+        cost_estimate=pl.CostEstimate(flops=0, bytes_accessed=0, transcendentals=0),
+    )(index, *parts, *weights)
 
 
 def ring(tokens, gate_weight, up_weight, down_weight, expert_ids, codes, expert_home):
@@ -158,7 +175,7 @@
     weights = (gate_own, up_own, swapped(gate_own, "seq", 0), swapped(up_own, "seq", 0))
 
     def activated(part, other):
-        return hidden_call(x_index, (part,), (other,), weights)
+        return hidden_call(x_index, (part, other), weights)
 
     def partial_out(own, other):
         both = in_order(own, other, x, 1)
@@ -186,19 +203,23 @@
     block3, other2, hidden1 = tied((block3, other2, hidden1))
     other3 = to_tensor(block3)
     part1 = partial_out(act1, hidden1).astype(bf16)
+    other2, part1 = tied((other2, part1))
     back1 = z_send(part1, 1)
     act2 = activated(block2, other2)
     hidden2 = to_tensor(act2)
-    other3, part1, hidden2 = tied((other3, part1, hidden2))
+    other3, act2 = tied((other3, act2))
+    act3 = activated(block3, other3)
+    act3, back1 = tied((act3, back1))
+    hidden3 = to_tensor(act3)
+    act3, hidden2 = tied((act3, hidden2))
     part2 = partial_out(act2, hidden2)
-    act3 = activated(block3, other3)
-    back1, part2, act3 = tied((back1, part2, act3))
+    part2, hidden3 = tied((part2, hidden3))
     sent_a2 = z_send(a_half(part2).astype(bf16), 1)
     home_b2 = z_send(added(b_half(part2), a_half(back1)), 2)
-    part3 = partial_out(act3, to_tensor(act3))
-    sent_a3 = z_send(a_half(part3).astype(bf16), 1)
-    sent_a2, home_b2, part3 = tied((sent_a2, home_b2, part3))
+    part3 = partial_out(act3, hidden3)
     home_b3 = z_send(added(b_half(part3), sent_a2), 3)
+    last_a, home_b2 = tied((a_half(part3).astype(bf16), home_b2))
+    sent_a3 = z_send(last_a, 1)
 
     def in_rows(part_a, part_b):
         return in_order(part_a, part_b, odd)
@@ -207,11 +228,11 @@
     home = jnp.where(ids == 0, expert_home[0], expert_home[1])
     ours = (home == z // 2)[:, None]
     scale = codes[:, 0].astype(f32) / 1024.0
-    from_pair = in_rows(
-        a_half(part0) + b_half(back1).astype(f32), b_half(part0) + sent_a3.astype(f32)
-    )
+    from_pair = in_rows(a_half(part0) + b_half(back1).astype(f32), b_half(part0))
     from_others = in_rows(home_b3, home_b2).astype(f32)
-    expert_out = jnp.where(ours, from_pair, from_others).astype(bf16)
+    so_far = tied(jnp.where(ours, from_pair, from_others))
+    last = in_rows(jnp.zeros_like(sent_a3), sent_a3).astype(f32)
+    expert_out = (so_far + jnp.where(ours, last, 0.0)).astype(bf16)
     return (scale[:, None] * expert_out.astype(f32)).astype(bf16)
 
 

time: 115 us -> 109 us (0.948)
  local copies, waits for them, and re-layouts: 12.3 us -> 6.05 us
  starting transfers between devices: 24.6 us -> 28.5 us
  waiting for transfers between devices: 58.2 us -> 54.6 us
  Pallas kernels: 8.99 us -> 10.7 us
    ppermute x14, waiting for transfers between devices: 22 us -> 31.4 us  [swapped(): lax.ppermute(x, axis, [(i, i ^ 1 << distance) for i in range(lax.axis_siz...]
    ppermute x5, waiting for transfers between devices: 21.3 us -> 13.3 us  [z_send(): return lax.ppermute(x, 'expert', [(i, i ^ distance) for i in range(size)])]
    unnamed x44 -> x22, local copies, waits for them, and re-layouts: 9.32 us -> 2.01 us
    ppermute x3, waiting for transfers between devices: 14.9 us -> 9.97 us  [ring_send(): return lax.ppermute(x, ('expert', 'seq'), pairs)]
    ppermute x5, starting transfers between devices: 7.99 us -> 11.5 us  [z_send(): return lax.ppermute(x, 'expert', [(i, i ^ distance) for i in range(size)])]
    pallas_call x4, Pallas kernels: 8.99 us -> 10.7 us  [hidden_call(): pl.pallas_call(functools.partial(hidden_kernel, len(parts)), out_shape=ja...]
    convert_element_type x2 -> x1, other arithmetic: 1.97 us -> 0.76 us  [added(): return (part + received.astype(f32)).astype(bf16)]
  transfers between devices with their start and end apart: 22 -> 22, of which waited for: 12 -> 14; matrix products, arithmetic and copies ran while one was open for 8% -> 8% of each run, Pallas kernels for 8% -> 10%
where the time goes in v3:
time: 109 us
  waiting for transfers between devices  54.6 us (50%)
  starting transfers between devices  28.5 us (26%)
  Pallas kernels  10.7 us (10%)
  local copies, waits for them, and re-layouts  6.05 us (6%)
  other arithmetic  5.55 us (5%)
  matrix products  3.32 us (3%)
    ppermute x14, waiting for transfers between devices, swapped(): lax.ppermute(x, axis, [(i, i ^ 1 << distance) for i in range(lax.axis_siz...  31.4 us
    ppermute x14, starting transfers between devices, swapped(): lax.ppermute(x, axis, [(i, i ^ 1 << distance) for i in range(lax.axis_siz...  13.9 us
    ppermute x5, waiting for transfers between devices, z_send(): return lax.ppermute(x, 'expert', [(i, i ^ distance) for i in range(size)])  13.3 us
    ppermute x5, starting transfers between devices, z_send(): return lax.ppermute(x, 'expert', [(i, i ^ distance) for i in range(size)])  11.5 us
    pallas_call x4, Pallas kernels, hidden_call(): pl.pallas_call(functools.partial(hidden_kernel, len(parts)), out_shape=ja...  10.7 us
    ppermute x3, waiting for transfers between devices, ring_send(): return lax.ppermute(x, ('expert', 'seq'), pairs)  9.97 us
    dot_general x4, matrix products, partial_out(): return jnp.dot(rows, down, preferred_element_type=f32)  3.32 us
    ppermute x3, starting transfers between devices, ring_send(): return lax.ppermute(x, ('expert', 'seq'), pairs)  3.11 us
  transfers between devices with their start and end apart: 22, of which 14 were waited for; matrix products, arithmetic and copies ran while one was open for 8% of the time, Pallas kernels for 10%

profile of v3, /device:TPU:0, one launch (start us, length us, event | category | flops | bytes accessed | tf_op | source)
XLA Modules:
  0.0 109.0 jit_solution(12634059461133597089)
XLA Ops:
  0.0 1.4 %constant_dynamic-slice_fusion.3 = (bf16[128,2048]{1,0:T(8,128)(2,1)S(1)}, bf16[128,2048]{1,0:T(8,128)(2,1)S(1)}) fusion(bf16[256,2048]{1,0:T(8,128)(2,1)} %param.7, s32[]{:T(128)S(6)} %select_n.98, s32[]{:T(128)S(6)} %select_n.99), kind=kLoop, calls=%fused_computation.58 | loop fusion | bytes 2097160 | tf_op jit(solution)/shard_map/dynamic_slice | solution.py:80
  1.4 0.5 collective-permute-start
  1.9 1.5 %collective-permute-done = bf16[128,2048]{1,0:T(8,128)(2,1)S(1)} collective-permute-done((bf16[128,2048]{1,0:T(8,128)(2,1)S(1)}, bf16[128,2048]{1,0:T(8,128)(2,1)S(1)}, u32[]{:S(2)}, u32[]{:S(2)}) %collective-permute-start) | collective-permute-done | bytes 524320 | tf_op jit(solution)/shard_map/ppermute | solution.py:12
  3.5 0.9 constant_dynamic-slice_fusion
  4.4 0.8 copy-done.1
  5.2 0.4 collective-permute-start.2
  5.9 2.8 %collective-permute-start.1 = (bf16[64,4096]{1,0:T(8,128)(2,1)}, bf16[64,4096]{1,0:T(8,128)(2,1)}, u32[]{:S(2)}, u32[]{:S(2)}) collective-permute-start(bf16[64,4096]{1,0:T(8,128)(2,1)} %get-tuple-element.31.refs_0_), channel_id=1, source_target_pairs={{0,4},{1,13},{4,8},{5,1},{8,12},{9,5},{12,0},{13,9},{2,6},{3,15},{... | collective-permute-start | bytes 1572872 | tf_op jit(solution)/shard_map/ppermute | solution.py:75
  8.7 2.2 %collective-permute-done.3.refs_5_ = bf16[2048,384]{1,0:T(8,128)(2,1)S(1)} collective-permute-done((bf16[2048,384]{1,0:T(8,128)(2,1)S(1)}, bf16[2048,384]{1,0:T(8,128)(2,1)S(1)}, u32[]{:S(2)}, u32[]{:S(2)}) %collective-permute-start.3) | collective-permute-done | bytes 1572896 | tf_op jit(solution)/shard_map/ppermute | solution.py:12
  10.9 1.2 %copy-done.6 = bf16[2048,384]{1,0:T(8,128)(2,1)} copy-done((bf16[2048,384]{1,0:T(8,128)(2,1)}, bf16[2048,384]{1,0:T(8,128)(2,1)S(1)}, u32[]{:S(2)}) %copy-start.6) | copy-done | bytes 1572888
  12.1 2.8 %shard_map.73 = bf16[128,384]{1,0:T(8,128)(2,1)S(1)} custom-call(s32[1]{0:T(128)} %bitcast.3.index, bf16[64,4096]{1,0:T(8,128)(2,1)} %get-tuple-element.31.refs_0_, bf16[64,4096]{1,0:T(8,128)(2,1)S(1)} %get-tuple-element.33.refs_1_, bf16[2048,384]{1,0:T(8,128)(2,1)S(1)} %bitcast.18, bf16[2048,384]{1,0:T(8,128)(2,1)S(1)} %bitcast.23, ...), custom_call_target="tpu_custom_call" | custom-call | tf_op jit(solution)/shard_map/pallas_call | solution.py:141
  14.8 2.9 %collective-permute-start.4 = (bf16[128,384]{1,0:T(8,128)(2,1)S(1)}, bf16[128,384]{1,0:T(8,128)(2,1)S(1)}, u32[]{:S(2)}, u32[]{:S(2)}) collective-permute-start(bf16[128,384]{1,0:T(8,128)(2,1)S(1)} %shard_map.73), channel_id=1, source_target_pairs={{0,2},{2,0},{1,3},{3,1},{4,6},{6,4},{5,7},{7,5},{8,10},{10,8},{9,1... | collective-permute-start | bytes 294920 | tf_op jit(solution)/shard_map/ppermute | solution.py:12
  17.8 5.8 %collective-permute-done.1.refs_0_ = bf16[64,4096]{1,0:T(8,128)(2,1)} collective-permute-done((bf16[64,4096]{1,0:T(8,128)(2,1)}, bf16[64,4096]{1,0:T(8,128)(2,1)}, u32[]{:S(2)}, u32[]{:S(2)}) %collective-permute-start.1) | collective-permute-done | bytes 524320 | tf_op jit(solution)/shard_map/ppermute | solution.py:75
  23.6 1.5 %collective-permute-start.6 = (bf16[64,4096]{1,0:T(8,128)(2,1)}, bf16[64,4096]{1,0:T(8,128)(2,1)}, u32[]{:S(2)}, u32[]{:S(2)}) collective-permute-start(bf16[64,4096]{1,0:T(8,128)(2,1)} %collective-permute-done.1.refs_0_), channel_id=1, source_target_pairs={{0,2},{2,0},{1,3},{3,1},{4,6},{6,4},{5,7},{7,5},{8,10},{10,8},{9,1... | collective-permute-start | bytes 1572872 | tf_op jit(solution)/shard_map/ppermute | solution.py:12
  25.1 1.5 %collective-permute-start.7 = (bf16[128,768]{1,0:T(8,128)(2,1)S(1)}, bf16[128,768]{1,0:T(8,128)(2,1)}, u32[]{:S(2)}, u32[]{:S(2)}) collective-permute-start(bf16[128,768]{1,0:T(8,128)(2,1)S(1)} %maximum_select_fusion.10), channel_id=1, source_target_pairs={{0,1},{1,0},{2,3},{3,2},{4,5},{5,4},{6,7},{7,6},{8,9},{9,8},{10,11... | collective-permute-start | bytes 589832 | tf_op jit(solution)/shard_map/ppermute | solution.py:12
  26.6 1.2 %collective-permute-done.7 = bf16[128,768]{1,0:T(8,128)(2,1)} collective-permute-done((bf16[128,768]{1,0:T(8,128)(2,1)S(1)}, bf16[128,768]{1,0:T(8,128)(2,1)}, u32[]{:S(2)}, u32[]{:S(2)}) %collective-permute-start.7) | collective-permute-done | bytes 196640 | tf_op jit(solution)/shard_map/ppermute | solution.py:12
  27.8 1.6 %fusion.6 = f32[256,1024]{1,0:T(8,128)S(1)} fusion(bf16[1,768,1024]{2,1,0:T(8,128)(2,1)S(1)} %copy-done, bf16[128,768]{1,0:T(8,128)(2,1)} %collective-permute-done.7, bf16[128,768]{1,0:T(8,128)(2,1)S(1)} %maximum_select_fusion.10, pred[]{:T(512)S(6)} %eq.38), kind=kOutput, calls=%fused_computation.6 | convolution fusion | flops 404422656 | bytes 3014657 | tf_op jit(solution)/shard_map/dot_general | solution.py:183
  29.5 6.2 %collective-permute-done.6.refs_1_ = bf16[64,4096]{1,0:T(8,128)(2,1)} collective-permute-done((bf16[64,4096]{1,0:T(8,128)(2,1)}, bf16[64,4096]{1,0:T(8,128)(2,1)}, u32[]{:S(2)}, u32[]{:S(2)}) %collective-permute-start.6) | collective-permute-done | bytes 524320 | tf_op jit(solution)/shard_map/ppermute | solution.py:12
  35.6 3.7 %collective-permute-done.5.refs_0_ = bf16[64,4096]{1,0:T(8,128)(2,1)} collective-permute-done((bf16[64,4096]{1,0:T(8,128)(2,1)}, bf16[64,4096]{1,0:T(8,128)(2,1)}, u32[]{:S(2)}, u32[]{:S(2)}) %collective-permute-start.5) | collective-permute-done | bytes 524320 | tf_op jit(solution)/shard_map/ppermute | solution.py:75
  39.3 0.5 collective-permute-start.9
  40.1 2.9 %shard_map.74 = bf16[128,384]{1,0:T(8,128)(2,1)S(1)} custom-call(s32[1]{0:T(128)} %bitcast.3.index, bf16[64,4096]{1,0:T(8,128)(2,1)} %collective-permute-done.1.refs_0_, bf16[64,4096]{1,0:T(8,128)(2,1)} %collective-permute-done.6.refs_1_, bf16[2048,384]{1,0:T(8,128)(2,1)S(1)} %bitcast.19, bf16[2048,384]{1,0:T(8,128)(2,1)S(1)} %bitcast.24, ...), custom_call_target="tpu_custom_call" | custom-call | tf_op jit(solution)/shard_map/pallas_call | solution.py:141
  43.0 1.6 %collective-permute-start.10 = (bf16[128,384]{1,0:T(8,128)(2,1)S(1)}, bf16[128,384]{1,0:T(8,128)(2,1)S(1)}, u32[]{:S(2)}, u32[]{:S(2)}) collective-permute-start(bf16[128,384]{1,0:T(8,128)(2,1)S(1)} %shard_map.74), channel_id=1, source_target_pairs={{0,2},{2,0},{1,3},{3,1},{4,6},{6,4},{5,7},{7,5},{8,10},{10,8},{9,1... | collective-permute-start | bytes 294920 | tf_op jit(solution)/shard_map/ppermute | solution.py:12
  44.6 9.4 %collective-permute-done.10 = bf16[128,384]{1,0:T(8,128)(2,1)S(1)} collective-permute-done((bf16[128,384]{1,0:T(8,128)(2,1)S(1)}, bf16[128,384]{1,0:T(8,128)(2,1)S(1)}, u32[]{:S(2)}, u32[]{:S(2)}) %collective-permute-start.10) | collective-permute-done | bytes 98336 | tf_op jit(solution)/shard_map/ppermute | solution.py:12
  54.0 0.5 collective-permute-done.8.refs_0_
  54.6 1.6 %collective-permute-start.11 = (bf16[64,4096]{1,0:T(8,128)(2,1)S(1)}, bf16[64,4096]{1,0:T(8,128)(2,1)S(1)}, u32[]{:S(2)}, u32[]{:S(2)}) collective-permute-start(bf16[64,4096]{1,0:T(8,128)(2,1)S(1)} %collective-permute-done.8.refs_0_), channel_id=1, source_target_pairs={{0,2},{2,0},{1,3},{3,1},{4,6},{6,4},{5,7},{7,5},{8,10},{10,8},{9,1... | collective-permute-start | bytes 1572872 | tf_op jit(solution)/shard_map/ppermute | solution.py:12
  56.2 0.6 fusion.8
  56.8 0.7 collective-permute-start.13
  57.5 2.8 %shard_map.75 = bf16[128,384]{1,0:T(8,128)(2,1)S(1)} custom-call(s32[1]{0:T(128)} %bitcast.3.index, bf16[64,4096]{1,0:T(8,128)(2,1)} %collective-permute-done.5.refs_0_, bf16[64,4096]{1,0:T(8,128)(2,1)S(1)} %collective-permute-done.9.refs_1_, bf16[2048,384]{1,0:T(8,128)(2,1)S(1)} %bitcast.20, bf16[2048,384]{1,0:T(8,128)(2,1)S(1)} %bitcast.25, ...), custom_call_target="tpu_custom_call" | custom-call | tf_op jit(solution)/shard_map/pallas_call | solution.py:141
  60.3 1.4 %collective-permute-start.14 = (bf16[128,384]{1,0:T(8,128)(2,1)S(1)}, bf16[128,384]{1,0:T(8,128)(2,1)S(1)}, u32[]{:S(2)}, u32[]{:S(2)}) collective-permute-start(bf16[128,384]{1,0:T(8,128)(2,1)S(1)} %shard_map.75), channel_id=1, source_target_pairs={{0,2},{2,0},{1,3},{3,1},{4,6},{6,4},{5,7},{7,5},{8,10},{10,8},{9,1... | collective-permute-start | bytes 294920 | tf_op jit(solution)/shard_map/ppermute | solution.py:12
  61.7 7.7 %collective-permute-done.11.refs_1_ = bf16[64,4096]{1,0:T(8,128)(2,1)S(1)} collective-permute-done((bf16[64,4096]{1,0:T(8,128)(2,1)S(1)}, bf16[64,4096]{1,0:T(8,128)(2,1)S(1)}, u32[]{:S(2)}, u32[]{:S(2)}) %collective-permute-start.11) | collective-permute-done | bytes 524320 | tf_op jit(solution)/shard_map/ppermute | solution.py:12
  69.4 2.3 %shard_map.76 = bf16[128,384]{1,0:T(8,128)(2,1)S(1)} custom-call(s32[1]{0:T(128)} %bitcast.3.index, bf16[64,4096]{1,0:T(8,128)(2,1)S(1)} %collective-permute-done.8.refs_0_, bf16[64,4096]{1,0:T(8,128)(2,1)S(1)} %collective-permute-done.11.refs_1_, bf16[2048,384]{1,0:T(8,128)(2,1)S(1)} %bitcast.21, bf16[2048,384]{1,0:T(8,128)(2,1)S(1)} %bitcast.26, ...), custom_call_target="tpu_custom_call" | custom-call | tf_op jit(solution)/shard_map/pallas_call | solution.py:141
  71.9 1.6 %collective-permute-start.16 = (bf16[128,384]{1,0:T(8,128)(2,1)S(1)}, bf16[128,384]{1,0:T(8,128)(2,1)S(1)}, u32[]{:S(2)}, u32[]{:S(2)}) collective-permute-start(bf16[128,384]{1,0:T(8,128)(2,1)S(1)} %shard_map.76), channel_id=1, source_target_pairs={{0,2},{2,0},{1,3},{3,1},{4,6},{6,4},{5,7},{7,5},{8,10},{10,8},{9,1... | collective-permute-start | bytes 294920 | tf_op jit(solution)/shard_map/ppermute | solution.py:12
  73.5 0.6 fusion.2
  74.0 3.1 %collective-permute-done.16 = bf16[128,384]{1,0:T(8,128)(2,1)S(1)} collective-permute-done((bf16[128,384]{1,0:T(8,128)(2,1)S(1)}, bf16[128,384]{1,0:T(8,128)(2,1)S(1)}, u32[]{:S(2)}, u32[]{:S(2)}) %collective-permute-start.16) | collective-permute-done | bytes 98336 | tf_op jit(solution)/shard_map/ppermute | solution.py:12
  77.3 0.7 collective-permute-start.18
  78.0 0.9 convert_add_fusion
  78.9 3.5 %collective-permute-start.20 = (bf16[128,1024]{1,0:T(8,128)(2,1)}, bf16[128,1024]{1,0:T(8,128)(2,1)S(1)}, u32[]{:S(2)}, u32[]{:S(2)}) collective-permute-start(bf16[128,1024]{1,0:T(8,128)(2,1)} %get-tuple-element.63), channel_id=1, source_target_pairs={{0,8},{4,12},{8,0},{12,4},{1,9},{5,13},{9,1},{13,5},{2,10},{6,14},... | collective-permute-start | bytes 786440 | tf_op jit(solution)/shard_map/ppermute | solution.py:65
  82.4 0.6 fusion
  83.0 7.4 %collective-permute-done.18 = bf16[128,1024]{1,0:T(8,128)(2,1)S(1)} collective-permute-done((bf16[128,1024]{1,0:T(8,128)(2,1)S(1)}, bf16[128,1024]{1,0:T(8,128)(2,1)S(1)}, u32[]{:S(2)}, u32[]{:S(2)}) %collective-permute-start.18) | collective-permute-done | bytes 262176 | tf_op jit(solution)/shard_map/ppermute | solution.py:65
  90.4 0.8 fusion.12
  91.2 1.7 %collective-permute-start.19 = (bf16[128,1024]{1,0:T(8,128)(2,1)}, bf16[128,1024]{1,0:T(8,128)(2,1)S(1)}, u32[]{:S(2)}, u32[]{:S(2)}) collective-permute-start(bf16[128,1024]{1,0:T(8,128)(2,1)} %fusion.12), channel_id=1, source_target_pairs={{0,12},{4,8},{8,4},{12,0},{1,13},{5,9},{9,5},{13,1},{2,14},{6,10},... | collective-permute-start | bytes 786440 | tf_op jit(solution)/shard_map/ppermute | solution.py:65
  92.8 0.7 fusion.41
  93.5 1.1 slice.54
  94.6 0.8 collective-permute-done.20
  95.3 4.9 %collective-permute-start.21 = (bf16[128,1024]{1,0:T(8,128)(2,1)S(1)}, bf16[128,1024]{1,0:T(8,128)(2,1)}, u32[]{:S(2)}, u32[]{:S(2)}) collective-permute-start(bf16[128,1024]{1,0:T(8,128)(2,1)S(1)} %slice.54), channel_id=1, source_target_pairs={{0,4},{4,0},{8,12},{12,8},{1,5},{5,1},{9,13},{13,9},{2,6},{6,2},{1... | collective-permute-start | bytes 786440 | tf_op jit(solution)/shard_map/ppermute | solution.py:65
  100.3 1.3 %compare_reduce_fusion = pred[256]{0:T(512)(128)(4,1)S(1)} fusion(s32[256,1]{0,1:T(1,128)S(1)} %copy-done.9, s32[]{:T(128)S(6)} %select_n.95, s32[]{:T(128)} %bitcast.2, s32[]{:T(128)} %bitcast.1), kind=kLoop, calls=%fused_computation.53 | loop fusion | flops 768 | bytes 1292 | tf_op jit(solution)/shard_map/eq | solution.py:229
  101.6 0.8 collective-permute-done.19
  102.7 4.3 %collective-permute-done.21 = bf16[128,1024]{1,0:T(8,128)(2,1)} collective-permute-done((bf16[128,1024]{1,0:T(8,128)(2,1)S(1)}, bf16[128,1024]{1,0:T(8,128)(2,1)}, u32[]{:S(2)}, u32[]{:S(2)}) %collective-permute-start.21) | collective-permute-done | bytes 262176 | tf_op jit(solution)/shard_map/ppermute | solution.py:65
  106.9 2.1 %multiply_convert_fusion = bf16[256,1024]{1,0:T(8,128)(2,1)} fusion(f32[256,1024]{1,0:T(8,128)S(1)} %fusion.11, bf16[128,1024]{1,0:T(8,128)(2,1)} %collective-permute-done.21, f32[256]{0:T(256)S(1)} %bitcast.27, pred[256]{0:T(512)(128)(4,1)S(1)} %compare_reduce_fusion, pred[]{:T(512)S(6)} %eq.37), kind=kLoop, calls=%fused_computation.12 | loop fusion | flops 2097152 | bytes 1836289 | tf_op jit(solution)/shard_map/convert_element_type | solution.py:236
  (42 shorter events, 1.4 us)
Async XLA Ops:
  0.0 27.8 %copy-start = (bf16[1,768,1024]{2,1,0:T(8,128)(2,1)S(1)}, bf16[1,768,1024]{2,1,0:T(8,128)(2,1)}, u32[]{:S(2)}) copy-start(bf16[1,768,1024]{2,1,0:T(8,128)(2,1)} %param.10) | copy-start | bytes 4718596
  1.4 2.1 %collective-permute-start = (bf16[128,2048]{1,0:T(8,128)(2,1)S(1)}, bf16[128,2048]{1,0:T(8,128)(2,1)S(1)}, u32[]{:S(2)}, u32[]{:S(2)}) collective-permute-start(bf16[128,2048]{1,0:T(8,128)(2,1)S(1)} %get-tuple-element.62), channel_id=1, source_target_pairs={{0,1},{1,0},{2,3},{3,2},{4,5},{5,4},{6,7},{7,6},{8,9},{9,8},{10,11... | collective-permute-start | bytes 1572872 | tf_op jit(solution)/shard_map/ppermute | solution.py:12
  3.4 2.2 %copy-start.2 = (bf16[1,2048,384]{2,1,0:T(8,128)(2,1)S(1)}, bf16[1,2048,384]{2,1,0:T(8,128)(2,1)}, u32[]{:S(2)}) copy-start(bf16[1,2048,384]{2,1,0:T(8,128)(2,1)} %param.9) | copy-start | bytes 4718596
  3.5 1.7 %copy-start.1 = (bf16[1,2048,384]{2,1,0:T(8,128)(2,1)S(1)}, bf16[1,2048,384]{2,1,0:T(8,128)(2,1)}, u32[]{:S(2)}) copy-start(bf16[1,2048,384]{2,1,0:T(8,128)(2,1)} %param.8) | copy-start | bytes 4718596
  5.2 3.5 %collective-permute-start.2 = (bf16[2048,384]{1,0:T(8,128)(2,1)S(1)}, bf16[2048,384]{1,0:T(8,128)(2,1)S(1)}, u32[]{:S(2)}, u32[]{:S(2)}) collective-permute-start(bf16[2048,384]{1,0:T(8,128)(2,1)S(1)} %bitcast.17), channel_id=1, source_target_pairs={{0,1},{1,0},{2,3},{3,2},{4,5},{5,4},{6,7},{7,6},{8,9},{9,8},{10,11... | collective-permute-start | bytes 4718600 | tf_op jit(solution)/shard_map/ppermute | solution.py:12
  5.6 5.3 %collective-permute-start.3 = (bf16[2048,384]{1,0:T(8,128)(2,1)S(1)}, bf16[2048,384]{1,0:T(8,128)(2,1)S(1)}, u32[]{:S(2)}, u32[]{:S(2)}) collective-permute-start(bf16[2048,384]{1,0:T(8,128)(2,1)S(1)} %bitcast.22), channel_id=1, source_target_pairs={{0,1},{1,0},{2,3},{3,2},{4,5},{5,4},{6,7},{7,6},{8,9},{9,8},{10,11... | collective-permute-start | bytes 4718600 | tf_op jit(solution)/shard_map/ppermute | solution.py:12
  5.9 17.7 %collective-permute-start.1 = (bf16[64,4096]{1,0:T(8,128)(2,1)}, bf16[64,4096]{1,0:T(8,128)(2,1)}, u32[]{:S(2)}, u32[]{:S(2)}) collective-permute-start(bf16[64,4096]{1,0:T(8,128)(2,1)} %get-tuple-element.31.refs_0_), channel_id=1, source_target_pairs={{0,4},{1,13},{4,8},{5,1},{8,12},{9,5},{12,0},{13,9},{2,6},{3,15},{... | collective-permute-start | bytes 1572872 | tf_op jit(solution)/shard_map/ppermute | solution.py:75
  8.7 6.1 %copy-start.4 = (bf16[2048,384]{1,0:T(8,128)(2,1)}, bf16[2048,384]{1,0:T(8,128)(2,1)S(1)}, u32[]{:S(2)}) copy-start(bf16[2048,384]{1,0:T(8,128)(2,1)S(1)} %collective-permute-done.2.refs_4_) | copy-start | bytes 4718596
  10.9 1.2 %copy-start.6 = (bf16[2048,384]{1,0:T(8,128)(2,1)}, bf16[2048,384]{1,0:T(8,128)(2,1)S(1)}, u32[]{:S(2)}) copy-start(bf16[2048,384]{1,0:T(8,128)(2,1)S(1)} %collective-permute-done.3.refs_5_) | copy-start | bytes 4718596
  14.8 8.7 %collective-permute-start.4 = (bf16[128,384]{1,0:T(8,128)(2,1)S(1)}, bf16[128,384]{1,0:T(8,128)(2,1)S(1)}, u32[]{:S(2)}, u32[]{:S(2)}) collective-permute-start(bf16[128,384]{1,0:T(8,128)(2,1)S(1)} %shard_map.73), channel_id=1, source_target_pairs={{0,2},{2,0},{1,3},{3,1},{4,6},{6,4},{5,7},{7,5},{8,10},{10,8},{9,1... | collective-permute-start | bytes 294920 | tf_op jit(solution)/shard_map/ppermute | solution.py:12
  23.6 12.1 %collective-permute-start.6 = (bf16[64,4096]{1,0:T(8,128)(2,1)}, bf16[64,4096]{1,0:T(8,128)(2,1)}, u32[]{:S(2)}, u32[]{:S(2)}) collective-permute-start(bf16[64,4096]{1,0:T(8,128)(2,1)} %collective-permute-done.1.refs_0_), channel_id=1, source_target_pairs={{0,2},{2,0},{1,3},{3,1},{4,6},{6,4},{5,7},{7,5},{8,10},{10,8},{9,1... | collective-permute-start | bytes 1572872 | tf_op jit(solution)/shard_map/ppermute | solution.py:12
  25.1 14.2 %collective-permute-start.5 = (bf16[64,4096]{1,0:T(8,128)(2,1)}, bf16[64,4096]{1,0:T(8,128)(2,1)}, u32[]{:S(2)}, u32[]{:S(2)}) collective-permute-start(bf16[64,4096]{1,0:T(8,128)(2,1)} %collective-permute-done.1.refs_0_), channel_id=1, source_target_pairs={{0,4},{1,13},{4,8},{5,1},{8,12},{9,5},{12,0},{13,9},{2,6},{3,15},{... | collective-permute-start | bytes 1572872 | tf_op jit(solution)/shard_map/ppermute | solution.py:75
  25.1 2.7 %collective-permute-start.7 = (bf16[128,768]{1,0:T(8,128)(2,1)S(1)}, bf16[128,768]{1,0:T(8,128)(2,1)}, u32[]{:S(2)}, u32[]{:S(2)}) collective-permute-start(bf16[128,768]{1,0:T(8,128)(2,1)S(1)} %maximum_select_fusion.10), channel_id=1, source_target_pairs={{0,1},{1,0},{2,3},{3,2},{4,5},{5,4},{6,7},{7,6},{8,9},{9,8},{10,11... | collective-permute-start | bytes 589832 | tf_op jit(solution)/shard_map/ppermute | solution.py:12
  26.6 13.4 %copy-start.3 = (bf16[1,2048,384]{2,1,0:T(8,128)(2,1)S(1)}, bf16[1,2048,384]{2,1,0:T(8,128)(2,1)}, u32[]{:S(2)}) copy-start(bf16[1,2048,384]{2,1,0:T(8,128)(2,1)} %param.9) | copy-start | bytes 4718596
  26.6 13.4 %copy-start.5 = (bf16[2048,384]{1,0:T(8,128)(2,1)S(1)}, bf16[2048,384]{1,0:T(8,128)(2,1)}, u32[]{:S(2)}) copy-start(bf16[2048,384]{1,0:T(8,128)(2,1)} %copy-done.4) | copy-start | bytes 4718596
  39.3 14.7 %collective-permute-start.9 = (bf16[64,4096]{1,0:T(8,128)(2,1)}, bf16[64,4096]{1,0:T(8,128)(2,1)S(1)}, u32[]{:S(2)}, u32[]{:S(2)}) collective-permute-start(bf16[64,4096]{1,0:T(8,128)(2,1)} %collective-permute-done.5.refs_0_), channel_id=1, source_target_pairs={{0,2},{2,0},{1,3},{3,1},{4,6},{6,4},{5,7},{7,5},{8,10},{10,8},{9,1... | collective-permute-start | bytes 1572872 | tf_op jit(solution)/shard_map/ppermute | solution.py:12
  39.8 14.7 %collective-permute-start.8 = (bf16[64,4096]{1,0:T(8,128)(2,1)}, bf16[64,4096]{1,0:T(8,128)(2,1)S(1)}, u32[]{:S(2)}, u32[]{:S(2)}) collective-permute-start(bf16[64,4096]{1,0:T(8,128)(2,1)} %collective-permute-done.5.refs_0_), channel_id=1, source_target_pairs={{0,4},{1,13},{4,8},{5,1},{8,12},{9,5},{12,0},{13,9},{2,6},{3,15},{... | collective-permute-start | bytes 1572872 | tf_op jit(solution)/shard_map/ppermute | solution.py:75
  43.0 11.0 %collective-permute-start.10 = (bf16[128,384]{1,0:T(8,128)(2,1)S(1)}, bf16[128,384]{1,0:T(8,128)(2,1)S(1)}, u32[]{:S(2)}, u32[]{:S(2)}) collective-permute-start(bf16[128,384]{1,0:T(8,128)(2,1)S(1)} %shard_map.74), channel_id=1, source_target_pairs={{0,2},{2,0},{1,3},{3,1},{4,6},{6,4},{5,7},{7,5},{8,10},{10,8},{9,1... | collective-permute-start | bytes 294920 | tf_op jit(solution)/shard_map/ppermute | solution.py:12
  54.6 1.6 %collective-permute-start.12 = (bf16[128,768]{1,0:T(8,128)(2,1)S(1)}, bf16[128,768]{1,0:T(8,128)(2,1)S(1)}, u32[]{:S(2)}, u32[]{:S(2)}) collective-permute-start(bf16[128,768]{1,0:T(8,128)(2,1)S(1)} %maximum_select_fusion.11), channel_id=1, source_target_pairs={{0,1},{1,0},{2,3},{3,2},{4,5},{5,4},{6,7},{7,6},{8,9},{9,8},{10,11... | collective-permute-start | bytes 589832 | tf_op jit(solution)/shard_map/ppermute | solution.py:12
  54.6 14.8 %collective-permute-start.11 = (bf16[64,4096]{1,0:T(8,128)(2,1)S(1)}, bf16[64,4096]{1,0:T(8,128)(2,1)S(1)}, u32[]{:S(2)}, u32[]{:S(2)}) collective-permute-start(bf16[64,4096]{1,0:T(8,128)(2,1)S(1)} %collective-permute-done.8.refs_0_), channel_id=1, source_target_pairs={{0,2},{2,0},{1,3},{3,1},{4,6},{6,4},{5,7},{7,5},{8,10},{10,8},{9,1... | collective-permute-start | bytes 1572872 | tf_op jit(solution)/shard_map/ppermute | solution.py:12
  56.8 15.0 %collective-permute-start.13 = (bf16[256,1024]{1,0:T(8,128)(2,1)S(1)}, bf16[256,1024]{1,0:T(8,128)(2,1)S(1)}, u32[]{:S(2)}, u32[]{:S(2)}) collective-permute-start(bf16[256,1024]{1,0:T(8,128)(2,1)S(1)} %fusion.8), channel_id=1, source_target_pairs={{0,4},{4,0},{8,12},{12,8},{1,5},{5,1},{9,13},{13,9},{2,6},{6,2},{1... | collective-permute-start | bytes 1572872 | tf_op jit(solution)/shard_map/ppermute | solution.py:65
  60.3 11.5 %collective-permute-start.14 = (bf16[128,384]{1,0:T(8,128)(2,1)S(1)}, bf16[128,384]{1,0:T(8,128)(2,1)S(1)}, u32[]{:S(2)}, u32[]{:S(2)}) collective-permute-start(bf16[128,384]{1,0:T(8,128)(2,1)S(1)} %shard_map.75), channel_id=1, source_target_pairs={{0,2},{2,0},{1,3},{3,1},{4,6},{6,4},{5,7},{7,5},{8,10},{10,8},{9,1... | collective-permute-start | bytes 294920 | tf_op jit(solution)/shard_map/ppermute | solution.py:12
  71.8 1.6 %collective-permute-start.15 = (bf16[128,768]{1,0:T(8,128)(2,1)S(1)}, bf16[128,768]{1,0:T(8,128)(2,1)S(1)}, u32[]{:S(2)}, u32[]{:S(2)}) collective-permute-start(bf16[128,768]{1,0:T(8,128)(2,1)S(1)} %maximum_select_fusion.12), channel_id=1, source_target_pairs={{0,1},{1,0},{2,3},{3,2},{4,5},{5,4},{6,7},{7,6},{8,9},{9,8},{10,11... | collective-permute-start | bytes 589832 | tf_op jit(solution)/shard_map/ppermute | solution.py:12
  71.9 5.2 %collective-permute-start.16 = (bf16[128,384]{1,0:T(8,128)(2,1)S(1)}, bf16[128,384]{1,0:T(8,128)(2,1)S(1)}, u32[]{:S(2)}, u32[]{:S(2)}) collective-permute-start(bf16[128,384]{1,0:T(8,128)(2,1)S(1)} %shard_map.76), channel_id=1, source_target_pairs={{0,2},{2,0},{1,3},{3,1},{4,6},{6,4},{5,7},{7,5},{8,10},{10,8},{9,1... | collective-permute-start | bytes 294920 | tf_op jit(solution)/shard_map/ppermute | solution.py:12
  77.2 5.2 %collective-permute-start.17 = (bf16[128,768]{1,0:T(8,128)(2,1)S(1)}, bf16[128,768]{1,0:T(8,128)(2,1)S(1)}, u32[]{:S(2)}, u32[]{:S(2)}) collective-permute-start(bf16[128,768]{1,0:T(8,128)(2,1)S(1)} %maximum_select_fusion.13), channel_id=1, source_target_pairs={{0,1},{1,0},{2,3},{3,2},{4,5},{5,4},{6,7},{7,6},{8,9},{9,8},{10,11... | collective-permute-start | bytes 589832 | tf_op jit(solution)/shard_map/ppermute | solution.py:12
  77.3 13.1 %collective-permute-start.18 = (bf16[128,1024]{1,0:T(8,128)(2,1)S(1)}, bf16[128,1024]{1,0:T(8,128)(2,1)S(1)}, u32[]{:S(2)}, u32[]{:S(2)}) collective-permute-start(bf16[128,1024]{1,0:T(8,128)(2,1)S(1)} %slice.55), channel_id=1, source_target_pairs={{0,4},{4,0},{8,12},{12,8},{1,5},{5,1},{9,13},{13,9},{2,6},{6,2},{1... | collective-permute-start | bytes 786440 | tf_op jit(solution)/shard_map/ppermute | solution.py:65
  78.9 13.9 %copy-start.10 = (s32[256,1]{0,1:T(1,128)S(1)}, s32[256,1]{0,1:T(1,128)}, u32[]{:S(2)}) copy-start(s32[256,1]{0,1:T(1,128)} %param.12) | copy-start | bytes 3076
  78.9 13.9 %copy-start.8 = (s32[2]{0:T(128)S(1)}, s32[2]{0:T(128)}, u32[]{:S(2)}) copy-start(s32[2]{0:T(128)} %param.13) | copy-start | bytes 28
  78.9 16.4 %collective-permute-start.20 = (bf16[128,1024]{1,0:T(8,128)(2,1)}, bf16[128,1024]{1,0:T(8,128)(2,1)S(1)}, u32[]{:S(2)}, u32[]{:S(2)}) collective-permute-start(bf16[128,1024]{1,0:T(8,128)(2,1)} %get-tuple-element.63), channel_id=1, source_target_pairs={{0,8},{4,12},{8,0},{12,4},{1,9},{5,13},{9,1},{13,5},{2,10},{6,14},... | collective-permute-start | bytes 786440 | tf_op jit(solution)/shard_map/ppermute | solution.py:65
  83.0 7.4 %copy-start.7 = (f32[256,1024]{1,0:T(8,128)}, f32[256,1024]{1,0:T(8,128)S(1)}, u32[]{:S(2)}) copy-start(f32[256,1024]{1,0:T(8,128)S(1)} %fusion) | copy-start | bytes 3145732
  83.0 17.3 %copy-start.9 = (s32[256,1]{0,1:T(1,128)S(1)}, s32[256,1]{0,1:T(1,128)}, u32[]{:S(2)}) copy-start(s32[256,1]{0,1:T(1,128)} %param.11) | copy-start | bytes 3076
  91.2 11.3 %collective-permute-start.19 = (bf16[128,1024]{1,0:T(8,128)(2,1)}, bf16[128,1024]{1,0:T(8,128)(2,1)S(1)}, u32[]{:S(2)}, u32[]{:S(2)}) collective-permute-start(bf16[128,1024]{1,0:T(8,128)(2,1)} %fusion.12), channel_id=1, source_target_pairs={{0,12},{4,8},{8,4},{12,0},{1,13},{5,9},{9,5},{13,1},{2,14},{6,10},... | collective-permute-start | bytes 786440 | tf_op jit(solution)/shard_map/ppermute | solution.py:65
  95.3 11.6 %collective-permute-start.21 = (bf16[128,1024]{1,0:T(8,128)(2,1)S(1)}, bf16[128,1024]{1,0:T(8,128)(2,1)}, u32[]{:S(2)}, u32[]{:S(2)}) collective-permute-start(bf16[128,1024]{1,0:T(8,128)(2,1)S(1)} %slice.54), channel_id=1, source_target_pairs={{0,4},{4,0},{8,12},{12,8},{1,5},{5,1},{9,13},{13,9},{2,6},{6,2},{1... | collective-permute-start | bytes 786440 | tf_op jit(solution)/shard_map/ppermute | solution.py:65

commit v4 on v3

--- a/solution.py
+++ b/solution.py
@@ -104,20 +104,20 @@
         target = rows.at[pl.ds(i * share, share), :]
         return pltpu.make_async_copy(taken[i], target, part_sems.at[i])
 
-    def block_copy(i, half):
-        source = weights[2 * (i // 2) + half].at[pl.ds(i % 2 * step, step), :]
-        return pltpu.make_async_copy(source, blocks.at[i, half], block_sems.at[i, half])
+    def block_copy(i, side):
+        source = weights[2 * (i // 2) + side].at[pl.ds(i % 2 * step, step), :]
+        return pltpu.make_async_copy(source, blocks.at[i, side], block_sems.at[i, side])
 
     for i in range(parts):
         part_copy(i).start()
     for i in range(4):
-        for half in range(2):
-            block_copy(i, half).start()
+        for side in range(2):
+            block_copy(i, side).start()
     for i in range(parts):
         part_copy(i).wait()
     for i in range(4):
-        for half in range(2):
-            block_copy(i, half).wait()
+        for side in range(2):
+            block_copy(i, side).wait()
         value = jnp.dot(
             rows[:, i * step : (i + 1) * step],
             jnp.concatenate([blocks[i, 0], blocks[i, 1]], axis=1),
@@ -130,8 +130,9 @@
 
     gate_act, up_act = acts[:, :width], acts[:, width:]
     value = (jax.nn.silu(gate_act) * up_act).astype(out.dtype)
-    out[pl.ds(pl.multiple_of(index[0] * share, share), share), :] = value[:share]
-    out[pl.ds(pl.multiple_of((1 - index[0]) * share, share), share), :] = value[share:]
+    half = out.shape[0] // 2
+    out[pl.ds(pl.multiple_of(index[0] * half, half), half), :] = value[:half]
+    out[pl.ds(pl.multiple_of((1 - index[0]) * half, half), half), :] = value[half:]
 
 
 def hidden_call(index, parts, weights):
@@ -170,12 +171,13 @@
     own_half, given_half = half(tokens, c), half(tokens, 1 - c)
     own_rows = tied(jnp.concatenate([own_half, swapped(given_half, "seq", 0)], axis=1))
     moving, staying = tied((half(own_rows, x), half(own_rows, 1 - x)))
-    block1 = ring_send(moving)
+    first, second = tied(tuple(jnp.split(moving, 2)))
+    block1a, block1b = ring_send(first), ring_send(second)
     gate_own, up_own, staying = tied((gate_weight[0], up_weight[0], staying))
     weights = (gate_own, up_own, swapped(gate_own, "seq", 0), swapped(up_own, "seq", 0))
 
-    def activated(part, other):
-        return hidden_call(x_index, (part, other), weights)
+    def activated(*parts):
+        return hidden_call(x_index, parts, weights)
 
     def partial_out(own, other):
         both = in_order(own, other, x, 1)
@@ -191,29 +193,33 @@
     def added(part, received):
         return (part + received.astype(f32)).astype(bf16)
 
+    block2a, other1a = ring_send(block1a), to_tensor(block1a)
     act0 = activated(moving, staying)
+    block1b, act0 = tied((block1b, act0))
     hidden0 = to_tensor(act0)
-    block1, act0, hidden0 = tied((block1, act0, hidden0))
-    block2, other1 = ring_send(block1), to_tensor(block1)
+    block2b, other1b = ring_send(block1b), to_tensor(block1b)
+    block2a, other1a = tied((block2a, other1a))
+    block3a, other2a = ring_send(block2a), to_tensor(block2a)
+    block2b, other1a, other1b = tied((block2b, other1a, other1b))
+    block3b, other2b = ring_send(block2b), to_tensor(block2b)
+    act1 = activated(block1a, block1b, other1a, other1b)
+    act1, block3a, other2a = tied((act1, block3a, other2a))
+    hidden1 = to_tensor(act1)
+    other3a = to_tensor(block3a)
+    block3b, hidden1, other2b = tied((block3b, hidden1, other2b))
+    other3b = to_tensor(block3b)
+    part1 = partial_out(act1, hidden1).astype(bf16)
+    other2a, other2b, part1 = tied((other2a, other2b, part1))
+    back1 = z_send(part1, 1)
     part0 = partial_out(act0, hidden0)
-    block2, other1, part0 = tied((block2, other1, part0))
-    block3, other2 = ring_send(block2), to_tensor(block2)
-    act1 = activated(block1, other1)
-    hidden1 = to_tensor(act1)
-    block3, other2, hidden1 = tied((block3, other2, hidden1))
-    other3 = to_tensor(block3)
-    part1 = partial_out(act1, hidden1).astype(bf16)
-    other2, part1 = tied((other2, part1))
-    back1 = z_send(part1, 1)
-    act2 = activated(block2, other2)
+    act2 = activated(block2a, block2b, other2a, other2b)
     hidden2 = to_tensor(act2)
-    other3, act2 = tied((other3, act2))
-    act3 = activated(block3, other3)
-    act3, back1 = tied((act3, back1))
+    other3a, other3b, act2, part0 = tied((other3a, other3b, act2, part0))
+    act3 = activated(block3a, block3b, other3a, other3b)
     hidden3 = to_tensor(act3)
     act3, hidden2 = tied((act3, hidden2))
     part2 = partial_out(act2, hidden2)
-    part2, hidden3 = tied((part2, hidden3))
+    part2, hidden3, back1 = tied((part2, hidden3, back1))
     sent_a2 = z_send(a_half(part2).astype(bf16), 1)
     home_b2 = z_send(added(b_half(part2), a_half(back1)), 2)
     part3 = partial_out(act3, hidden3)

time: 109 us -> 106 us (0.972)
  waiting for transfers between devices: 54.6 us -> 49.3 us
  local copies, waits for them, and re-layouts: 6.05 us -> 7.9 us
  other arithmetic: 5.55 us -> 7.39 us
    ppermute x14 -> x17, waiting for transfers between devices: 31.4 us -> 14.5 us  [swapped(): lax.ppermute(x, axis, [(i, i ^ 1 << distance) for i in range(lax.axis_siz...]
    ppermute x3 -> x6, waiting for transfers between devices: 9.97 us -> 17.6 us  [ring_send(): return lax.ppermute(x, ('expert', 'seq'), pairs)]
    ppermute x5, starting transfers between devices: 11.5 us -> 7.39 us  [z_send(): return lax.ppermute(x, 'expert', [(i, i ^ distance) for i in range(size)])]
    ppermute x5, waiting for transfers between devices: 13.3 us -> 17.2 us  [z_send(): return lax.ppermute(x, 'expert', [(i, i ^ distance) for i in range(size)])]
    unnamed x22 -> x36, local copies, waits for them, and re-layouts: 2.01 us -> 4.69 us
    select_n x4, other arithmetic: 0.21 us -> 2.13 us  [in_order(): jnp.where(index == 0, jnp.concatenate([own, other], axis), jnp.concatenat...]
    ppermute x14 -> x17, starting transfers between devices: 13.9 us -> 15.7 us  [swapped(): lax.ppermute(x, axis, [(i, i ^ 1 << distance) for i in range(lax.axis_siz...]
    ppermute x3 -> x6, starting transfers between devices: 3.11 us -> 4.43 us  [ring_send(): return lax.ppermute(x, ('expert', 'seq'), pairs)]
  transfers between devices with their start and end apart: 22 -> 28, of which waited for: 14 -> 14; matrix products, arithmetic and copies ran while one was open for 8% -> 10% of each run, Pallas kernels for 10% -> 10%
where the time goes in v4:
time: 106 us
  waiting for transfers between devices  49.3 us (47%)
  starting transfers between devices  27.5 us (26%)
  Pallas kernels  10.1 us (10%)
  local copies, waits for them, and re-layouts  7.9 us (7%)
  other arithmetic  7.39 us (7%)
  matrix products  3.32 us (3%)
    ppermute x6, waiting for transfers between devices, ring_send(): return lax.ppermute(x, ('expert', 'seq'), pairs)  17.6 us
    ppermute x5, waiting for transfers between devices, z_send(): return lax.ppermute(x, 'expert', [(i, i ^ distance) for i in range(size)])  17.2 us
    ppermute x17, starting transfers between devices, swapped(): lax.ppermute(x, axis, [(i, i ^ 1 << distance) for i in range(lax.axis_siz...  15.7 us
    ppermute x17, waiting for transfers between devices, swapped(): lax.ppermute(x, axis, [(i, i ^ 1 << distance) for i in range(lax.axis_siz...  14.5 us
    pallas_call x4, Pallas kernels, hidden_call(): pl.pallas_call(functools.partial(hidden_kernel, len(parts)), out_shape=ja...  10.1 us
    ppermute x5, starting transfers between devices, z_send(): return lax.ppermute(x, 'expert', [(i, i ^ distance) for i in range(size)])  7.39 us
    unnamed x36, local copies, waits for them, and re-layouts  4.69 us
    ppermute x6, starting transfers between devices, ring_send(): return lax.ppermute(x, ('expert', 'seq'), pairs)  4.43 us
  transfers between devices with their start and end apart: 28, of which 14 were waited for; matrix products, arithmetic and copies ran while one was open for 10% of the time, Pallas kernels for 10%

profile of v4, /device:TPU:0, one launch (start us, length us, event | category | flops | bytes accessed | tf_op | source)
XLA Modules:
  0.0 105.9 jit_solution(6492400867120933885)
XLA Ops:
  0.0 1.4 %constant_dynamic-slice_fusion.3 = (bf16[128,2048]{1,0:T(8,128)(2,1)S(1)}, bf16[128,2048]{1,0:T(8,128)(2,1)S(1)}) fusion(bf16[256,2048]{1,0:T(8,128)(2,1)} %param.7, s32[]{:T(128)S(6)} %select_n.98, s32[]{:T(128)S(6)} %select_n.99), kind=kLoop, calls=%fused_computation.58 | loop fusion | bytes 2097160 | tf_op jit(solution)/shard_map/dynamic_slice | solution.py:80
  1.4 0.5 collective-permute-start
  1.9 1.5 %collective-permute-done = bf16[128,2048]{1,0:T(8,128)(2,1)S(1)} collective-permute-done((bf16[128,2048]{1,0:T(8,128)(2,1)S(1)}, bf16[128,2048]{1,0:T(8,128)(2,1)S(1)}, u32[]{:S(2)}, u32[]{:S(2)}) %collective-permute-start) | collective-permute-done | bytes 524320 | tf_op jit(solution)/shard_map/ppermute | solution.py:12
  3.6 1.4 %copy-done.1 = bf16[1,2048,384]{2,1,0:T(8,128)(2,1)S(1)} copy-done((bf16[1,2048,384]{2,1,0:T(8,128)(2,1)S(1)}, bf16[1,2048,384]{2,1,0:T(8,128)(2,1)}, u32[]{:S(2)}) %copy-start.1) | copy-done | bytes 1572888
  5.7 2.8 %collective-permute-start.1 = (bf16[32,4096]{1,0:T(8,128)(2,1)S(1)}, bf16[32,4096]{1,0:T(8,128)(2,1)S(1)}, u32[]{:S(2)}, u32[]{:S(2)}) collective-permute-start(bf16[32,4096]{1,0:T(8,128)(2,1)S(1)} %get-tuple-element.40), channel_id=1, source_target_pairs={{0,4},{1,13},{4,8},{5,1},{8,12},{9,5},{12,0},{13,9},{2,6},{3,15},{... | collective-permute-start | bytes 786440 | tf_op jit(solution)/shard_map/ppermute | solution.py:75
  8.6 1.6 %collective-permute-start.2 = (bf16[32,4096]{1,0:T(8,128)(2,1)S(1)}, bf16[32,4096]{1,0:T(8,128)(2,1)S(1)}, u32[]{:S(2)}, u32[]{:S(2)}) collective-permute-start(bf16[32,4096]{1,0:T(8,128)(2,1)S(1)} %get-tuple-element.41), channel_id=1, source_target_pairs={{0,4},{1,13},{4,8},{5,1},{8,12},{9,5},{12,0},{13,9},{2,6},{3,15},{... | collective-permute-start | bytes 786440 | tf_op jit(solution)/shard_map/ppermute | solution.py:75
  10.2 7.6 %collective-permute-done.1.refs_0_ = bf16[32,4096]{1,0:T(8,128)(2,1)S(1)} collective-permute-done((bf16[32,4096]{1,0:T(8,128)(2,1)S(1)}, bf16[32,4096]{1,0:T(8,128)(2,1)S(1)}, u32[]{:S(2)}, u32[]{:S(2)}) %collective-permute-start.1) | collective-permute-done | bytes 262176 | tf_op jit(solution)/shard_map/ppermute | solution.py:75
  17.8 1.6 %collective-permute-start.7 = (bf16[32,4096]{1,0:T(8,128)(2,1)S(1)}, bf16[32,4096]{1,0:T(8,128)(2,1)S(1)}, u32[]{:S(2)}, u32[]{:S(2)}) collective-permute-start(bf16[32,4096]{1,0:T(8,128)(2,1)S(1)} %collective-permute-done.1.refs_0_), channel_id=1, source_target_pairs={{0,2},{2,0},{1,3},{3,1},{4,6},{6,4},{5,7},{7,5},{8,10},{10,8},{9,1... | collective-permute-start | bytes 786440 | tf_op jit(solution)/shard_map/ppermute | solution.py:12
  19.4 1.2 %copy-done.12 = bf16[2048,384]{1,0:T(8,128)(2,1)} copy-done((bf16[2048,384]{1,0:T(8,128)(2,1)}, bf16[2048,384]{1,0:T(8,128)(2,1)S(1)}, u32[]{:S(2)}) %copy-start.12) | copy-done | bytes 1572888
  20.6 2.3 %shard_map.73 = bf16[128,384]{1,0:T(8,128)(2,1)S(1)} custom-call(s32[1]{0:T(128)} %bitcast.3.index, bf16[64,4096]{1,0:T(8,128)(2,1)S(1)} %get-tuple-element.39.refs_0_, bf16[64,4096]{1,0:T(8,128)(2,1)S(1)} %get-tuple-element.43.refs_1_, bf16[2048,384]{1,0:T(8,128)(2,1)S(1)} %bitcast.18, bf16[2048,384]{1,0:T(8,128)(2,1)S(1)} %bitcast.23, ...), custom_call_target="tpu_custom_call" | custom-call | tf_op jit(solution)/shard_map/pallas_call | solution.py:142
  22.9 0.5 collective-permute-done.2.refs_1_
  23.4 1.6 %collective-permute-start.8 = (bf16[32,4096]{1,0:T(8,128)(2,1)S(1)}, bf16[32,4096]{1,0:T(8,128)(2,1)S(1)}, u32[]{:S(2)}, u32[]{:S(2)}) collective-permute-start(bf16[32,4096]{1,0:T(8,128)(2,1)S(1)} %collective-permute-done.2.refs_1_), channel_id=1, source_target_pairs={{0,2},{2,0},{1,3},{3,1},{4,6},{6,4},{5,7},{7,5},{8,10},{10,8},{9,1... | collective-permute-start | bytes 786440 | tf_op jit(solution)/shard_map/ppermute | solution.py:12
  25.0 4.0 %collective-permute-done.6.refs_0_ = bf16[32,4096]{1,0:T(8,128)(2,1)S(1)} collective-permute-done((bf16[32,4096]{1,0:T(8,128)(2,1)S(1)}, bf16[32,4096]{1,0:T(8,128)(2,1)S(1)}, u32[]{:S(2)}, u32[]{:S(2)}) %collective-permute-start.6) | collective-permute-done | bytes 262176 | tf_op jit(solution)/shard_map/ppermute | solution.py:75
  29.0 1.7 %collective-permute-start.10 = (bf16[32,4096]{1,0:T(8,128)(2,1)S(1)}, bf16[32,4096]{1,0:T(8,128)(2,1)S(1)}, u32[]{:S(2)}, u32[]{:S(2)}) collective-permute-start(bf16[32,4096]{1,0:T(8,128)(2,1)S(1)} %collective-permute-done.6.refs_0_), channel_id=1, source_target_pairs={{0,2},{2,0},{1,3},{3,1},{4,6},{6,4},{5,7},{7,5},{8,10},{10,8},{9,1... | collective-permute-start | bytes 786440 | tf_op jit(solution)/shard_map/ppermute | solution.py:12
  30.7 4.0 %collective-permute-done.5.refs_1_ = bf16[32,4096]{1,0:T(8,128)(2,1)} collective-permute-done((bf16[32,4096]{1,0:T(8,128)(2,1)S(1)}, bf16[32,4096]{1,0:T(8,128)(2,1)}, u32[]{:S(2)}, u32[]{:S(2)}) %collective-permute-start.5) | collective-permute-done | bytes 262176 | tf_op jit(solution)/shard_map/ppermute | solution.py:75
  34.7 1.6 %collective-permute-start.14 = (bf16[32,4096]{1,0:T(8,128)(2,1)}, bf16[32,4096]{1,0:T(8,128)(2,1)}, u32[]{:S(2)}, u32[]{:S(2)}) collective-permute-start(bf16[32,4096]{1,0:T(8,128)(2,1)} %collective-permute-done.5.refs_1_), channel_id=1, source_target_pairs={{0,2},{2,0},{1,3},{3,1},{4,6},{6,4},{5,7},{7,5},{8,10},{10,8},{9,1... | collective-permute-start | bytes 786440 | tf_op jit(solution)/shard_map/ppermute | solution.py:12
  36.4 2.3 %shard_map.74 = bf16[128,384]{1,0:T(8,128)(2,1)S(1)} custom-call(s32[1]{0:T(128)} %bitcast.3.index, bf16[32,4096]{1,0:T(8,128)(2,1)S(1)} %collective-permute-done.1.refs_0_, bf16[32,4096]{1,0:T(8,128)(2,1)S(1)} %collective-permute-done.2.refs_1_, bf16[32,4096]{1,0:T(8,128)(2,1)S(1)} %collective-permute-done.7.refs_2_, ...), custom_call_target="tpu_custom_call" | custom-call | tf_op jit(solution)/shard_map/pallas_call | solution.py:142
  38.7 1.5 %collective-permute-done.9.refs_0_ = bf16[32,4096]{1,0:T(8,128)(2,1)S(1)} collective-permute-done((bf16[32,4096]{1,0:T(8,128)(2,1)S(1)}, bf16[32,4096]{1,0:T(8,128)(2,1)S(1)}, u32[]{:S(2)}, u32[]{:S(2)}) %collective-permute-start.9) | collective-permute-done | bytes 262176 | tf_op jit(solution)/shard_map/ppermute | solution.py:75
  40.3 0.7 copy-done.8
  41.0 0.7 copy-done.10
  41.7 1.6 %collective-permute-start.13 = (bf16[128,384]{1,0:T(8,128)(2,1)S(1)}, bf16[128,384]{1,0:T(8,128)(2,1)S(1)}, u32[]{:S(2)}, u32[]{:S(2)}) collective-permute-start(bf16[128,384]{1,0:T(8,128)(2,1)S(1)} %shard_map.74), channel_id=1, source_target_pairs={{0,2},{2,0},{1,3},{3,1},{4,6},{6,4},{5,7},{7,5},{8,10},{10,8},{9,1... | collective-permute-start | bytes 294920 | tf_op jit(solution)/shard_map/ppermute | solution.py:12
  43.7 3.6 %collective-permute-done.13 = bf16[128,384]{1,0:T(8,128)(2,1)S(1)} collective-permute-done((bf16[128,384]{1,0:T(8,128)(2,1)S(1)}, bf16[128,384]{1,0:T(8,128)(2,1)S(1)}, u32[]{:S(2)}, u32[]{:S(2)}) %collective-permute-start.13) | collective-permute-done | bytes 98336 | tf_op jit(solution)/shard_map/ppermute | solution.py:12
  47.3 0.6 copy-done.14
  48.0 1.0 maximum_select_fusion.10
  49.4 1.0 maximum_select_fusion.11
  50.7 1.6 %collective-permute-start.11 = (bf16[32,4096]{1,0:T(8,128)(2,1)}, bf16[32,4096]{1,0:T(8,128)(2,1)S(1)}, u32[]{:S(2)}, u32[]{:S(2)}) collective-permute-start(bf16[32,4096]{1,0:T(8,128)(2,1)} %copy-done.8), channel_id=1, source_target_pairs={{0,2},{2,0},{1,3},{3,1},{4,6},{6,4},{5,7},{7,5},{8,10},{10,8},{9,1... | collective-permute-start | bytes 786440 | tf_op jit(solution)/shard_map/ppermute | solution.py:12
  52.7 1.6 %fusion.8 = bf16[256,1024]{1,0:T(8,128)(2,1)S(1)} fusion(bf16[1,768,1024]{2,1,0:T(8,128)(2,1)S(1)} %copy-done, bf16[128,768]{1,0:T(8,128)(2,1)} %collective-permute-done.16, bf16[128,768]{1,0:T(8,128)(2,1)S(1)} %maximum_select_fusion.10, pred[]{:T(512)S(6)} %eq.38), kind=kOutput, calls=%fused_computation.8 | convolution fusion | flops 404684800 | bytes 2490369 | tf_op jit(solution)/shard_map/dot_general | solution.py:185
  54.4 2.8 %shard_map.75 = bf16[128,384]{1,0:T(8,128)(2,1)S(1)} custom-call(s32[1]{0:T(128)} %bitcast.3.index, bf16[32,4096]{1,0:T(8,128)(2,1)S(1)} %copy-done.7, bf16[32,4096]{1,0:T(8,128)(2,1)} %collective-permute-done.5.refs_1_, bf16[32,4096]{1,0:T(8,128)(2,1)S(1)} %copy-done.11, bf16[32,4096]{1,0:T(8,128)(2,1)} %collective-permute-done.14.refs_3_, ...), custom_call_target="tpu_custom_call" | custom-call | tf_op jit(solution)/shard_map/pallas_call | solution.py:142
  57.2 1.7 %collective-permute-start.19 = (bf16[128,384]{1,0:T(8,128)(2,1)S(1)}, bf16[128,384]{1,0:T(8,128)(2,1)S(1)}, u32[]{:S(2)}, u32[]{:S(2)}) collective-permute-start(bf16[128,384]{1,0:T(8,128)(2,1)S(1)} %shard_map.75), channel_id=1, source_target_pairs={{0,2},{2,0},{1,3},{3,1},{4,6},{6,4},{5,7},{7,5},{8,10},{10,8},{9,1... | collective-permute-start | bytes 294920 | tf_op jit(solution)/shard_map/ppermute | solution.py:12
  58.9 0.6 fusion.4
  59.5 0.5 collective-permute-done.11.refs_2_
  60.0 5.6 %collective-permute-done.15.refs_3_ = bf16[32,4096]{1,0:T(8,128)(2,1)S(1)} collective-permute-done((bf16[32,4096]{1,0:T(8,128)(2,1)}, bf16[32,4096]{1,0:T(8,128)(2,1)S(1)}, u32[]{:S(2)}, u32[]{:S(2)}) %collective-permute-start.15) | collective-permute-done | bytes 262176 | tf_op jit(solution)/shard_map/ppermute | solution.py:12
  65.7 2.7 %shard_map.76 = bf16[128,384]{1,0:T(8,128)(2,1)S(1)} custom-call(s32[1]{0:T(128)} %bitcast.3.index, bf16[32,4096]{1,0:T(8,128)(2,1)S(1)} %copy-done.9, bf16[32,4096]{1,0:T(8,128)(2,1)} %collective-permute-done.12.refs_1_, bf16[32,4096]{1,0:T(8,128)(2,1)S(1)} %collective-permute-done.11.refs_2_, bf16[32,4096]{1,0:T(8,128)(2,1)S(1)} %collective-permute-done.15.refs_3_, ...), custom_call_target="tpu_custom_call" | custom-call | tf_op jit(solution)/shard_map/pallas_call | solution.py:142
  68.5 1.7 %collective-permute-start.21 = (bf16[128,384]{1,0:T(8,128)(2,1)S(1)}, bf16[128,384]{1,0:T(8,128)(2,1)S(1)}, u32[]{:S(2)}, u32[]{:S(2)}) collective-permute-start(bf16[128,384]{1,0:T(8,128)(2,1)S(1)} %shard_map.76), channel_id=1, source_target_pairs={{0,2},{2,0},{1,3},{3,1},{4,6},{6,4},{5,7},{7,5},{8,10},{10,8},{9,1... | collective-permute-start | bytes 294920 | tf_op jit(solution)/shard_map/ppermute | solution.py:12
  70.2 0.6 fusion.2
  70.8 2.9 %collective-permute-done.21 = bf16[128,384]{1,0:T(8,128)(2,1)S(1)} collective-permute-done((bf16[128,384]{1,0:T(8,128)(2,1)S(1)}, bf16[128,384]{1,0:T(8,128)(2,1)S(1)}, u32[]{:S(2)}, u32[]{:S(2)}) %collective-permute-start.21) | collective-permute-done | bytes 98336 | tf_op jit(solution)/shard_map/ppermute | solution.py:12
  73.9 0.9 convert_add_fusion
  74.9 2.7 %collective-permute-start.24 = (bf16[128,1024]{1,0:T(8,128)(2,1)S(1)}, bf16[128,1024]{1,0:T(8,128)(2,1)S(1)}, u32[]{:S(2)}, u32[]{:S(2)}) collective-permute-start(bf16[128,1024]{1,0:T(8,128)(2,1)S(1)} %slice.55), channel_id=1, source_target_pairs={{0,4},{4,0},{8,12},{12,8},{1,5},{5,1},{9,13},{13,9},{2,6},{6,2},{1... | collective-permute-start | bytes 786440 | tf_op jit(solution)/shard_map/ppermute | solution.py:65
  77.7 0.6 fusion
  78.3 8.9 %collective-permute-done.24 = bf16[128,1024]{1,0:T(8,128)(2,1)S(1)} collective-permute-done((bf16[128,1024]{1,0:T(8,128)(2,1)S(1)}, bf16[128,1024]{1,0:T(8,128)(2,1)S(1)}, u32[]{:S(2)}, u32[]{:S(2)}) %collective-permute-start.24) | collective-permute-done | bytes 262176 | tf_op jit(solution)/shard_map/ppermute | solution.py:65
  87.2 0.8 fusion.12
  87.9 4.4 %collective-permute-start.25 = (bf16[128,1024]{1,0:T(8,128)(2,1)}, bf16[128,1024]{1,0:T(8,128)(2,1)S(1)}, u32[]{:S(2)}, u32[]{:S(2)}) collective-permute-start(bf16[128,1024]{1,0:T(8,128)(2,1)} %fusion.12), channel_id=1, source_target_pairs={{0,12},{4,8},{8,4},{12,0},{1,13},{5,9},{9,5},{13,1},{2,14},{6,10},... | collective-permute-start | bytes 786440 | tf_op jit(solution)/shard_map/ppermute | solution.py:65
  92.3 0.6 fusion.42
  92.9 1.1 %slice.54 = bf16[128,1024]{1,0:T(8,128)(2,1)S(1)} slice(f32[256,1024]{1,0:T(8,128)} %copy-done.13), slice={[0:128], [0:1024]} | slice | bytes 524288 | tf_op jit(solution)/shard_map/slice | solution.py:188
  94.1 1.2 %compare_reduce_fusion = pred[256]{0:T(512)(128)(4,1)S(1)} fusion(s32[256,1]{0,1:T(1,128)S(1)} %copy-done.16, s32[]{:T(128)S(6)} %select_n.95, s32[]{:T(128)} %bitcast.2, s32[]{:T(128)} %bitcast.1), kind=kLoop, calls=%fused_computation.53 | loop fusion | flops 768 | bytes 1292 | tf_op jit(solution)/shard_map/eq | solution.py:235
  95.3 4.4 %collective-permute-done.25 = bf16[128,1024]{1,0:T(8,128)(2,1)S(1)} collective-permute-done((bf16[128,1024]{1,0:T(8,128)(2,1)}, bf16[128,1024]{1,0:T(8,128)(2,1)S(1)}, u32[]{:S(2)}, u32[]{:S(2)}) %collective-permute-start.25) | collective-permute-done | bytes 262176 | tf_op jit(solution)/shard_map/ppermute | solution.py:65
  100.0 3.8 %collective-permute-done.27 = bf16[128,1024]{1,0:T(8,128)(2,1)} collective-permute-done((bf16[128,1024]{1,0:T(8,128)(2,1)S(1)}, bf16[128,1024]{1,0:T(8,128)(2,1)}, u32[]{:S(2)}, u32[]{:S(2)}) %collective-permute-start.27) | collective-permute-done | bytes 262176 | tf_op jit(solution)/shard_map/ppermute | solution.py:65
  103.8 2.1 %multiply_convert_fusion = bf16[256,1024]{1,0:T(8,128)(2,1)} fusion(f32[256,1024]{1,0:T(8,128)S(1)} %fusion.11, bf16[128,1024]{1,0:T(8,128)(2,1)} %collective-permute-done.27, f32[256]{0:T(256)S(1)} %bitcast.27, pred[256]{0:T(512)(128)(4,1)S(1)} %compare_reduce_fusion, pred[]{:T(512)S(6)} %eq.37), kind=kLoop, calls=%fused_computation.12 | loop fusion | flops 2097152 | bytes 1836289 | tf_op jit(solution)/shard_map/convert_element_type | solution.py:242
  (69 shorter events, 3.2 us)
Async XLA Ops:
  0.0 52.7 %copy-start = (bf16[1,768,1024]{2,1,0:T(8,128)(2,1)S(1)}, bf16[1,768,1024]{2,1,0:T(8,128)(2,1)}, u32[]{:S(2)}) copy-start(bf16[1,768,1024]{2,1,0:T(8,128)(2,1)} %param.10) | copy-start | bytes 4718596
  1.4 2.1 %collective-permute-start = (bf16[128,2048]{1,0:T(8,128)(2,1)S(1)}, bf16[128,2048]{1,0:T(8,128)(2,1)S(1)}, u32[]{:S(2)}, u32[]{:S(2)}) collective-permute-start(bf16[128,2048]{1,0:T(8,128)(2,1)S(1)} %get-tuple-element.78), channel_id=1, source_target_pairs={{0,1},{1,0},{2,3},{3,2},{4,5},{5,4},{6,7},{7,6},{8,9},{9,8},{10,11... | collective-permute-start | bytes 1572872 | tf_op jit(solution)/shard_map/ppermute | solution.py:12
  3.4 2.0 %copy-start.2 = (bf16[1,2048,384]{2,1,0:T(8,128)(2,1)S(1)}, bf16[1,2048,384]{2,1,0:T(8,128)(2,1)}, u32[]{:S(2)}) copy-start(bf16[1,2048,384]{2,1,0:T(8,128)(2,1)} %param.9) | copy-start | bytes 4718596
  3.5 1.5 %copy-start.1 = (bf16[1,2048,384]{2,1,0:T(8,128)(2,1)S(1)}, bf16[1,2048,384]{2,1,0:T(8,128)(2,1)}, u32[]{:S(2)}) copy-start(bf16[1,2048,384]{2,1,0:T(8,128)(2,1)} %param.8) | copy-start | bytes 4718596
  5.0 14.4 %collective-permute-start.3 = (bf16[2048,384]{1,0:T(8,128)(2,1)S(1)}, bf16[2048,384]{1,0:T(8,128)(2,1)S(1)}, u32[]{:S(2)}, u32[]{:S(2)}) collective-permute-start(bf16[2048,384]{1,0:T(8,128)(2,1)S(1)} %bitcast.17), channel_id=1, source_target_pairs={{0,1},{1,0},{2,3},{3,2},{4,5},{5,4},{6,7},{7,6},{8,9},{9,8},{10,11... | collective-permute-start | bytes 4718600 | tf_op jit(solution)/shard_map/ppermute | solution.py:12
  5.4 14.0 %collective-permute-start.4 = (bf16[2048,384]{1,0:T(8,128)(2,1)S(1)}, bf16[2048,384]{1,0:T(8,128)(2,1)S(1)}, u32[]{:S(2)}, u32[]{:S(2)}) collective-permute-start(bf16[2048,384]{1,0:T(8,128)(2,1)S(1)} %bitcast.22), channel_id=1, source_target_pairs={{0,1},{1,0},{2,3},{3,2},{4,5},{5,4},{6,7},{7,6},{8,9},{9,8},{10,11... | collective-permute-start | bytes 4718600 | tf_op jit(solution)/shard_map/ppermute | solution.py:12
  5.7 12.0 %collective-permute-start.1 = (bf16[32,4096]{1,0:T(8,128)(2,1)S(1)}, bf16[32,4096]{1,0:T(8,128)(2,1)S(1)}, u32[]{:S(2)}, u32[]{:S(2)}) collective-permute-start(bf16[32,4096]{1,0:T(8,128)(2,1)S(1)} %get-tuple-element.40), channel_id=1, source_target_pairs={{0,4},{1,13},{4,8},{5,1},{8,12},{9,5},{12,0},{13,9},{2,6},{3,15},{... | collective-permute-start | bytes 786440 | tf_op jit(solution)/shard_map/ppermute | solution.py:75
  8.6 14.8 %collective-permute-start.2 = (bf16[32,4096]{1,0:T(8,128)(2,1)S(1)}, bf16[32,4096]{1,0:T(8,128)(2,1)S(1)}, u32[]{:S(2)}, u32[]{:S(2)}) collective-permute-start(bf16[32,4096]{1,0:T(8,128)(2,1)S(1)} %get-tuple-element.41), channel_id=1, source_target_pairs={{0,4},{1,13},{4,8},{5,1},{8,12},{9,5},{12,0},{13,9},{2,6},{3,15},{... | collective-permute-start | bytes 786440 | tf_op jit(solution)/shard_map/ppermute | solution.py:75
  17.8 11.2 %collective-permute-start.6 = (bf16[32,4096]{1,0:T(8,128)(2,1)S(1)}, bf16[32,4096]{1,0:T(8,128)(2,1)S(1)}, u32[]{:S(2)}, u32[]{:S(2)}) collective-permute-start(bf16[32,4096]{1,0:T(8,128)(2,1)S(1)} %collective-permute-done.1.refs_0_), channel_id=1, source_target_pairs={{0,4},{1,13},{4,8},{5,1},{8,12},{9,5},{12,0},{13,9},{2,6},{3,15},{... | collective-permute-start | bytes 786440 | tf_op jit(solution)/shard_map/ppermute | solution.py:75
  17.8 11.2 %collective-permute-start.7 = (bf16[32,4096]{1,0:T(8,128)(2,1)S(1)}, bf16[32,4096]{1,0:T(8,128)(2,1)S(1)}, u32[]{:S(2)}, u32[]{:S(2)}) collective-permute-start(bf16[32,4096]{1,0:T(8,128)(2,1)S(1)} %collective-permute-done.1.refs_0_), channel_id=1, source_target_pairs={{0,2},{2,0},{1,3},{3,1},{4,6},{6,4},{5,7},{7,5},{8,10},{10,8},{9,1... | collective-permute-start | bytes 786440 | tf_op jit(solution)/shard_map/ppermute | solution.py:12
  19.4 17.0 %copy-start.4 = (bf16[2048,384]{1,0:T(8,128)(2,1)}, bf16[2048,384]{1,0:T(8,128)(2,1)S(1)}, u32[]{:S(2)}) copy-start(bf16[2048,384]{1,0:T(8,128)(2,1)S(1)} %collective-permute-done.3.refs_4_.refs_6_) | copy-start | bytes 4718596
  19.4 1.2 %copy-start.12 = (bf16[2048,384]{1,0:T(8,128)(2,1)}, bf16[2048,384]{1,0:T(8,128)(2,1)S(1)}, u32[]{:S(2)}) copy-start(bf16[2048,384]{1,0:T(8,128)(2,1)S(1)} %collective-permute-done.4.refs_5_.refs_7_) | copy-start | bytes 4718596
  23.4 11.3 %collective-permute-start.5 = (bf16[32,4096]{1,0:T(8,128)(2,1)S(1)}, bf16[32,4096]{1,0:T(8,128)(2,1)}, u32[]{:S(2)}, u32[]{:S(2)}) collective-permute-start(bf16[32,4096]{1,0:T(8,128)(2,1)S(1)} %collective-permute-done.2.refs_1_), channel_id=1, source_target_pairs={{0,4},{1,13},{4,8},{5,1},{8,12},{9,5},{12,0},{13,9},{2,6},{3,15},{... | collective-permute-start | bytes 786440 | tf_op jit(solution)/shard_map/ppermute | solution.py:75
  23.4 11.3 %collective-permute-start.8 = (bf16[32,4096]{1,0:T(8,128)(2,1)S(1)}, bf16[32,4096]{1,0:T(8,128)(2,1)S(1)}, u32[]{:S(2)}, u32[]{:S(2)}) collective-permute-start(bf16[32,4096]{1,0:T(8,128)(2,1)S(1)} %collective-permute-done.2.refs_1_), channel_id=1, source_target_pairs={{0,2},{2,0},{1,3},{3,1},{4,6},{6,4},{5,7},{7,5},{8,10},{10,8},{9,1... | collective-permute-start | bytes 786440 | tf_op jit(solution)/shard_map/ppermute | solution.py:12
  29.0 9.7 %copy-start.6 = (bf16[32,4096]{1,0:T(8,128)(2,1)}, bf16[32,4096]{1,0:T(8,128)(2,1)S(1)}, u32[]{:S(2)}) copy-start(bf16[32,4096]{1,0:T(8,128)(2,1)S(1)} %collective-permute-done.6.refs_0_) | copy-start | bytes 786436
  29.0 11.2 %collective-permute-start.9 = (bf16[32,4096]{1,0:T(8,128)(2,1)S(1)}, bf16[32,4096]{1,0:T(8,128)(2,1)S(1)}, u32[]{:S(2)}, u32[]{:S(2)}) collective-permute-start(bf16[32,4096]{1,0:T(8,128)(2,1)S(1)} %collective-permute-done.6.refs_0_), channel_id=1, source_target_pairs={{0,4},{1,13},{4,8},{5,1},{8,12},{9,5},{12,0},{13,9},{2,6},{3,15},{... | collective-permute-start | bytes 786440 | tf_op jit(solution)/shard_map/ppermute | solution.py:75
  29.0 11.2 %collective-permute-start.10 = (bf16[32,4096]{1,0:T(8,128)(2,1)S(1)}, bf16[32,4096]{1,0:T(8,128)(2,1)S(1)}, u32[]{:S(2)}, u32[]{:S(2)}) collective-permute-start(bf16[32,4096]{1,0:T(8,128)(2,1)S(1)} %collective-permute-done.6.refs_0_), channel_id=1, source_target_pairs={{0,2},{2,0},{1,3},{3,1},{4,6},{6,4},{5,7},{7,5},{8,10},{10,8},{9,1... | collective-permute-start | bytes 786440 | tf_op jit(solution)/shard_map/ppermute | solution.py:12
  34.7 12.6 %collective-permute-start.12 = (bf16[32,4096]{1,0:T(8,128)(2,1)}, bf16[32,4096]{1,0:T(8,128)(2,1)}, u32[]{:S(2)}, u32[]{:S(2)}) collective-permute-start(bf16[32,4096]{1,0:T(8,128)(2,1)} %collective-permute-done.5.refs_1_), channel_id=1, source_target_pairs={{0,4},{1,13},{4,8},{5,1},{8,12},{9,5},{12,0},{13,9},{2,6},{3,15},{... | collective-permute-start | bytes 786440 | tf_op jit(solution)/shard_map/ppermute | solution.py:75
  34.7 13.2 %collective-permute-start.14 = (bf16[32,4096]{1,0:T(8,128)(2,1)}, bf16[32,4096]{1,0:T(8,128)(2,1)}, u32[]{:S(2)}, u32[]{:S(2)}) collective-permute-start(bf16[32,4096]{1,0:T(8,128)(2,1)} %collective-permute-done.5.refs_1_), channel_id=1, source_target_pairs={{0,2},{2,0},{1,3},{3,1},{4,6},{6,4},{5,7},{7,5},{8,10},{10,8},{9,1... | collective-permute-start | bytes 786440 | tf_op jit(solution)/shard_map/ppermute | solution.py:12
  40.2 0.7 copy-start.8
  41.0 0.7 copy-start.10
  41.7 5.7 %collective-permute-start.13 = (bf16[128,384]{1,0:T(8,128)(2,1)S(1)}, bf16[128,384]{1,0:T(8,128)(2,1)S(1)}, u32[]{:S(2)}, u32[]{:S(2)}) collective-permute-start(bf16[128,384]{1,0:T(8,128)(2,1)S(1)} %shard_map.74), channel_id=1, source_target_pairs={{0,2},{2,0},{1,3},{3,1},{4,6},{6,4},{5,7},{7,5},{8,10},{10,8},{9,1... | collective-permute-start | bytes 294920 | tf_op jit(solution)/shard_map/ppermute | solution.py:12
  43.3 6.1 %collective-permute-start.17 = (bf16[128,384]{1,0:T(8,128)(2,1)S(1)}, bf16[128,384]{1,0:T(8,128)(2,1)}, u32[]{:S(2)}, u32[]{:S(2)}) collective-permute-start(bf16[128,384]{1,0:T(8,128)(2,1)S(1)} %shard_map.73), channel_id=1, source_target_pairs={{0,2},{2,0},{1,3},{3,1},{4,6},{6,4},{5,7},{7,5},{8,10},{10,8},{9,1... | collective-permute-start | bytes 294920 | tf_op jit(solution)/shard_map/ppermute | solution.py:12
  47.3 0.6 copy-start.14
  49.0 3.7 %collective-permute-start.16 = (bf16[128,768]{1,0:T(8,128)(2,1)S(1)}, bf16[128,768]{1,0:T(8,128)(2,1)}, u32[]{:S(2)}, u32[]{:S(2)}) collective-permute-start(bf16[128,768]{1,0:T(8,128)(2,1)S(1)} %maximum_select_fusion.10), channel_id=1, source_target_pairs={{0,1},{1,0},{2,3},{3,2},{4,5},{5,4},{6,7},{7,6},{8,9},{9,8},{10,11... | collective-permute-start | bytes 589832 | tf_op jit(solution)/shard_map/ppermute | solution.py:12
  50.4 4.0 %copy-start.3 = (bf16[1,2048,384]{2,1,0:T(8,128)(2,1)S(1)}, bf16[1,2048,384]{2,1,0:T(8,128)(2,1)}, u32[]{:S(2)}) copy-start(bf16[1,2048,384]{2,1,0:T(8,128)(2,1)} %param.9) | copy-start | bytes 4718596
  50.4 4.0 %copy-start.5 = (bf16[2048,384]{1,0:T(8,128)(2,1)S(1)}, bf16[2048,384]{1,0:T(8,128)(2,1)}, u32[]{:S(2)}) copy-start(bf16[2048,384]{1,0:T(8,128)(2,1)} %copy-done.4) | copy-start | bytes 4718596
  50.4 4.0 %copy-start.7 = (bf16[32,4096]{1,0:T(8,128)(2,1)S(1)}, bf16[32,4096]{1,0:T(8,128)(2,1)}, u32[]{:S(2)}) copy-start(bf16[32,4096]{1,0:T(8,128)(2,1)} %copy-done.6) | copy-start | bytes 786436
  50.4 4.0 %copy-start.11 = (bf16[32,4096]{1,0:T(8,128)(2,1)S(1)}, bf16[32,4096]{1,0:T(8,128)(2,1)}, u32[]{:S(2)}) copy-start(bf16[32,4096]{1,0:T(8,128)(2,1)} %copy-done.10) | copy-start | bytes 786436
  50.4 8.4 %collective-permute-start.18 = (bf16[128,768]{1,0:T(8,128)(2,1)S(1)}, bf16[128,768]{1,0:T(8,128)(2,1)S(1)}, u32[]{:S(2)}, u32[]{:S(2)}) collective-permute-start(bf16[128,768]{1,0:T(8,128)(2,1)S(1)} %maximum_select_fusion.11), channel_id=1, source_target_pairs={{0,1},{1,0},{2,3},{3,2},{4,5},{5,4},{6,7},{7,6},{8,9},{9,8},{10,11... | collective-permute-start | bytes 589832 | tf_op jit(solution)/shard_map/ppermute | solution.py:12
  50.7 9.3 %collective-permute-start.11 = (bf16[32,4096]{1,0:T(8,128)(2,1)}, bf16[32,4096]{1,0:T(8,128)(2,1)S(1)}, u32[]{:S(2)}, u32[]{:S(2)}) collective-permute-start(bf16[32,4096]{1,0:T(8,128)(2,1)} %copy-done.8), channel_id=1, source_target_pairs={{0,2},{2,0},{1,3},{3,1},{4,6},{6,4},{5,7},{7,5},{8,10},{10,8},{9,1... | collective-permute-start | bytes 786440 | tf_op jit(solution)/shard_map/ppermute | solution.py:12
  52.3 13.4 %collective-permute-start.15 = (bf16[32,4096]{1,0:T(8,128)(2,1)}, bf16[32,4096]{1,0:T(8,128)(2,1)S(1)}, u32[]{:S(2)}, u32[]{:S(2)}) collective-permute-start(bf16[32,4096]{1,0:T(8,128)(2,1)} %collective-permute-done.12.refs_1_), channel_id=1, source_target_pairs={{0,2},{2,0},{1,3},{3,1},{4,6},{6,4},{5,7},{7,5},{8,10},{10,8},{9,1... | collective-permute-start | bytes 786440 | tf_op jit(solution)/shard_map/ppermute | solution.py:12
  57.2 8.5 %copy-start.9 = (bf16[32,4096]{1,0:T(8,128)(2,1)S(1)}, bf16[32,4096]{1,0:T(8,128)(2,1)}, u32[]{:S(2)}) copy-start(bf16[32,4096]{1,0:T(8,128)(2,1)} %copy-done.8) | copy-start | bytes 786436
  57.2 11.2 %collective-permute-start.19 = (bf16[128,384]{1,0:T(8,128)(2,1)S(1)}, bf16[128,384]{1,0:T(8,128)(2,1)S(1)}, u32[]{:S(2)}, u32[]{:S(2)}) collective-permute-start(bf16[128,384]{1,0:T(8,128)(2,1)S(1)} %shard_map.75), channel_id=1, source_target_pairs={{0,2},{2,0},{1,3},{3,1},{4,6},{6,4},{5,7},{7,5},{8,10},{10,8},{9,1... | collective-permute-start | bytes 294920 | tf_op jit(solution)/shard_map/ppermute | solution.py:12
  59.4 14.3 %collective-permute-start.22 = (bf16[256,1024]{1,0:T(8,128)(2,1)S(1)}, bf16[256,1024]{1,0:T(8,128)(2,1)S(1)}, u32[]{:S(2)}, u32[]{:S(2)}) collective-permute-start(bf16[256,1024]{1,0:T(8,128)(2,1)S(1)} %fusion.8), channel_id=1, source_target_pairs={{0,4},{4,0},{8,12},{12,8},{1,5},{5,1},{9,13},{13,9},{2,6},{6,2},{1... | collective-permute-start | bytes 1572872 | tf_op jit(solution)/shard_map/ppermute | solution.py:65
  68.4 1.8 %collective-permute-start.20 = (bf16[128,768]{1,0:T(8,128)(2,1)S(1)}, bf16[128,768]{1,0:T(8,128)(2,1)S(1)}, u32[]{:S(2)}, u32[]{:S(2)}) collective-permute-start(bf16[128,768]{1,0:T(8,128)(2,1)S(1)} %maximum_select_fusion.12), channel_id=1, source_target_pairs={{0,1},{1,0},{2,3},{3,2},{4,5},{5,4},{6,7},{7,6},{8,9},{9,8},{10,11... | collective-permute-start | bytes 589832 | tf_op jit(solution)/shard_map/ppermute | solution.py:12
  68.5 5.2 %collective-permute-start.21 = (bf16[128,384]{1,0:T(8,128)(2,1)S(1)}, bf16[128,384]{1,0:T(8,128)(2,1)S(1)}, u32[]{:S(2)}, u32[]{:S(2)}) collective-permute-start(bf16[128,384]{1,0:T(8,128)(2,1)S(1)} %shard_map.76), channel_id=1, source_target_pairs={{0,2},{2,0},{1,3},{3,1},{4,6},{6,4},{5,7},{7,5},{8,10},{10,8},{9,1... | collective-permute-start | bytes 294920 | tf_op jit(solution)/shard_map/ppermute | solution.py:12
  73.8 3.9 %collective-permute-start.23 = (bf16[128,768]{1,0:T(8,128)(2,1)S(1)}, bf16[128,768]{1,0:T(8,128)(2,1)S(1)}, u32[]{:S(2)}, u32[]{:S(2)}) collective-permute-start(bf16[128,768]{1,0:T(8,128)(2,1)S(1)} %maximum_select_fusion.13), channel_id=1, source_target_pairs={{0,1},{1,0},{2,3},{3,2},{4,5},{5,4},{6,7},{7,6},{8,9},{9,8},{10,11... | collective-permute-start | bytes 589832 | tf_op jit(solution)/shard_map/ppermute | solution.py:12
  74.8 17.5 %copy-start.17 = (s32[256,1]{0,1:T(1,128)S(1)}, s32[256,1]{0,1:T(1,128)}, u32[]{:S(2)}) copy-start(s32[256,1]{0,1:T(1,128)} %param.12) | copy-start | bytes 3076
  74.8 17.5 %copy-start.15 = (s32[2]{0:T(128)S(1)}, s32[2]{0:T(128)}, u32[]{:S(2)}) copy-start(s32[2]{0:T(128)} %param.13) | copy-start | bytes 28
  74.8 19.2 %collective-permute-start.26 = (bf16[128,1024]{1,0:T(8,128)(2,1)}, bf16[128,1024]{1,0:T(8,128)(2,1)S(1)}, u32[]{:S(2)}, u32[]{:S(2)}) collective-permute-start(bf16[128,1024]{1,0:T(8,128)(2,1)} %get-tuple-element.79), channel_id=1, source_target_pairs={{0,8},{4,12},{8,0},{12,4},{1,9},{5,13},{9,1},{13,5},{2,10},{6,14},... | collective-permute-start | bytes 786440 | tf_op jit(solution)/shard_map/ppermute | solution.py:65
  74.9 12.2 %collective-permute-start.24 = (bf16[128,1024]{1,0:T(8,128)(2,1)S(1)}, bf16[128,1024]{1,0:T(8,128)(2,1)S(1)}, u32[]{:S(2)}, u32[]{:S(2)}) collective-permute-start(bf16[128,1024]{1,0:T(8,128)(2,1)S(1)} %slice.55), channel_id=1, source_target_pairs={{0,4},{4,0},{8,12},{12,8},{1,5},{5,1},{9,13},{13,9},{2,6},{6,2},{1... | collective-permute-start | bytes 786440 | tf_op jit(solution)/shard_map/ppermute | solution.py:65
  78.3 8.9 %copy-start.13 = (f32[256,1024]{1,0:T(8,128)}, f32[256,1024]{1,0:T(8,128)S(1)}, u32[]{:S(2)}) copy-start(f32[256,1024]{1,0:T(8,128)S(1)} %fusion) | copy-start | bytes 3145732
  78.3 15.8 %copy-start.16 = (s32[256,1]{0,1:T(1,128)S(1)}, s32[256,1]{0,1:T(1,128)}, u32[]{:S(2)}) copy-start(s32[256,1]{0,1:T(1,128)} %param.11) | copy-start | bytes 3076
  87.9 11.8 %collective-permute-start.25 = (bf16[128,1024]{1,0:T(8,128)(2,1)}, bf16[128,1024]{1,0:T(8,128)(2,1)S(1)}, u32[]{:S(2)}, u32[]{:S(2)}) collective-permute-start(bf16[128,1024]{1,0:T(8,128)(2,1)} %fusion.12), channel_id=1, source_target_pairs={{0,12},{4,8},{8,4},{12,0},{1,13},{5,9},{9,5},{13,1},{2,14},{6,10},... | collective-permute-start | bytes 786440 | tf_op jit(solution)/shard_map/ppermute | solution.py:65
  94.0 9.9 %collective-permute-start.27 = (bf16[128,1024]{1,0:T(8,128)(2,1)S(1)}, bf16[128,1024]{1,0:T(8,128)(2,1)}, u32[]{:S(2)}, u32[]{:S(2)}) collective-permute-start(bf16[128,1024]{1,0:T(8,128)(2,1)S(1)} %slice.54), channel_id=1, source_target_pairs={{0,4},{4,0},{8,12},{12,8},{1,5},{5,1},{9,13},{13,9},{2,6},{6,2},{1... | collective-permute-start | bytes 786440 | tf_op jit(solution)/shard_map/ppermute | solution.py:65

commit v5 on v4

--- a/solution.py
+++ b/solution.py
@@ -234,11 +234,11 @@
     home = jnp.where(ids == 0, expert_home[0], expert_home[1])
     ours = (home == z // 2)[:, None]
     scale = codes[:, 0].astype(f32) / 1024.0
-    from_pair = in_rows(a_half(part0) + b_half(back1).astype(f32), b_half(part0))
+    from_pair = in_rows(
+        a_half(part0) + b_half(back1).astype(f32), b_half(part0) + sent_a3.astype(f32)
+    )
     from_others = in_rows(home_b3, home_b2).astype(f32)
-    so_far = tied(jnp.where(ours, from_pair, from_others))
-    last = in_rows(jnp.zeros_like(sent_a3), sent_a3).astype(f32)
-    expert_out = (so_far + jnp.where(ours, last, 0.0)).astype(bf16)
+    expert_out = jnp.where(ours, from_pair, from_others).astype(bf16)
     return (scale[:, None] * expert_out.astype(f32)).astype(bf16)
 
 

time: 106 us -> 104 us (0.981)
  waiting for transfers between devices: 49.3 us -> 55.2 us
  starting transfers between devices: 27.5 us -> 22.9 us
  other arithmetic: 7.39 us -> 5.01 us
    ppermute x5, waiting for transfers between devices: 17.2 us -> 20.6 us  [z_send(): return lax.ppermute(x, 'expert', [(i, i ^ distance) for i in range(size)])]
    ppermute x5, starting transfers between devices: 7.39 us -> 4.42 us  [z_send(): return lax.ppermute(x, 'expert', [(i, i ^ distance) for i in range(size)])]
    ppermute x17, waiting for transfers between devices: 14.5 us -> 17 us  [swapped(): lax.ppermute(x, axis, [(i, i ^ 1 << distance) for i in range(lax.axis_siz...]
    select_n x4, other arithmetic: 2.13 us -> 0.21 us  [in_order(): jnp.where(index == 0, jnp.concatenate([own, other], axis), jnp.concatenat...]
    ppermute x17, starting transfers between devices: 15.7 us -> 14 us  [swapped(): lax.ppermute(x, axis, [(i, i ^ 1 << distance) for i in range(lax.axis_siz...]
    unnamed x36 -> x38, local copies, waits for them, and re-layouts: 4.69 us -> 5.06 us
  transfers between devices with their start and end apart: 28 -> 28, of which waited for: 14 -> 14; matrix products, arithmetic and copies ran while one was open for 10% -> 7% of each run, Pallas kernels for 10% -> 10%
where the time goes in v5:
time: 104 us
  waiting for transfers between devices  55.2 us (53%)
  starting transfers between devices  22.9 us (22%)
  Pallas kernels  10.1 us (10%)
  local copies, waits for them, and re-layouts  7.25 us (7%)
  other arithmetic  5.01 us (5%)
  matrix products  3.26 us (3%)
    ppermute x5, waiting for transfers between devices, z_send(): return lax.ppermute(x, 'expert', [(i, i ^ distance) for i in range(size)])  20.6 us
    ppermute x6, waiting for transfers between devices, ring_send(): return lax.ppermute(x, ('expert', 'seq'), pairs)  17.6 us
    ppermute x17, waiting for transfers between devices, swapped(): lax.ppermute(x, axis, [(i, i ^ 1 << distance) for i in range(lax.axis_siz...  17 us
    ppermute x17, starting transfers between devices, swapped(): lax.ppermute(x, axis, [(i, i ^ 1 << distance) for i in range(lax.axis_siz...  14 us
    pallas_call x4, Pallas kernels, hidden_call(): pl.pallas_call(functools.partial(hidden_kernel, len(parts)), out_shape=ja...  10.1 us
    unnamed x38, local copies, waits for them, and re-layouts  5.06 us
    ppermute x6, starting transfers between devices, ring_send(): return lax.ppermute(x, ('expert', 'seq'), pairs)  4.43 us
    ppermute x5, starting transfers between devices, z_send(): return lax.ppermute(x, 'expert', [(i, i ^ distance) for i in range(size)])  4.42 us
  transfers between devices with their start and end apart: 28, of which 14 were waited for; matrix products, arithmetic and copies ran while one was open for 7% of the time, Pallas kernels for 10%

profile of v5, /device:TPU:0, one launch (start us, length us, event | category | flops | bytes accessed | tf_op | source)
XLA Modules:
  0.0 104.1 jit_solution(13695999251900268387)
XLA Ops:
  0.0 1.4 %constant_dynamic-slice_fusion.3 = (bf16[128,2048]{1,0:T(8,128)(2,1)S(1)}, bf16[128,2048]{1,0:T(8,128)(2,1)S(1)}) fusion(bf16[256,2048]{1,0:T(8,128)(2,1)} %param.7, s32[]{:T(128)S(6)} %select_n.90, s32[]{:T(128)S(6)} %select_n.91), kind=kLoop, calls=%fused_computation.59 | loop fusion | bytes 2097160 | tf_op jit(solution)/shard_map/dynamic_slice | solution.py:80
  1.4 0.5 collective-permute-start
  1.9 1.5 %collective-permute-done = bf16[128,2048]{1,0:T(8,128)(2,1)S(1)} collective-permute-done((bf16[128,2048]{1,0:T(8,128)(2,1)S(1)}, bf16[128,2048]{1,0:T(8,128)(2,1)S(1)}, u32[]{:S(2)}, u32[]{:S(2)}) %collective-permute-start) | collective-permute-done | bytes 524320 | tf_op jit(solution)/shard_map/ppermute | solution.py:12
  3.6 1.4 %copy-done.1 = bf16[1,2048,384]{2,1,0:T(8,128)(2,1)S(1)} copy-done((bf16[1,2048,384]{2,1,0:T(8,128)(2,1)S(1)}, bf16[1,2048,384]{2,1,0:T(8,128)(2,1)}, u32[]{:S(2)}) %copy-start.1) | copy-done | bytes 1572888
  5.7 2.8 %collective-permute-start.1 = (bf16[32,4096]{1,0:T(8,128)(2,1)S(1)}, bf16[32,4096]{1,0:T(8,128)(2,1)S(1)}, u32[]{:S(2)}, u32[]{:S(2)}) collective-permute-start(bf16[32,4096]{1,0:T(8,128)(2,1)S(1)} %get-tuple-element.40), channel_id=1, source_target_pairs={{0,4},{1,13},{4,8},{5,1},{8,12},{9,5},{12,0},{13,9},{2,6},{3,15},{... | collective-permute-start | bytes 786440 | tf_op jit(solution)/shard_map/ppermute | solution.py:75
  8.6 1.6 %collective-permute-start.2 = (bf16[32,4096]{1,0:T(8,128)(2,1)S(1)}, bf16[32,4096]{1,0:T(8,128)(2,1)S(1)}, u32[]{:S(2)}, u32[]{:S(2)}) collective-permute-start(bf16[32,4096]{1,0:T(8,128)(2,1)S(1)} %get-tuple-element.41), channel_id=1, source_target_pairs={{0,4},{1,13},{4,8},{5,1},{8,12},{9,5},{12,0},{13,9},{2,6},{3,15},{... | collective-permute-start | bytes 786440 | tf_op jit(solution)/shard_map/ppermute | solution.py:75
  10.2 7.6 %collective-permute-done.1.refs_0_ = bf16[32,4096]{1,0:T(8,128)(2,1)S(1)} collective-permute-done((bf16[32,4096]{1,0:T(8,128)(2,1)S(1)}, bf16[32,4096]{1,0:T(8,128)(2,1)S(1)}, u32[]{:S(2)}, u32[]{:S(2)}) %collective-permute-start.1) | collective-permute-done | bytes 262176 | tf_op jit(solution)/shard_map/ppermute | solution.py:75
  17.8 1.6 %collective-permute-start.7 = (bf16[32,4096]{1,0:T(8,128)(2,1)S(1)}, bf16[32,4096]{1,0:T(8,128)(2,1)S(1)}, u32[]{:S(2)}, u32[]{:S(2)}) collective-permute-start(bf16[32,4096]{1,0:T(8,128)(2,1)S(1)} %collective-permute-done.1.refs_0_), channel_id=1, source_target_pairs={{0,2},{2,0},{1,3},{3,1},{4,6},{6,4},{5,7},{7,5},{8,10},{10,8},{9,1... | collective-permute-start | bytes 786440 | tf_op jit(solution)/shard_map/ppermute | solution.py:12
  19.4 1.2 %copy-done.12 = bf16[2048,384]{1,0:T(8,128)(2,1)} copy-done((bf16[2048,384]{1,0:T(8,128)(2,1)}, bf16[2048,384]{1,0:T(8,128)(2,1)S(1)}, u32[]{:S(2)}) %copy-start.12) | copy-done | bytes 1572888
  20.6 2.3 %shard_map.73 = bf16[128,384]{1,0:T(8,128)(2,1)S(1)} custom-call(s32[1]{0:T(128)} %bitcast.3.index, bf16[64,4096]{1,0:T(8,128)(2,1)S(1)} %get-tuple-element.39.refs_0_, bf16[64,4096]{1,0:T(8,128)(2,1)S(1)} %get-tuple-element.43.refs_1_, bf16[2048,384]{1,0:T(8,128)(2,1)S(1)} %bitcast.18, bf16[2048,384]{1,0:T(8,128)(2,1)S(1)} %bitcast.23, ...), custom_call_target="tpu_custom_call" | custom-call | tf_op jit(solution)/shard_map/pallas_call | solution.py:142
  23.0 0.4 collective-permute-done.2.refs_1_
  23.4 1.6 %collective-permute-start.8 = (bf16[32,4096]{1,0:T(8,128)(2,1)S(1)}, bf16[32,4096]{1,0:T(8,128)(2,1)S(1)}, u32[]{:S(2)}, u32[]{:S(2)}) collective-permute-start(bf16[32,4096]{1,0:T(8,128)(2,1)S(1)} %collective-permute-done.2.refs_1_), channel_id=1, source_target_pairs={{0,2},{2,0},{1,3},{3,1},{4,6},{6,4},{5,7},{7,5},{8,10},{10,8},{9,1... | collective-permute-start | bytes 786440 | tf_op jit(solution)/shard_map/ppermute | solution.py:12
  25.0 4.0 %collective-permute-done.6.refs_0_ = bf16[32,4096]{1,0:T(8,128)(2,1)S(1)} collective-permute-done((bf16[32,4096]{1,0:T(8,128)(2,1)S(1)}, bf16[32,4096]{1,0:T(8,128)(2,1)S(1)}, u32[]{:S(2)}, u32[]{:S(2)}) %collective-permute-start.6) | collective-permute-done | bytes 262176 | tf_op jit(solution)/shard_map/ppermute | solution.py:75
  29.0 1.7 %collective-permute-start.10 = (bf16[32,4096]{1,0:T(8,128)(2,1)S(1)}, bf16[32,4096]{1,0:T(8,128)(2,1)S(1)}, u32[]{:S(2)}, u32[]{:S(2)}) collective-permute-start(bf16[32,4096]{1,0:T(8,128)(2,1)S(1)} %collective-permute-done.6.refs_0_), channel_id=1, source_target_pairs={{0,2},{2,0},{1,3},{3,1},{4,6},{6,4},{5,7},{7,5},{8,10},{10,8},{9,1... | collective-permute-start | bytes 786440 | tf_op jit(solution)/shard_map/ppermute | solution.py:12
  30.7 4.0 %collective-permute-done.5.refs_1_ = bf16[32,4096]{1,0:T(8,128)(2,1)} collective-permute-done((bf16[32,4096]{1,0:T(8,128)(2,1)S(1)}, bf16[32,4096]{1,0:T(8,128)(2,1)}, u32[]{:S(2)}, u32[]{:S(2)}) %collective-permute-start.5) | collective-permute-done | bytes 262176 | tf_op jit(solution)/shard_map/ppermute | solution.py:75
  34.7 1.6 %collective-permute-start.14 = (bf16[32,4096]{1,0:T(8,128)(2,1)}, bf16[32,4096]{1,0:T(8,128)(2,1)}, u32[]{:S(2)}, u32[]{:S(2)}) collective-permute-start(bf16[32,4096]{1,0:T(8,128)(2,1)} %collective-permute-done.5.refs_1_), channel_id=1, source_target_pairs={{0,2},{2,0},{1,3},{3,1},{4,6},{6,4},{5,7},{7,5},{8,10},{10,8},{9,1... | collective-permute-start | bytes 786440 | tf_op jit(solution)/shard_map/ppermute | solution.py:12
  36.4 2.3 %shard_map.74 = bf16[128,384]{1,0:T(8,128)(2,1)S(1)} custom-call(s32[1]{0:T(128)} %bitcast.3.index, bf16[32,4096]{1,0:T(8,128)(2,1)S(1)} %collective-permute-done.1.refs_0_, bf16[32,4096]{1,0:T(8,128)(2,1)S(1)} %collective-permute-done.2.refs_1_, bf16[32,4096]{1,0:T(8,128)(2,1)S(1)} %collective-permute-done.7.refs_2_, ...), custom_call_target="tpu_custom_call" | custom-call | tf_op jit(solution)/shard_map/pallas_call | solution.py:142
  38.7 1.5 %collective-permute-done.9.refs_0_ = bf16[32,4096]{1,0:T(8,128)(2,1)S(1)} collective-permute-done((bf16[32,4096]{1,0:T(8,128)(2,1)S(1)}, bf16[32,4096]{1,0:T(8,128)(2,1)S(1)}, u32[]{:S(2)}, u32[]{:S(2)}) %collective-permute-start.9) | collective-permute-done | bytes 262176 | tf_op jit(solution)/shard_map/ppermute | solution.py:75
  40.3 0.7 copy-done.8
  41.0 0.7 copy-done.10
  41.7 1.6 %collective-permute-start.13 = (bf16[128,384]{1,0:T(8,128)(2,1)S(1)}, bf16[128,384]{1,0:T(8,128)(2,1)S(1)}, u32[]{:S(2)}, u32[]{:S(2)}) collective-permute-start(bf16[128,384]{1,0:T(8,128)(2,1)S(1)} %shard_map.74), channel_id=1, source_target_pairs={{0,2},{2,0},{1,3},{3,1},{4,6},{6,4},{5,7},{7,5},{8,10},{10,8},{9,1... | collective-permute-start | bytes 294920 | tf_op jit(solution)/shard_map/ppermute | solution.py:12
  43.3 0.4 collective-permute-start.17
  43.7 3.6 %collective-permute-done.13 = bf16[128,384]{1,0:T(8,128)(2,1)S(1)} collective-permute-done((bf16[128,384]{1,0:T(8,128)(2,1)S(1)}, bf16[128,384]{1,0:T(8,128)(2,1)S(1)}, u32[]{:S(2)}, u32[]{:S(2)}) %collective-permute-start.13) | collective-permute-done | bytes 98336 | tf_op jit(solution)/shard_map/ppermute | solution.py:12
  47.5 0.6 fusion.43
  48.1 1.2 %collective-permute-done.17 = bf16[128,384]{1,0:T(8,128)(2,1)S(1)} collective-permute-done((bf16[128,384]{1,0:T(8,128)(2,1)S(1)}, bf16[128,384]{1,0:T(8,128)(2,1)S(1)}, u32[]{:S(2)}, u32[]{:S(2)}) %collective-permute-start.17) | collective-permute-done | bytes 98336 | tf_op jit(solution)/shard_map/ppermute | solution.py:12
  49.4 0.9 collective-permute-start.11
  50.3 1.2 %collective-permute-start.15 = (bf16[32,4096]{1,0:T(8,128)(2,1)}, bf16[32,4096]{1,0:T(8,128)(2,1)S(1)}, u32[]{:S(2)}, u32[]{:S(2)}) collective-permute-start(bf16[32,4096]{1,0:T(8,128)(2,1)} %collective-permute-done.12.refs_1_), channel_id=1, source_target_pairs={{0,2},{2,0},{1,3},{3,1},{4,6},{6,4},{5,7},{7,5},{8,10},{10,8},{9,1... | collective-permute-start | bytes 786440 | tf_op jit(solution)/shard_map/ppermute | solution.py:12
  51.5 0.6 fusion.8
  52.1 2.8 %shard_map.75 = bf16[128,384]{1,0:T(8,128)(2,1)S(1)} custom-call(s32[1]{0:T(128)} %bitcast.3.index, bf16[32,4096]{1,0:T(8,128)(2,1)S(1)} %copy-done.7, bf16[32,4096]{1,0:T(8,128)(2,1)} %collective-permute-done.5.refs_1_, bf16[32,4096]{1,0:T(8,128)(2,1)S(1)} %copy-done.11, bf16[32,4096]{1,0:T(8,128)(2,1)} %collective-permute-done.14.refs_3_, ...), custom_call_target="tpu_custom_call" | custom-call | tf_op jit(solution)/shard_map/pallas_call | solution.py:142
  54.9 0.9 collective-permute-start.19
  55.9 1.5 %fusion.4 = f32[256,1024]{1,0:T(8,128)} fusion(bf16[1,768,1024]{2,1,0:T(8,128)(2,1)S(1)} %copy-done, bf16[128,768]{1,0:T(8,128)(2,1)S(1)} %collective-permute-done.18, bf16[128,768]{1,0:T(8,128)(2,1)S(1)} %maximum_select_fusion.11, pred[]{:T(512)S(6)} %eq.37), kind=kOutput, calls=%fused_computation.4 | convolution fusion | flops 404422656 | bytes 3014657 | tf_op jit(solution)/shard_map/dot_general | solution.py:185
  57.4 1.4 %collective-permute-done.11.refs_2_ = bf16[32,4096]{1,0:T(8,128)(2,1)S(1)} collective-permute-done((bf16[32,4096]{1,0:T(8,128)(2,1)}, bf16[32,4096]{1,0:T(8,128)(2,1)S(1)}, u32[]{:S(2)}, u32[]{:S(2)}) %collective-permute-start.11) | collective-permute-done | bytes 262176 | tf_op jit(solution)/shard_map/ppermute | solution.py:12
  58.8 5.6 %collective-permute-done.15.refs_3_ = bf16[32,4096]{1,0:T(8,128)(2,1)S(1)} collective-permute-done((bf16[32,4096]{1,0:T(8,128)(2,1)}, bf16[32,4096]{1,0:T(8,128)(2,1)S(1)}, u32[]{:S(2)}, u32[]{:S(2)}) %collective-permute-start.15) | collective-permute-done | bytes 262176 | tf_op jit(solution)/shard_map/ppermute | solution.py:12
  64.4 2.7 %shard_map.76 = bf16[128,384]{1,0:T(8,128)(2,1)S(1)} custom-call(s32[1]{0:T(128)} %bitcast.3.index, bf16[32,4096]{1,0:T(8,128)(2,1)S(1)} %copy-done.9, bf16[32,4096]{1,0:T(8,128)(2,1)} %collective-permute-done.12.refs_1_, bf16[32,4096]{1,0:T(8,128)(2,1)S(1)} %collective-permute-done.11.refs_2_, bf16[32,4096]{1,0:T(8,128)(2,1)S(1)} %collective-permute-done.15.refs_3_, ...), custom_call_target="tpu_custom_call" | custom-call | tf_op jit(solution)/shard_map/pallas_call | solution.py:142
  67.3 0.9 collective-permute-start.21
  68.2 0.5 collective-permute-done.20
  68.7 0.6 fusion.2
  69.3 3.2 %collective-permute-done.21 = bf16[128,384]{1,0:T(8,128)(2,1)S(1)} collective-permute-done((bf16[128,384]{1,0:T(8,128)(2,1)S(1)}, bf16[128,384]{1,0:T(8,128)(2,1)S(1)}, u32[]{:S(2)}, u32[]{:S(2)}) %collective-permute-start.21) | collective-permute-done | bytes 98336 | tf_op jit(solution)/shard_map/ppermute | solution.py:12
  72.8 2.8 %collective-permute-start.26 = (bf16[128,1024]{1,0:T(8,128)(2,1)S(1)}, bf16[128,1024]{1,0:T(8,128)(2,1)}, u32[]{:S(2)}, u32[]{:S(2)}) collective-permute-start(bf16[128,1024]{1,0:T(8,128)(2,1)S(1)} %slice.55), channel_id=1, source_target_pairs={{0,4},{4,0},{8,12},{12,8},{1,5},{5,1},{9,13},{13,9},{2,6},{6,2},{1... | collective-permute-start | bytes 786440 | tf_op jit(solution)/shard_map/ppermute | solution.py:65
  75.6 0.6 fusion
  76.2 1.0 copy-done.14
  77.2 10.6 %collective-permute-done.24 = bf16[128,1024]{1,0:T(8,128)(2,1)S(1)} collective-permute-done((bf16[128,1024]{1,0:T(8,128)(2,1)S(1)}, bf16[128,1024]{1,0:T(8,128)(2,1)S(1)}, u32[]{:S(2)}, u32[]{:S(2)}) %collective-permute-start.24) | collective-permute-done | bytes 262176 | tf_op jit(solution)/shard_map/ppermute | solution.py:65
  87.8 1.2 %compare_reduce_fusion = pred[256]{0:T(512)(128)(4,1)S(1)} fusion(s32[256,1]{0,1:T(1,128)S(1)} %copy-done.17, s32[]{:T(128)S(6)} %select_n.87, s32[]{:T(128)} %bitcast.2, s32[]{:T(128)} %bitcast.1), kind=kLoop, calls=%fused_computation.54 | loop fusion | flops 768 | bytes 1292 | tf_op jit(solution)/shard_map/eq | solution.py:235
  89.0 1.2 %fusion.13 = bf16[128,1024]{1,0:T(8,128)(2,1)S(1)} fusion(f32[256,1024]{1,0:T(8,128)} %copy-done.14, bf16[128,1024]{1,0:T(8,128)(2,1)} %collective-permute-done.26), kind=kLoop, calls=%fused_computation.16 | loop fusion | flops 393216 | bytes 1048576 | tf_op jit(solution)/shard_map/convert_element_type | solution.py:194
  90.2 1.6 %collective-permute-start.27 = (bf16[128,1024]{1,0:T(8,128)(2,1)S(1)}, bf16[128,1024]{1,0:T(8,128)(2,1)S(1)}, u32[]{:S(2)}, u32[]{:S(2)}) collective-permute-start(bf16[128,1024]{1,0:T(8,128)(2,1)S(1)} %fusion.13), channel_id=1, source_target_pairs={{0,12},{4,8},{8,4},{12,0},{1,13},{5,9},{9,5},{13,1},{2,14},{6,10},... | collective-permute-start | bytes 786440 | tf_op jit(solution)/shard_map/ppermute | solution.py:65
  91.8 10.0 %collective-permute-done.25 = bf16[128,1024]{1,0:T(8,128)(2,1)} collective-permute-done((bf16[128,1024]{1,0:T(8,128)(2,1)S(1)}, bf16[128,1024]{1,0:T(8,128)(2,1)}, u32[]{:S(2)}, u32[]{:S(2)}) %collective-permute-start.25) | collective-permute-done | bytes 262176 | tf_op jit(solution)/shard_map/ppermute | solution.py:65
  101.8 1.2 %convert_add_fusion = (bf16[128,1024]{1,0:T(8,128)(2,1)S(1)}, bf16[128,1024]{1,0:T(8,128)(2,1)S(1)}) fusion(bf16[128,1024]{1,0:T(8,128)(2,1)} %collective-permute-done.25, f32[256,1024]{1,0:T(8,128)S(1)} %copy-done.13, bf16[256,1024]{1,0:T(8,128)(2,1)} %copy-done.15), kind=kLoop, calls=%fused_computation.19 | loop fusion | flops 786432 | bytes 2097152 | tf_op jit(solution)/shard_map/add | solution.py:238
  103.0 1.1 %multiply_convert_fusion = bf16[256,1024]{1,0:T(8,128)(2,1)} fusion(bf16[128,1024]{1,0:T(8,128)(2,1)S(1)} %get-tuple-element.74, bf16[128,1024]{1,0:T(8,128)(2,1)S(1)} %get-tuple-element.73, bf16[128,1024]{1,0:T(8,128)(2,1)S(1)} %collective-permute-done.24, bf16[128,1024]{1,0:T(8,128)(2,1)S(1)} %collective-permute-done.27, f32[256]{0:T(256)S(1)} %bitcast.27, ...), kind=kLoop, calls=%fused_computation.13 | loop fusion | flops 6029312 | bytes 1574145 | tf_op jit(solution)/shard_map/convert_element_type | solution.py:242
  (71 shorter events, 1.7 us)
Async XLA Ops:
  0.0 51.5 %copy-start = (bf16[1,768,1024]{2,1,0:T(8,128)(2,1)S(1)}, bf16[1,768,1024]{2,1,0:T(8,128)(2,1)}, u32[]{:S(2)}) copy-start(bf16[1,768,1024]{2,1,0:T(8,128)(2,1)} %param.10) | copy-start | bytes 4718596
  1.4 2.1 %collective-permute-start = (bf16[128,2048]{1,0:T(8,128)(2,1)S(1)}, bf16[128,2048]{1,0:T(8,128)(2,1)S(1)}, u32[]{:S(2)}, u32[]{:S(2)}) collective-permute-start(bf16[128,2048]{1,0:T(8,128)(2,1)S(1)} %get-tuple-element.78), channel_id=1, source_target_pairs={{0,1},{1,0},{2,3},{3,2},{4,5},{5,4},{6,7},{7,6},{8,9},{9,8},{10,11... | collective-permute-start | bytes 1572872 | tf_op jit(solution)/shard_map/ppermute | solution.py:12
  3.4 2.0 %copy-start.2 = (bf16[1,2048,384]{2,1,0:T(8,128)(2,1)S(1)}, bf16[1,2048,384]{2,1,0:T(8,128)(2,1)}, u32[]{:S(2)}) copy-start(bf16[1,2048,384]{2,1,0:T(8,128)(2,1)} %param.9) | copy-start | bytes 4718596
  3.5 1.5 %copy-start.1 = (bf16[1,2048,384]{2,1,0:T(8,128)(2,1)S(1)}, bf16[1,2048,384]{2,1,0:T(8,128)(2,1)}, u32[]{:S(2)}) copy-start(bf16[1,2048,384]{2,1,0:T(8,128)(2,1)} %param.8) | copy-start | bytes 4718596
  5.0 14.4 %collective-permute-start.3 = (bf16[2048,384]{1,0:T(8,128)(2,1)S(1)}, bf16[2048,384]{1,0:T(8,128)(2,1)S(1)}, u32[]{:S(2)}, u32[]{:S(2)}) collective-permute-start(bf16[2048,384]{1,0:T(8,128)(2,1)S(1)} %bitcast.17), channel_id=1, source_target_pairs={{0,1},{1,0},{2,3},{3,2},{4,5},{5,4},{6,7},{7,6},{8,9},{9,8},{10,11... | collective-permute-start | bytes 4718600 | tf_op jit(solution)/shard_map/ppermute | solution.py:12
  5.4 14.0 %collective-permute-start.4 = (bf16[2048,384]{1,0:T(8,128)(2,1)S(1)}, bf16[2048,384]{1,0:T(8,128)(2,1)S(1)}, u32[]{:S(2)}, u32[]{:S(2)}) collective-permute-start(bf16[2048,384]{1,0:T(8,128)(2,1)S(1)} %bitcast.22), channel_id=1, source_target_pairs={{0,1},{1,0},{2,3},{3,2},{4,5},{5,4},{6,7},{7,6},{8,9},{9,8},{10,11... | collective-permute-start | bytes 4718600 | tf_op jit(solution)/shard_map/ppermute | solution.py:12
  5.7 12.0 %collective-permute-start.1 = (bf16[32,4096]{1,0:T(8,128)(2,1)S(1)}, bf16[32,4096]{1,0:T(8,128)(2,1)S(1)}, u32[]{:S(2)}, u32[]{:S(2)}) collective-permute-start(bf16[32,4096]{1,0:T(8,128)(2,1)S(1)} %get-tuple-element.40), channel_id=1, source_target_pairs={{0,4},{1,13},{4,8},{5,1},{8,12},{9,5},{12,0},{13,9},{2,6},{3,15},{... | collective-permute-start | bytes 786440 | tf_op jit(solution)/shard_map/ppermute | solution.py:75
  8.6 14.8 %collective-permute-start.2 = (bf16[32,4096]{1,0:T(8,128)(2,1)S(1)}, bf16[32,4096]{1,0:T(8,128)(2,1)S(1)}, u32[]{:S(2)}, u32[]{:S(2)}) collective-permute-start(bf16[32,4096]{1,0:T(8,128)(2,1)S(1)} %get-tuple-element.41), channel_id=1, source_target_pairs={{0,4},{1,13},{4,8},{5,1},{8,12},{9,5},{12,0},{13,9},{2,6},{3,15},{... | collective-permute-start | bytes 786440 | tf_op jit(solution)/shard_map/ppermute | solution.py:75
  17.8 11.2 %collective-permute-start.6 = (bf16[32,4096]{1,0:T(8,128)(2,1)S(1)}, bf16[32,4096]{1,0:T(8,128)(2,1)S(1)}, u32[]{:S(2)}, u32[]{:S(2)}) collective-permute-start(bf16[32,4096]{1,0:T(8,128)(2,1)S(1)} %collective-permute-done.1.refs_0_), channel_id=1, source_target_pairs={{0,4},{1,13},{4,8},{5,1},{8,12},{9,5},{12,0},{13,9},{2,6},{3,15},{... | collective-permute-start | bytes 786440 | tf_op jit(solution)/shard_map/ppermute | solution.py:75
  17.8 11.2 %collective-permute-start.7 = (bf16[32,4096]{1,0:T(8,128)(2,1)S(1)}, bf16[32,4096]{1,0:T(8,128)(2,1)S(1)}, u32[]{:S(2)}, u32[]{:S(2)}) collective-permute-start(bf16[32,4096]{1,0:T(8,128)(2,1)S(1)} %collective-permute-done.1.refs_0_), channel_id=1, source_target_pairs={{0,2},{2,0},{1,3},{3,1},{4,6},{6,4},{5,7},{7,5},{8,10},{10,8},{9,1... | collective-permute-start | bytes 786440 | tf_op jit(solution)/shard_map/ppermute | solution.py:12
  19.4 17.0 %copy-start.4 = (bf16[2048,384]{1,0:T(8,128)(2,1)}, bf16[2048,384]{1,0:T(8,128)(2,1)S(1)}, u32[]{:S(2)}) copy-start(bf16[2048,384]{1,0:T(8,128)(2,1)S(1)} %collective-permute-done.3.refs_4_.refs_6_) | copy-start | bytes 4718596
  19.4 1.2 %copy-start.12 = (bf16[2048,384]{1,0:T(8,128)(2,1)}, bf16[2048,384]{1,0:T(8,128)(2,1)S(1)}, u32[]{:S(2)}) copy-start(bf16[2048,384]{1,0:T(8,128)(2,1)S(1)} %collective-permute-done.4.refs_5_.refs_7_) | copy-start | bytes 4718596
  22.9 24.5 %copy-start.16 = (s32[2]{0:T(128)S(1)}, s32[2]{0:T(128)}, u32[]{:S(2)}) copy-start(s32[2]{0:T(128)} %param.13) | copy-start | bytes 28
  23.4 11.3 %collective-permute-start.5 = (bf16[32,4096]{1,0:T(8,128)(2,1)S(1)}, bf16[32,4096]{1,0:T(8,128)(2,1)}, u32[]{:S(2)}, u32[]{:S(2)}) collective-permute-start(bf16[32,4096]{1,0:T(8,128)(2,1)S(1)} %collective-permute-done.2.refs_1_), channel_id=1, source_target_pairs={{0,4},{1,13},{4,8},{5,1},{8,12},{9,5},{12,0},{13,9},{2,6},{3,15},{... | collective-permute-start | bytes 786440 | tf_op jit(solution)/shard_map/ppermute | solution.py:75
  23.4 11.3 %collective-permute-start.8 = (bf16[32,4096]{1,0:T(8,128)(2,1)S(1)}, bf16[32,4096]{1,0:T(8,128)(2,1)S(1)}, u32[]{:S(2)}, u32[]{:S(2)}) collective-permute-start(bf16[32,4096]{1,0:T(8,128)(2,1)S(1)} %collective-permute-done.2.refs_1_), channel_id=1, source_target_pairs={{0,2},{2,0},{1,3},{3,1},{4,6},{6,4},{5,7},{7,5},{8,10},{10,8},{9,1... | collective-permute-start | bytes 786440 | tf_op jit(solution)/shard_map/ppermute | solution.py:12
  29.0 9.7 %copy-start.6 = (bf16[32,4096]{1,0:T(8,128)(2,1)}, bf16[32,4096]{1,0:T(8,128)(2,1)S(1)}, u32[]{:S(2)}) copy-start(bf16[32,4096]{1,0:T(8,128)(2,1)S(1)} %collective-permute-done.6.refs_0_) | copy-start | bytes 786436
  29.0 11.2 %collective-permute-start.9 = (bf16[32,4096]{1,0:T(8,128)(2,1)S(1)}, bf16[32,4096]{1,0:T(8,128)(2,1)S(1)}, u32[]{:S(2)}, u32[]{:S(2)}) collective-permute-start(bf16[32,4096]{1,0:T(8,128)(2,1)S(1)} %collective-permute-done.6.refs_0_), channel_id=1, source_target_pairs={{0,4},{1,13},{4,8},{5,1},{8,12},{9,5},{12,0},{13,9},{2,6},{3,15},{... | collective-permute-start | bytes 786440 | tf_op jit(solution)/shard_map/ppermute | solution.py:75
  29.0 11.2 %collective-permute-start.10 = (bf16[32,4096]{1,0:T(8,128)(2,1)S(1)}, bf16[32,4096]{1,0:T(8,128)(2,1)S(1)}, u32[]{:S(2)}, u32[]{:S(2)}) collective-permute-start(bf16[32,4096]{1,0:T(8,128)(2,1)S(1)} %collective-permute-done.6.refs_0_), channel_id=1, source_target_pairs={{0,2},{2,0},{1,3},{3,1},{4,6},{6,4},{5,7},{7,5},{8,10},{10,8},{9,1... | collective-permute-start | bytes 786440 | tf_op jit(solution)/shard_map/ppermute | solution.py:12
  34.7 12.6 %collective-permute-start.12 = (bf16[32,4096]{1,0:T(8,128)(2,1)}, bf16[32,4096]{1,0:T(8,128)(2,1)}, u32[]{:S(2)}, u32[]{:S(2)}) collective-permute-start(bf16[32,4096]{1,0:T(8,128)(2,1)} %collective-permute-done.5.refs_1_), channel_id=1, source_target_pairs={{0,4},{1,13},{4,8},{5,1},{8,12},{9,5},{12,0},{13,9},{2,6},{3,15},{... | collective-permute-start | bytes 786440 | tf_op jit(solution)/shard_map/ppermute | solution.py:75
  34.7 12.6 %collective-permute-start.14 = (bf16[32,4096]{1,0:T(8,128)(2,1)}, bf16[32,4096]{1,0:T(8,128)(2,1)}, u32[]{:S(2)}, u32[]{:S(2)}) collective-permute-start(bf16[32,4096]{1,0:T(8,128)(2,1)} %collective-permute-done.5.refs_1_), channel_id=1, source_target_pairs={{0,2},{2,0},{1,3},{3,1},{4,6},{6,4},{5,7},{7,5},{8,10},{10,8},{9,1... | collective-permute-start | bytes 786440 | tf_op jit(solution)/shard_map/ppermute | solution.py:12
  40.2 0.7 copy-start.8
  40.9 0.7 copy-start.10
  41.7 5.7 %collective-permute-start.13 = (bf16[128,384]{1,0:T(8,128)(2,1)S(1)}, bf16[128,384]{1,0:T(8,128)(2,1)S(1)}, u32[]{:S(2)}, u32[]{:S(2)}) collective-permute-start(bf16[128,384]{1,0:T(8,128)(2,1)S(1)} %shard_map.74), channel_id=1, source_target_pairs={{0,2},{2,0},{1,3},{3,1},{4,6},{6,4},{5,7},{7,5},{8,10},{10,8},{9,1... | collective-permute-start | bytes 294920 | tf_op jit(solution)/shard_map/ppermute | solution.py:12
  43.3 6.0 %collective-permute-start.17 = (bf16[128,384]{1,0:T(8,128)(2,1)S(1)}, bf16[128,384]{1,0:T(8,128)(2,1)S(1)}, u32[]{:S(2)}, u32[]{:S(2)}) collective-permute-start(bf16[128,384]{1,0:T(8,128)(2,1)S(1)} %shard_map.73), channel_id=1, source_target_pairs={{0,2},{2,0},{1,3},{3,1},{4,6},{6,4},{5,7},{7,5},{8,10},{10,8},{9,1... | collective-permute-start | bytes 294920 | tf_op jit(solution)/shard_map/ppermute | solution.py:12
  47.4 4.1 %collective-permute-start.16 = (bf16[128,768]{1,0:T(8,128)(2,1)S(1)}, bf16[128,768]{1,0:T(8,128)(2,1)S(1)}, u32[]{:S(2)}, u32[]{:S(2)}) collective-permute-start(bf16[128,768]{1,0:T(8,128)(2,1)S(1)} %maximum_select_fusion.10), channel_id=1, source_target_pairs={{0,1},{1,0},{2,3},{3,2},{4,5},{5,4},{6,7},{7,6},{8,9},{9,8},{10,11... | collective-permute-start | bytes 589832 | tf_op jit(solution)/shard_map/ppermute | solution.py:12
  49.3 2.8 %copy-start.3 = (bf16[1,2048,384]{2,1,0:T(8,128)(2,1)S(1)}, bf16[1,2048,384]{2,1,0:T(8,128)(2,1)}, u32[]{:S(2)}) copy-start(bf16[1,2048,384]{2,1,0:T(8,128)(2,1)} %param.9) | copy-start | bytes 4718596
  49.3 2.8 %copy-start.5 = (bf16[2048,384]{1,0:T(8,128)(2,1)S(1)}, bf16[2048,384]{1,0:T(8,128)(2,1)}, u32[]{:S(2)}) copy-start(bf16[2048,384]{1,0:T(8,128)(2,1)} %copy-done.4) | copy-start | bytes 4718596
  49.3 2.8 %copy-start.7 = (bf16[32,4096]{1,0:T(8,128)(2,1)S(1)}, bf16[32,4096]{1,0:T(8,128)(2,1)}, u32[]{:S(2)}) copy-start(bf16[32,4096]{1,0:T(8,128)(2,1)} %copy-done.6) | copy-start | bytes 786436
  49.3 2.8 %copy-start.11 = (bf16[32,4096]{1,0:T(8,128)(2,1)S(1)}, bf16[32,4096]{1,0:T(8,128)(2,1)}, u32[]{:S(2)}) copy-start(bf16[32,4096]{1,0:T(8,128)(2,1)} %copy-done.10) | copy-start | bytes 786436
  49.3 6.5 %collective-permute-start.18 = (bf16[128,768]{1,0:T(8,128)(2,1)S(1)}, bf16[128,768]{1,0:T(8,128)(2,1)S(1)}, u32[]{:S(2)}, u32[]{:S(2)}) collective-permute-start(bf16[128,768]{1,0:T(8,128)(2,1)S(1)} %maximum_select_fusion.11), channel_id=1, source_target_pairs={{0,1},{1,0},{2,3},{3,2},{4,5},{5,4},{6,7},{7,6},{8,9},{9,8},{10,11... | collective-permute-start | bytes 589832 | tf_op jit(solution)/shard_map/ppermute | solution.py:12
  49.4 9.4 %collective-permute-start.11 = (bf16[32,4096]{1,0:T(8,128)(2,1)}, bf16[32,4096]{1,0:T(8,128)(2,1)S(1)}, u32[]{:S(2)}, u32[]{:S(2)}) collective-permute-start(bf16[32,4096]{1,0:T(8,128)(2,1)} %copy-done.8), channel_id=1, source_target_pairs={{0,2},{2,0},{1,3},{3,1},{4,6},{6,4},{5,7},{7,5},{8,10},{10,8},{9,1... | collective-permute-start | bytes 786440 | tf_op jit(solution)/shard_map/ppermute | solution.py:12
  50.3 14.1 %collective-permute-start.15 = (bf16[32,4096]{1,0:T(8,128)(2,1)}, bf16[32,4096]{1,0:T(8,128)(2,1)S(1)}, u32[]{:S(2)}, u32[]{:S(2)}) collective-permute-start(bf16[32,4096]{1,0:T(8,128)(2,1)} %collective-permute-done.12.refs_1_), channel_id=1, source_target_pairs={{0,2},{2,0},{1,3},{3,1},{4,6},{6,4},{5,7},{7,5},{8,10},{10,8},{9,1... | collective-permute-start | bytes 786440 | tf_op jit(solution)/shard_map/ppermute | solution.py:12
  54.9 9.5 %copy-start.9 = (bf16[32,4096]{1,0:T(8,128)(2,1)S(1)}, bf16[32,4096]{1,0:T(8,128)(2,1)}, u32[]{:S(2)}) copy-start(bf16[32,4096]{1,0:T(8,128)(2,1)} %copy-done.8) | copy-start | bytes 786436
  54.9 12.2 %collective-permute-start.19 = (bf16[128,384]{1,0:T(8,128)(2,1)S(1)}, bf16[128,384]{1,0:T(8,128)(2,1)S(1)}, u32[]{:S(2)}, u32[]{:S(2)}) collective-permute-start(bf16[128,384]{1,0:T(8,128)(2,1)S(1)} %shard_map.75), channel_id=1, source_target_pairs={{0,2},{2,0},{1,3},{3,1},{4,6},{6,4},{5,7},{7,5},{8,10},{10,8},{9,1... | collective-permute-start | bytes 294920 | tf_op jit(solution)/shard_map/ppermute | solution.py:12
  57.4 9.9 %copy-start.18 = (s32[256,1]{0,1:T(1,128)S(1)}, s32[256,1]{0,1:T(1,128)}, u32[]{:S(2)}) copy-start(s32[256,1]{0,1:T(1,128)} %param.12) | copy-start | bytes 3076
  57.4 15.1 %collective-permute-start.22 = (bf16[256,1024]{1,0:T(8,128)(2,1)S(1)}, bf16[256,1024]{1,0:T(8,128)(2,1)S(1)}, u32[]{:S(2)}, u32[]{:S(2)}) collective-permute-start(bf16[256,1024]{1,0:T(8,128)(2,1)S(1)} %fusion.8), channel_id=1, source_target_pairs={{0,4},{4,0},{8,12},{12,8},{1,5},{5,1},{9,13},{13,9},{2,6},{6,2},{1... | collective-permute-start | bytes 1572872 | tf_op jit(solution)/shard_map/ppermute | solution.py:65
  67.2 1.5 %collective-permute-start.20 = (bf16[128,768]{1,0:T(8,128)(2,1)S(1)}, bf16[128,768]{1,0:T(8,128)(2,1)S(1)}, u32[]{:S(2)}, u32[]{:S(2)}) collective-permute-start(bf16[128,768]{1,0:T(8,128)(2,1)S(1)} %maximum_select_fusion.12), channel_id=1, source_target_pairs={{0,1},{1,0},{2,3},{3,2},{4,5},{5,4},{6,7},{7,6},{8,9},{9,8},{10,11... | collective-permute-start | bytes 589832 | tf_op jit(solution)/shard_map/ppermute | solution.py:12
  67.3 5.2 %collective-permute-start.21 = (bf16[128,384]{1,0:T(8,128)(2,1)S(1)}, bf16[128,384]{1,0:T(8,128)(2,1)S(1)}, u32[]{:S(2)}, u32[]{:S(2)}) collective-permute-start(bf16[128,384]{1,0:T(8,128)(2,1)S(1)} %shard_map.76), channel_id=1, source_target_pairs={{0,2},{2,0},{1,3},{3,1},{4,6},{6,4},{5,7},{7,5},{8,10},{10,8},{9,1... | collective-permute-start | bytes 294920 | tf_op jit(solution)/shard_map/ppermute | solution.py:12
  72.5 3.7 %copy-start.15 = (bf16[256,1024]{1,0:T(8,128)(2,1)}, bf16[256,1024]{1,0:T(8,128)(2,1)S(1)}, u32[]{:S(2)}) copy-start(bf16[256,1024]{1,0:T(8,128)(2,1)S(1)} %collective-permute-done.22) | copy-start | bytes 1572868
  72.6 3.1 %collective-permute-start.23 = (bf16[128,768]{1,0:T(8,128)(2,1)S(1)}, bf16[128,768]{1,0:T(8,128)(2,1)S(1)}, u32[]{:S(2)}, u32[]{:S(2)}) collective-permute-start(bf16[128,768]{1,0:T(8,128)(2,1)S(1)} %maximum_select_fusion.13), channel_id=1, source_target_pairs={{0,1},{1,0},{2,3},{3,2},{4,5},{5,4},{6,7},{7,6},{8,9},{9,8},{10,11... | collective-permute-start | bytes 589832 | tf_op jit(solution)/shard_map/ppermute | solution.py:12
  72.8 15.1 %copy-start.17 = (s32[256,1]{0,1:T(1,128)S(1)}, s32[256,1]{0,1:T(1,128)}, u32[]{:S(2)}) copy-start(s32[256,1]{0,1:T(1,128)} %param.11) | copy-start | bytes 3076
  72.8 15.1 %collective-permute-start.24 = (bf16[128,1024]{1,0:T(8,128)(2,1)S(1)}, bf16[128,1024]{1,0:T(8,128)(2,1)S(1)}, u32[]{:S(2)}, u32[]{:S(2)}) collective-permute-start(bf16[128,1024]{1,0:T(8,128)(2,1)S(1)} %add_convert_fusion), channel_id=1, source_target_pairs={{0,8},{4,12},{8,0},{12,4},{1,9},{5,13},{9,1},{13,5},{2,10},{6,14},... | collective-permute-start | bytes 786440 | tf_op jit(solution)/shard_map/ppermute | solution.py:65
  72.8 16.2 %collective-permute-start.26 = (bf16[128,1024]{1,0:T(8,128)(2,1)S(1)}, bf16[128,1024]{1,0:T(8,128)(2,1)}, u32[]{:S(2)}, u32[]{:S(2)}) collective-permute-start(bf16[128,1024]{1,0:T(8,128)(2,1)S(1)} %slice.55), channel_id=1, source_target_pairs={{0,4},{4,0},{8,12},{12,8},{1,5},{5,1},{9,13},{13,9},{2,6},{6,2},{1... | collective-permute-start | bytes 786440 | tf_op jit(solution)/shard_map/ppermute | solution.py:65
  76.2 1.0 copy-start.14
  77.2 24.6 %copy-start.13 = (f32[256,1024]{1,0:T(8,128)S(1)}, f32[256,1024]{1,0:T(8,128)}, u32[]{:S(2)}) copy-start(f32[256,1024]{1,0:T(8,128)} %fusion.4) | copy-start | bytes 3145732
  87.8 13.9 %collective-permute-start.25 = (bf16[128,1024]{1,0:T(8,128)(2,1)S(1)}, bf16[128,1024]{1,0:T(8,128)(2,1)}, u32[]{:S(2)}, u32[]{:S(2)}) collective-permute-start(bf16[128,1024]{1,0:T(8,128)(2,1)S(1)} %slice.56), channel_id=1, source_target_pairs={{0,4},{4,0},{8,12},{12,8},{1,5},{5,1},{9,13},{13,9},{2,6},{6,2},{1... | collective-permute-start | bytes 786440 | tf_op jit(solution)/shard_map/ppermute | solution.py:65
  90.2 12.7 %collective-permute-start.27 = (bf16[128,1024]{1,0:T(8,128)(2,1)S(1)}, bf16[128,1024]{1,0:T(8,128)(2,1)S(1)}, u32[]{:S(2)}, u32[]{:S(2)}) collective-permute-start(bf16[128,1024]{1,0:T(8,128)(2,1)S(1)} %fusion.13), channel_id=1, source_target_pairs={{0,12},{4,8},{8,4},{12,0},{1,13},{5,9},{9,5},{13,1},{2,14},{6,10},... | collective-permute-start | bytes 786440 | tf_op jit(solution)/shard_map/ppermute | solution.py:65
